TPU v7x, 256 devices: a whole 4x4x8 slice. The times are simulated.
256 devices in a mesh: inst: 16 (over z, core), tp: 8 (over y_lo, x), pp: 2 (over y_hi).
Axes of the slice: x: 4, y: 4 (y_hi: 2, y_lo: 2; y = y_hi * 2 + y_lo), z: 8, core: 2. Of those that a mesh axis runs over, the one named last changes fastest.
Arguments:
- residual: bfloat16 [1024, 2, 4096], P(('inst', 'tp')), may hold values from -6 to 6
- queries: bfloat16 [2, 1024, 2, 8192], P('pp', 'inst', None, 'tp'), may hold values from -10 to 10
- new_kv: bfloat16 [2, 1024, 2, 2, 1024], P('pp', 'inst', None, None, 'tp'), may hold values from -12 to 12
- kv_pool: bfloat16 [2, 4096, 2, 8, 16, 128], P('pp', 'inst', None, 'tp'), may hold values from -8 to 8
- out_weight: bfloat16 [2, 8192, 4096], P('pp', 'tp'), may hold values from -0.0625 to 0.0625
- lengths: int32 [1024], P('inst'), may hold values from 0 to 64, as said below
- page_table: int32 [1024, 4], P('inst'), may hold values from 0 to 255, as said below
- move_slot: int32 [16, 16, 2], replicated, may hold values from -1 to 63, as said below
- move_pages: int32 [16, 16, 2, 4], P('inst'), may hold values from 0 to 255, as said below
Outputs:
- hidden_out: bfloat16 [2, 1024, 2, 4096], P('pp', ('inst', 'tp'))
- pool_after: bfloat16 [2, 4096, 2, 8, 16, 128], P('pp', 'inst', None, 'tp')
Inputs may be any that keep to these rules, and one draw needn't show every extreme that they name: `lengths`: a slot whose request left holds a new request with no cached tokens; some slot holds 64. `page_table`: the 64 rows of one instance hold each of its 256 pages once. `move_slot`: -1 where no move is made, always where s = d. Every instance may send to and take from every other; from one sender to one receiver the moves take k = 0, 1, ... in order, at most 2 of them and exactly 2 for some pair; the slots taken at one instance are distinct and differ from the slots that its own moved requests left, and one instance takes at most 2 * (15) requests, some instance exactly that many. `move_pages`: for a move that is made, the page table row of the request at its old instance; other entries are arbitrary pages.
All inputs are finite; a program needn't handle non-finite values.
Results may differ from a plain program's by a relative error of at most 0.019.
Values may be sent and summed in bfloat16 or wider, within the bound.
No kernel may reach another device: no remote copies, remote signals or barrier semaphores. Data moves between devices by JAX's collectives and lax.ppermute only.
A program may use at most 64 MiB of HBM per device.

v0:
```python
import math

import jax
import jax.numpy as jnp
from jax import lax
from jax.sharding import PartitionSpec as P


def passed_along(value, axis, steps):
    count = lax.axis_size(axis)
    leading, last = (max(0, -steps), min(count, count - steps))
    return lax.ppermute(value, axis, [(source, source + steps) for source in range(leading, last)])


def attend(query_rows, fresh_rows, page_block, context):
    row_count, step_count, col_width = query_rows.shape
    kv_heads = page_block.shape[3]
    head_dim = page_block.shape[5]
    group_size = col_width // (kv_heads * head_dim)
    pages_each = page_block.shape[1]
    page_len = page_block.shape[4]
    score_scale = 1.0 / math.sqrt(head_dim)
    head_query = query_rows.reshape(row_count, step_count, kv_heads, group_size, head_dim)
    fresh_keys = fresh_rows[:, :, 0].reshape(row_count, step_count, kv_heads, head_dim)
    fresh_values = fresh_rows[:, :, 1].reshape(row_count, step_count, kv_heads, head_dim)
    cache_scores = (
        jnp.einsum(
            "nskgd,npktd->nskgpt",
            head_query,
            page_block[:, :, 0],
            preferred_element_type=jnp.float32,
        )
        * score_scale
    )
    fresh_scores = (
        jnp.einsum("nskgd,njkd->nskgj", head_query, fresh_keys, preferred_element_type=jnp.float32)
        * score_scale
    )
    position = jnp.arange(pages_each * page_len, dtype=jnp.int32).reshape(pages_each, page_len)
    cache_mask = position[None, None, None, None, :, :] < context[:, None, None, None, None, None]
    step_index = jnp.arange(step_count, dtype=jnp.int32)
    fresh_mask = (step_index[None, :] <= step_index[:, None])[None, :, None, None, :]
    top_cache = jnp.max(jnp.where(cache_mask, cache_scores, -jnp.inf), axis=(4, 5))
    top_fresh = jnp.max(jnp.where(fresh_mask, fresh_scores, -jnp.inf), axis=4)
    top_score = jnp.maximum(top_cache, top_fresh)
    cache_weights = jnp.where(cache_mask, jnp.exp(cache_scores - top_score[..., None, None]), 0.0)
    fresh_weights = jnp.where(fresh_mask, jnp.exp(fresh_scores - top_score[..., None]), 0.0)
    weight_total = jnp.sum(cache_weights, axis=(4, 5)) + jnp.sum(fresh_weights, axis=4)
    weighted = jnp.einsum(
        "nskgpt,npktd->nskgd",
        cache_weights.astype(jnp.bfloat16),
        page_block[:, :, 1],
        preferred_element_type=jnp.float32,
    )
    weighted = weighted + jnp.einsum(
        "nskgj,njkd->nskgd",
        fresh_weights.astype(jnp.bfloat16),
        fresh_values,
        preferred_element_type=jnp.float32,
    )
    attended = (weighted / weight_total[..., None]).astype(jnp.bfloat16)
    return attended.reshape(row_count, step_count, col_width)


def shards(
    residual, queries, new_kv, kv_pool, out_weight, lengths, page_table, move_slot, move_pages
):
    own_instance = lax.axis_index("inst")
    pool_local = kv_pool[0]
    page_total = pool_local.shape[0]
    slot_count = lengths.shape[0]
    outgoing = pool_local[move_pages[0]]
    arrived = lax.all_to_all(outgoing, "inst", split_axis=0, concat_axis=0, tiled=True)
    arrival_slots = lax.dynamic_index_in_dim(move_slot, own_instance, 1, keepdims=False)
    arrival_valid = arrival_slots >= 0
    safe_slots = jnp.maximum(arrival_slots, 0)
    target_pages = jnp.where(arrival_valid[:, :, None], page_table[safe_slots], page_total)
    updated = pool_local.at[target_pages].set(arrived, mode="drop")
    query_rows = queries[0]
    fresh_rows = new_kv[0]
    attended = attend(query_rows, fresh_rows, updated[page_table], lengths)
    step_count = attended.shape[1]
    col_width = attended.shape[2]
    flat_rows = attended.reshape(slot_count * step_count, col_width)
    weight_rows = out_weight[0]
    branch = lax.psum_scatter(
        jnp.dot(flat_rows, weight_rows, preferred_element_type=jnp.float32).astype(jnp.bfloat16),
        "tp",
        scatter_dimension=0,
        tiled=True,
    ).astype(jnp.float32)
    branch = branch.reshape(residual.shape)
    first_out = (residual.astype(jnp.float32) + branch).astype(jnp.bfloat16)
    passed = passed_along(first_out, "pp", 1)
    second_out = (passed.astype(jnp.float32) + branch).astype(jnp.bfloat16)
    section_index = lax.axis_index("pp")
    hidden_out = jnp.where(section_index == 0, first_out, second_out)
    return (hidden_out[None], updated[None])


def solution(mesh):
    return jax.shard_map(
        shards,
        mesh=mesh,
        in_specs=(
            P(("inst", "tp"), None, None),
            P("pp", "inst", None, "tp"),
            P("pp", "inst", None, None, "tp"),
            P("pp", "inst", None, "tp", None, None),
            P("pp", "tp", None),
            P("inst"),
            P("inst", None),
            P(),
            P("inst", None, None, None),
        ),
        out_specs=(P("pp", ("inst", "tp"), None, None), P("pp", "inst", None, "tp", None, None)),
        check_vma=False,
    )
```

profile of v0, /device:TPU:16, one launch (start us, length us, event | category | flops | bytes accessed | tf_op | source)
XLA Modules:
  0.0 120.3 jit_solution(4846226938990566801)
XLA Ops:
  7.2 0.0 copy-start.7
  7.2 1.6 %copy.55 = bf16[1,256,2,1,16,128]{5,4,3,2,1,0:T(8,128)(2,1)S(1)} copy(bf16[1,256,2,1,16,128]{5,4,3,2,1,0:T(8,128)(2,1)} %param.12) | data formatting | bytes 4194304
  8.8 0.0 copy-done.7
  8.8 0.1 copy.33
  8.9 0.1 reshape.203
  9.0 0.0 copy-start.1
  9.0 1.7 %gather_fusion.1 = bf16[128,2,16,128]{3,2,1,0:T(8,128)(2,1)} fusion(bf16[256,2,16,128]{3,2,1,0:T(8,128)(2,1)S(1)} %bitcast.122, s32[1024]{0:T(1024)S(1)} %pad_clamp_fusion.1), kind=kCustom, calls=%fused_computation.1 | custom fusion | bytes 2097664 | tf_op jit(solution)/shard_map/gather | solution.py:72
  10.7 0.0 copy-start.5
  10.7 0.0 copy-start.6
  10.7 0.0 copy-start.4
  10.7 0.0 copy-start.8
  10.7 8.7 %all-to-all-start = ((bf16[16,2,4,2,1,16,128]{6,5,3,2,1,4,0:T(8,128)(2,1)}), bf16[16,2,4,2,1,16,128]{6,5,3,2,1,4,0:T(8,128)(2,1)S(1)}, u32[]{:S(2)}, u32[]{:S(2)}) async-start(bf16[16,2,4,2,1,16,128]{6,5,3,2,1,4,0:T(8,128)(2,1)} %bitcast.128), calls=%async_computation | async-start | bytes 2097152 | tf_op jit(solution)/shard_map/all_to_all | solution.py:73
  19.4 0.0 reduce-scatter.2.cloned.1.call-start
  19.5 0.0 copy-done.1
  19.5 0.9 reshape.244
  20.4 0.9 reshape.182
  21.2 0.0 copy-done.5
  21.2 0.4 maximum_reduce_fusion
  21.7 0.1 reshape.193
  21.8 0.1 dynamic-slice_compare_fusion
  21.9 0.1 copy.30
  22.0 0.1 copy.31
  22.1 0.0 copy-done.6
  22.1 0.1 copy.32
  22.2 0.1 copy.36
  22.3 0.1 reshape.213
  22.4 0.6 gather_fusion
  23.0 0.1 compare_select_fusion.1
  23.1 0.1 reshape.223
  23.2 0.0 copy-done.4
  23.3 2.3 %select_reduce_fusion = (f32[64,2,8]{2,1,0:T(2,128)S(1)}, f32[64,2,1,8,2]{3,4,1,0,2:T(2,128)S(1)}) fusion(pred[2,2]{1,0:T(4,128)(4,1)S(1)} %iota_compare_fusion, bf16[64,2,8,128]{3,2,1,0:T(8,128)(2,1)} %reshape.182, bf16[64,2,2,128]{3,1,0,2:T(2,128)(2,1)S(1)} %bitcast.133), kind=kOutput, calls=%fused_computation.38 | convolution fusion | flops 529408 | bytes 307712 | tf_op jit(solution)/shard_map/nskgd,njkd->nskgj/dot_general | solution.py:36
  25.5 0.0 copy-done.8
  25.6 0.1 broadcast_compare_fusion
  25.7 20.4 %all-to-all-done = bf16[16,2,4,2,1,16,128]{6,5,3,2,1,4,0:T(8,128)(2,1)S(1)} async-done(((bf16[16,2,4,2,1,16,128]{6,5,3,2,1,4,0:T(8,128)(2,1)}), bf16[16,2,4,2,1,16,128]{6,5,3,2,1,4,0:T(8,128)(2,1)S(1)}, u32[]{:S(2)}, u32[]{:S(2)}) %all-to-all-start) | async-done | bytes 1048608 | tf_op jit(solution)/shard_map/all_to_all | solution.py:73
  46.1 4.6 %scatter_fusion = bf16[256,2,16,128]{3,2,1,0:T(8,128)(2,1)S(1)} fusion(bf16[256,2,16,128]{3,2,1,0:T(8,128)(2,1)S(1)} %bitcast.123, s32[128]{0:T(128)S(1)} %reshape.223, bf16[128,2,16,128]{3,2,1,0:T(8,128)(2,1)S(1)} %bitcast.127), kind=kCustom, calls=%fused_computation.3 | custom fusion | bytes 3146240 | tf_op jit(solution)/shard_map/scatter | solution.py:78
  50.7 0.0 copy-start
  50.7 2.2 %gather_fusion.2 = bf16[256,2,16,128]{3,2,1,0:T(8,128)(2,1)} fusion(bf16[256,2,16,128]{3,2,1,0:T(8,128)(2,1)S(1)} %scatter_fusion, s32[1024]{0:T(1024)S(1)} %pad_clamp_fusion), kind=kCustom, calls=%fused_computation.2 | custom fusion | bytes 4195328 | tf_op jit(solution)/shard_map/gather | solution.py:81
  52.9 0.0 copy-done
  52.9 0.0 copy-start.2
  52.9 2.0 %copy.37 = bf16[256,2,16,128]{3,2,0,1:T(8,128)(2,1)S(1)} copy(bf16[256,2,16,128]{3,2,1,0:T(8,128)(2,1)} %gather_fusion.2) | data formatting | bytes 4194304 | tf_op jit(solution)/shard_map/gather | solution.py:81
  54.9 0.0 copy-done.2
  54.9 0.0 slice-start
  54.9 2.6 %fusion.5 = (f32[64,2,8]{2,1,0:T(2,128)S(1)}, f32[64,4,16,2,8]{2,4,3,1,0:T(8,128)S(1)}) fusion(pred[64,4,16]{2,1,0:T(4,128)(4,1)S(1)} %broadcast_compare_fusion, bf16[64,2,8,128,1]{3,2,1,0,4:T(8,128)(2,1)S(1)} %copy-done.2, bf16[64,4,2,1,16,128]{5,4,1,0,3,2:T(8,128)(2,1)S(1)} %bitcast.129), kind=kOutput, calls=%fused_computation.11 | convolution fusion | flops 16972800 | bytes 1609728 | tf_op jit(solution)/shard_map/nskgd,npktd->nskgpt/dot_general | solution.py:27
  57.6 0.0 slice-start.1
  57.6 1.1 convolution_bitcast_fusion
  58.7 0.9 bitcast_reduce_fusion
  59.5 0.3 fusion.26
  59.9 0.4 fusion.19
  60.3 0.0 slice-done
  60.3 0.0 slice-done.1
  60.3 0.0 copy-start.3
  60.3 2.3 %fusion.2 = bf16[128,4096]{1,0:T(8,128)(2,1)} fusion(bf16[1,1024,4096]{2,1,0:T(8,128)(2,1)S(1)} %bitcast.126, bf16[16,8,8,128]{3,2,1,0:T(8,128)(2,1)S(1)} %bitcast.131), kind=kOutput, calls=%fused_computation.6 | convolution fusion | flops 1074266112 | bytes 9699328 | tf_op jit(solution)/shard_map/dot_general | solution.py:87
  62.6 0.0 reduce-scatter.2.cloned.1.call-update
  62.6 40.4 %reduce-scatter.2.cloned.1.call-done = bf16[16,4096]{1,0:T(8,128)(2,1)} async-done(((bf16[128,4096]{1,0:T(8,128)(2,1)}), bf16[16,4096]{1,0:T(8,128)(2,1)}) %reduce-scatter.2.cloned.1.call-update) | async-done | bytes 131088 | tf_op jit(solution)/shard_map/reduce_scatter | solution.py:86
  103.0 1.1 reshape.190
  104.1 0.0 copy-done.3
  104.1 0.1 add_convert_fusion.1
  104.3 1.3 %collective-permute-start = (bf16[8,2,4096]{2,1,0:T(2,128)(2,1)S(1)}, bf16[8,2,4096]{2,1,0:T(2,128)(2,1)S(1)}, u32[]{:S(2)}, u32[]{:S(2)}) collective-permute-start(bf16[8,2,4096]{2,1,0:T(2,128)(2,1)S(1)} %add_convert_fusion.1), channel_id=1, source_target_pairs={{0,1},{2,3},{4,5},{6,7},{8,9},{10,11},{12,13},{14,15},{16,17},{18,... | collective-permute-start | bytes 393224 | tf_op jit(solution)/shard_map/ppermute | solution.py:12
  105.6 7.1 %collective-permute-done = bf16[8,2,4096]{2,1,0:T(2,128)(2,1)S(1)} collective-permute-done((bf16[8,2,4096]{2,1,0:T(2,128)(2,1)S(1)}, bf16[8,2,4096]{2,1,0:T(2,128)(2,1)S(1)}, u32[]{:S(2)}, u32[]{:S(2)}) %collective-permute-start) | collective-permute-done | bytes 131104 | tf_op jit(solution)/shard_map/ppermute | solution.py:12
  112.6 0.8 fusion.23
  (11 shorter events, 0.2 us)
Async XLA Ops:
  7.2 1.6 %copy-start.7 = (s32[1,16,2,4]{1,3,2,0:T(4,128)S(1)}, s32[1,16,2,4]{1,3,2,0:T(4,128)}, u32[]{:S(2)}) copy-start(s32[1,16,2,4]{1,3,2,0:T(4,128)} %param.17) | copy-start | bytes 1540
  9.0 10.5 %copy-start.1 = (bf16[1,64,2,1024]{3,2,1,0:T(2,128)(2,1)S(1)}, bf16[1,64,2,1024]{3,2,1,0:T(2,128)(2,1)}, u32[]{:S(2)}) copy-start(bf16[1,64,2,1024]{3,2,1,0:T(2,128)(2,1)} %param.10) | copy-start | bytes 786436
  10.7 10.6 %copy-start.5 = (s32[16,16,2]{1,2,0:T(2,128)S(1)}, s32[16,16,2]{1,2,0:T(2,128)}, u32[]{:S(2)}) copy-start(s32[16,16,2]{1,2,0:T(2,128)} %param.16) | copy-start | bytes 6148
  10.7 11.4 %copy-start.6 = (s32[64,4]{0,1:T(4,128)S(1)}, s32[64,4]{0,1:T(4,128)}, u32[]{:S(2)}) copy-start(s32[64,4]{0,1:T(4,128)} %param.15) | copy-start | bytes 3076
  10.7 12.5 %copy-start.4 = (bf16[1,64,2,2,128]{4,3,2,1,0:T(2,128)(2,1)S(1)}, bf16[1,64,2,2,128]{4,3,2,1,0:T(2,128)(2,1)}, u32[]{:S(2)}) copy-start(bf16[1,64,2,2,128]{4,3,2,1,0:T(2,128)(2,1)} %param.11) | copy-start | bytes 196612
  10.7 14.9 %copy-start.8 = (s32[64]{0:T(128)S(1)}, s32[64]{0:T(128)}, u32[]{:S(2)}) copy-start(s32[64]{0:T(128)} %param.14) | copy-start | bytes 772
  10.7 35.4 %all-to-all-start = ((bf16[16,2,4,2,1,16,128]{6,5,3,2,1,4,0:T(8,128)(2,1)}), bf16[16,2,4,2,1,16,128]{6,5,3,2,1,4,0:T(8,128)(2,1)S(1)}, u32[]{:S(2)}, u32[]{:S(2)}) async-start(bf16[16,2,4,2,1,16,128]{6,5,3,2,1,4,0:T(8,128)(2,1)} %bitcast.128), calls=%async_computation | async-start | bytes 2097152 | tf_op jit(solution)/shard_map/all_to_all | solution.py:73
  19.4 83.6 %reduce-scatter.2.cloned.1.call-start = ((), (), s32[]{:S(2)}) async-start(), calls=%async_computation.2 | async-start | bytes 1179648 | tf_op jit(solution)/shard_map/reduce_scatter | solution.py:86
  50.7 2.2 %copy-start = (bf16[256,2,16,128]{3,2,1,0:T(8,128)(2,1)}, bf16[256,2,16,128]{3,2,1,0:T(8,128)(2,1)S(1)}, u32[]{:S(2)}) copy-start(bf16[256,2,16,128]{3,2,1,0:T(8,128)(2,1)S(1)} %scatter_fusion) | copy-start | bytes 6291460
  52.9 2.0 %copy-start.2 = (bf16[64,2,8,128,1]{3,2,1,0,4:T(8,128)(2,1)S(1)}, bf16[64,2,8,128,1]{3,2,1,0,4:T(8,128)(2,1)}, u32[]{:S(2)}) copy-start(bf16[64,2,8,128,1]{3,2,1,0,4:T(8,128)(2,1)} %reshape.244) | copy-start | bytes 786436
  54.9 5.4 %slice-start = ((s8[8388608]{0:T(1024)(128)(4,1)}), s8[4194304]{0:T(1024)(128)(4,1)S(1)}, s32[]{:S(2)}) async-start(s8[8388608]{0:T(1024)(128)(4,1)} %bitcast.125), calls=%async_computation.3 | async-start | bytes 8388608
  57.6 2.7 %slice-start.1 = ((s8[8388608]{0:T(1024)(128)(4,1)}), s8[4194304]{0:T(1024)(128)(4,1)S(1)}, s32[]{:S(2)}) async-start(s8[8388608]{0:T(1024)(128)(4,1)} %bitcast.125), calls=%async_computation.4 | async-start | bytes 8388608
  60.3 43.8 %copy-start.3 = (bf16[8,2,4096]{2,1,0:T(2,128)(2,1)S(1)}, bf16[8,2,4096]{2,1,0:T(2,128)(2,1)}, u32[]{:S(2)}) copy-start(bf16[8,2,4096]{2,1,0:T(2,128)(2,1)} %param.9) | copy-start | bytes 393220
  104.3 8.4 %collective-permute-start = (bf16[8,2,4096]{2,1,0:T(2,128)(2,1)S(1)}, bf16[8,2,4096]{2,1,0:T(2,128)(2,1)S(1)}, u32[]{:S(2)}, u32[]{:S(2)}) collective-permute-start(bf16[8,2,4096]{2,1,0:T(2,128)(2,1)S(1)} %add_convert_fusion.1), channel_id=1, source_target_pairs={{0,1},{2,3},{4,5},{6,7},{8,9},{10,11},{12,13},{14,15},{16,17},{18,... | collective-permute-start | bytes 393224 | tf_op jit(solution)/shard_map/ppermute | solution.py:12
Sparse Core Ops, SparseCore 0:
  62.7 40.2 reduce-scatter.1
where the time goes:
time: 121 us; the launch traced here: 120 us
  waiting for transfers between devices  67.9 us (56%)
  local copies, waits for them, and re-layouts  16.5 us (14%)
  between operations  14.3 us (12%)
  starting transfers between devices  10 us (8%)
  matrix products  8.63 us (7%)
  other arithmetic  2.98 us (2%)
    reduce_scatter x1, waiting for transfers between devices, shards(): lax.psum_scatter(jnp.dot(flat_rows, weight_rows, preferred_element_type=j...  40.4 us
    all_to_all x1, waiting for transfers between devices, shards(): lax.all_to_all(outgoing, 'inst', split_axis=0, concat_axis=0, tiled=True)  20.4 us
    all_to_all x1, starting transfers between devices, shards(): lax.all_to_all(outgoing, 'inst', split_axis=0, concat_axis=0, tiled=True)  8.72 us
    ppermute x1, waiting for transfers between devices, passed_along(): lax.ppermute(value, axis, [(source, source + steps) for source in range(l...  7.06 us
    scatter x1, local copies, waits for them, and re-layouts, shards(): updated = pool_local.at[target_pages].set(arrived, mode='drop')  4.59 us
    gather x2, local copies, waits for them, and re-layouts, shards(): attended = attend(query_rows, fresh_rows, updated[page_table], lengths)  4.2 us
    dot_general x1, matrix products, attend(): jnp.einsum('nskgd,npktd->nskgpt', head_query, page_block[:, :, 0], prefer...  2.64 us
  transfers between devices with their start and end apart: 3, of which 3 were waited for; matrix products, arithmetic and copies ran while one was open for 5% of the time, Pallas kernels for 0%

commit v1 on v0

v1 whole, which is shorter than its diff:
```python
import functools
import math

import jax
import jax.numpy as jnp
from jax import lax
from jax.experimental import pallas as pl
from jax.experimental.pallas import tpu as pltpu
from jax.sharding import PartitionSpec as P

SMEM = pl.BlockSpec(memory_space=pltpu.SMEM)
VMEM = pl.BlockSpec(memory_space=pltpu.VMEM)
ANY = pl.BlockSpec(memory_space=pl.ANY)
MASKED = -1e30
VMEM_LIMIT = 32 * 1024 * 1024
BF16 = jnp.bfloat16
F32 = jnp.float32


def iota(shape, axis):
    return lax.broadcasted_iota(jnp.int32, shape, axis)


def dot_last(a, b):
    return lax.dot_general(a, b, (((1,), (1,)), ((), ())), preferred_element_type=F32)


def pick4(index, values):
    low = jnp.where(index == 0, values[0], values[1])
    high = jnp.where(index == 2, values[2], values[3])
    return jnp.where(index < 2, low, high)


def fresh_part(query, keys, values, slots, scale):
    shape = (query.shape[0], keys.shape[0])
    row, col = iota(shape, 0), iota(shape, 1)
    valid = (col // 2 == pick4((row // 2) % 4, slots)) & (col % 2 <= row % 2)
    score = jnp.where(valid, dot_last(query, keys) * scale, MASKED)
    top = jnp.max(score, axis=1, keepdims=True)
    weight = jnp.where(valid, jnp.exp(score - top), 0.0)
    total = jnp.sum(weight, axis=1, keepdims=True)
    return top, total, jnp.dot(weight.astype(BF16), values, preferred_element_type=F32)


def cached_part(query, keys, values, limits, fresh, scale):
    fresh_top, fresh_total, fresh_sum = fresh
    shape = (query.shape[0], keys.shape[0])
    row, col = iota(shape, 0), iota(shape, 1)
    request = col // 64
    valid = ((row // 2) % 4 == request) & (col % 64 < pick4(request, limits))
    score = jnp.where(valid, dot_last(query, keys) * scale, MASKED)
    top = jnp.maximum(jnp.max(score, axis=1, keepdims=True), fresh_top)
    weight = jnp.where(valid, jnp.exp(score - top), 0.0)
    rescale = jnp.exp(fresh_top - top)
    total = jnp.sum(weight, axis=1, keepdims=True) + fresh_total * rescale
    summed = jnp.dot(weight.astype(BF16), values, preferred_element_type=F32)
    return (summed + fresh_sum * rescale) / total


def gather_kernel(pages, pool, out, sem):
    count = out.shape[0]
    for index in range(count):
        pltpu.make_async_copy(pool.at[pages[index]], out.at[index], sem).start()
    pltpu.make_async_copy(pool.at[pl.ds(0, count)], out, sem).wait()


def local_kernel(
    scale, table, lengths, arrivals, query, fresh, slot_rows, pool,
    attended, arrival_query, arrival_top, arrival_total, arrival_sum, pool_copy,
    gathered, sem,
):
    copy = pltpu.make_async_copy(pool, pool_copy, sem)
    copy.start()
    head_dim = pool.shape[-1]
    heads = query.shape[1] // head_dim
    fresh_keys = fresh[:, :head_dim].astype(BF16)
    fresh_values = fresh[:, head_dim:].astype(BF16)

    def stacked(ref, start):
        return jnp.concatenate(
            [ref[pl.ds(start, 8), h * head_dim : (h + 1) * head_dim] for h in range(heads)], axis=0
        ).astype(BF16)

    rows = query.shape[0]
    pick = (slot_rows[...] * 2 + iota((gathered.shape[0], rows), 0) % 2) == iota(
        (gathered.shape[0], rows), 1
    )
    gathered[...] = jnp.dot(
        pick.astype(BF16), query[...].astype(BF16), preferred_element_type=F32
    )

    def one_arrival(group, carry):
        start = pl.multiple_of(group * 8, 8)
        rows_in = stacked(gathered, start)
        slots = [jnp.maximum(arrivals[group * 4 + i], 0) for i in range(4)]
        top, total, summed = fresh_part(rows_in, fresh_keys, fresh_values, slots, scale)
        arrival_query[group] = rows_in
        arrival_top[group] = jnp.broadcast_to(top, summed.shape)
        arrival_total[group] = jnp.broadcast_to(total, summed.shape)
        arrival_sum[group] = summed
        return carry

    lax.fori_loop(0, gathered.shape[0] // 8, one_arrival, 0)

    def one_group(group, carry):
        start = pl.multiple_of(group * 8, 8)
        rows_in = stacked(query, start)
        slots = [group * 4 + i for i in range(4)]
        part = fresh_part(rows_in, fresh_keys, fresh_values, slots, scale)
        pages = [table[group * 16 + i] for i in range(16)]
        keys = jnp.concatenate([pool[page, 0] for page in pages], axis=0)
        values = jnp.concatenate([pool[page, 1] for page in pages], axis=0)
        limits = [lengths[slot] for slot in slots]
        out = cached_part(rows_in, keys, values, limits, part, scale)
        for h in range(heads):
            attended[pl.ds(start, 8), h * head_dim : (h + 1) * head_dim] = out[h * 8 : h * 8 + 8]
        return carry

    lax.fori_loop(0, rows // 8, one_group, 0)
    copy.wait()


def arrival_kernel(
    scale, lengths, arrivals, arrived, arrival_query, arrival_top, arrival_total, arrival_sum,
    attended, slot_cols, out, found,
):
    head_dim = arrived.shape[-1]
    groups = arrival_query.shape[0]
    heads = attended.shape[1] // head_dim
    for group in range(groups):
        limits = [lengths[jnp.maximum(arrivals[group * 4 + i], 0)] for i in range(4)]
        block = arrived[pl.ds(group * 16, 16)]
        keys = block[:, 0].reshape(256, head_dim)
        values = block[:, 1].reshape(256, head_dim)
        part = (arrival_top[group, :, :1], arrival_total[group, :, :1], arrival_sum[group])
        result = cached_part(arrival_query[group], keys, values, limits, part, scale)
        for h in range(heads):
            found[group * 8 : group * 8 + 8, h * head_dim : (h + 1) * head_dim] = result[
                h * 8 : h * 8 + 8
            ]
    shape = (attended.shape[0], found.shape[0])
    row, col = iota(shape, 0), iota(shape, 1)
    slot = slot_cols[...]
    place = (row // 2 == slot) & (row % 2 == col % 2)
    moved = jnp.dot(
        place.astype(BF16), found[...].astype(BF16), preferred_element_type=F32
    )
    taken = jnp.sum(place.astype(F32), axis=1, keepdims=True) > 0
    out[...] = jnp.where(taken, moved, attended[...]).astype(BF16)


def place_kernel(table, arrivals, arrived, pool_in, pool, sems):
    del pool_in
    count = arrivals.shape[0]

    def copies(index):
        slot = jnp.maximum(arrivals[index], 0)
        for page in range(4):
            yield pltpu.make_async_copy(
                arrived.at[index * 4 + page], pool.at[table[slot * 4 + page]], sems.at[index]
            )

    for index in range(count):

        @pl.when(arrivals[index] >= 0)
        def _(index=index):
            for copy in copies(index):
                copy.start()

    for index in range(count):

        @pl.when(arrivals[index] >= 0)
        def _(index=index):
            span = pl.ds(index * 4, 4)
            pltpu.make_async_copy(arrived.at[span], arrived.at[span], sems.at[index]).wait()


def shards(
    residual, queries, new_kv, kv_pool, out_weight, lengths, page_table, move_slot, move_pages
):
    me = lax.axis_index("inst")
    n_tp = lax.axis_size("tp")
    pages, _, _, page_len, head_dim = kv_pool.shape[1:]
    slots, steps, width = queries.shape[1:]
    rows = slots * steps
    scale = 1.0 / math.sqrt(head_dim)
    pool = kv_pool.reshape(pages, 2, page_len, head_dim)
    outgoing_pages = move_pages.reshape(-1)
    moved = outgoing_pages.shape[0]
    count = moved // 4
    sources = move_slot.shape[0]

    outgoing = pl.pallas_call(
        gather_kernel,
        out_shape=jax.ShapeDtypeStruct((moved, 2, page_len, head_dim), BF16),
        in_specs=[SMEM, ANY],
        out_specs=ANY,
        scratch_shapes=[pltpu.SemaphoreType.DMA(())],
        compiler_params=pltpu.CompilerParams(vmem_limit_bytes=VMEM_LIMIT),
        cost_estimate=pl.CostEstimate(flops=0, bytes_accessed=2**21, transcendentals=0),
        name="gather_pages",
    )(outgoing_pages, pool)
    arrived = lax.all_to_all(
        outgoing.reshape(sources, moved // sources, 2, page_len, head_dim),
        "inst", split_axis=0, concat_axis=0, tiled=True,
    ).reshape(moved, 2, page_len, head_dim)

    arrivals = lax.dynamic_index_in_dim(move_slot, me, 1, keepdims=False).reshape(-1)
    arrival_rows = jnp.repeat(arrivals, steps)
    table = page_table.reshape(-1)
    groups = count // 4
    query = queries.reshape(rows, width).astype(F32)
    fresh = new_kv.reshape(rows, 2 * head_dim).astype(F32)
    group_rows = 4 * width // head_dim * steps
    part_shape = jax.ShapeDtypeStruct((groups, group_rows, head_dim), F32)
    local = pl.pallas_call(
        functools.partial(local_kernel, scale),
        out_shape=[
            jax.ShapeDtypeStruct((rows, width), F32),
            jax.ShapeDtypeStruct((groups, group_rows, head_dim), BF16),
            part_shape,
            part_shape,
            part_shape,
            jax.ShapeDtypeStruct(pool.shape, BF16),
        ],
        in_specs=[SMEM, SMEM, SMEM, VMEM, VMEM, VMEM, VMEM],
        out_specs=[VMEM, VMEM, VMEM, VMEM, VMEM, ANY],
        scratch_shapes=[pltpu.VMEM((count * steps, width), F32), pltpu.SemaphoreType.DMA(())],
        compiler_params=pltpu.CompilerParams(vmem_limit_bytes=VMEM_LIMIT),
        cost_estimate=pl.CostEstimate(flops=2**28, bytes_accessed=2**24, transcendentals=2**18),
        name="local_attention",
    )
    attended, arrival_query, top, total, summed, pool_copy = local(
        table, lengths, arrivals, query, fresh, arrival_rows[:, None], pool
    )
    attended = pl.pallas_call(
        functools.partial(arrival_kernel, scale),
        out_shape=jax.ShapeDtypeStruct((rows, width), BF16),
        in_specs=[SMEM, SMEM] + [VMEM] * 7,
        out_specs=VMEM,
        scratch_shapes=[pltpu.VMEM((count * steps, width), F32)],
        compiler_params=pltpu.CompilerParams(vmem_limit_bytes=VMEM_LIMIT),
        cost_estimate=pl.CostEstimate(flops=2**27, bytes_accessed=2**22, transcendentals=2**17),
        name="arrival_attention",
    )(lengths, arrivals, arrived, arrival_query, top, total, summed, attended, arrival_rows[None])

    contribution = jnp.dot(attended, out_weight[0], preferred_element_type=F32).astype(BF16)
    model = contribution.shape[1]
    own = rows // n_tp
    received = lax.all_to_all(
        contribution.reshape(n_tp, own, model), "tp", split_axis=0, concat_axis=0, tiled=True
    )
    pool_after = pl.pallas_call(
        place_kernel,
        out_shape=jax.ShapeDtypeStruct(pool.shape, BF16),
        in_specs=[SMEM, SMEM, ANY, ANY],
        out_specs=ANY,
        input_output_aliases={3: 0},
        scratch_shapes=[pltpu.SemaphoreType.DMA((count,))],
        compiler_params=pltpu.CompilerParams(vmem_limit_bytes=VMEM_LIMIT),
        cost_estimate=pl.CostEstimate(flops=0, bytes_accessed=2**21, transcendentals=0),
        name="place_pages",
    )(table, arrivals, arrived, pool_copy)
    branch = jnp.sum(received.astype(F32), axis=0)
    first_out = (residual.reshape(own, model).astype(F32) + branch).astype(BF16)
    passed = lax.ppermute(first_out, "pp", [(0, 1)])
    second_out = (passed.astype(F32) + branch).astype(BF16)
    hidden_out = jnp.where(lax.axis_index("pp") == 0, first_out, second_out)
    return (hidden_out.reshape((1,) + residual.shape), pool_after.reshape(kv_pool.shape))


def solution(mesh):
    return jax.shard_map(
        shards,
        mesh=mesh,
        in_specs=(
            P(("inst", "tp"), None, None),
            P("pp", "inst", None, "tp"),
            P("pp", "inst", None, None, "tp"),
            P("pp", "inst", None, "tp", None, None),
            P("pp", "tp", None),
            P("inst"),
            P("inst", None),
            P(),
            P("inst", None, None, None),
        ),
        out_specs=(P("pp", ("inst", "tp"), None, None), P("pp", "inst", None, "tp", None, None)),
        check_vma=False,
    )
```

time: 121 us -> 87.3 us (0.72)
  waiting for transfers between devices: 67.9 us -> 29.1 us
  Pallas kernels: 0 us -> 21 us
  between operations: 14.3 us -> 0.82 us
  starting transfers between devices: 10 us -> 15.1 us
  matrix products: 8.63 us -> 5.65 us
  other arithmetic: 2.98 us -> 0.21 us
  local copies, waits for them, and re-layouts: 16.5 us -> 14.7 us
    reduce_scatter x1 -> x0, waiting for transfers between devices: 40.4 us -> none  [shards(): lax.psum_scatter(jnp.dot(flat_rows, weight_rows, preferred_element_type=j...]
    pallas_call x0 -> x4, Pallas kernels: none -> 21 us  [the longest x1 13.4 us: shards(): local(table, lengths, arrivals, query, fresh, arrival_rows[:, None], pool)]
    unnamed x25 -> x37, local copies, waits for them, and re-layouts: 1.79 us -> 12.1 us
    gather x4 -> x0, local copies, waits for them, and re-layouts: 6.43 us -> none  [the longest x2 4.2 us: shards(): attended = attend(query_rows, fresh_rows, updated[page_table], lengths)]
    all_to_all x1 -> x2, starting transfers between devices: 8.72 us -> 13.9 us  [the longest x1 8.7 us: shards(): lax.all_to_all(outgoing.reshape(sources, moved // sources, 2, page_len, h...]
    scatter x1 -> x0, local copies, waits for them, and re-layouts: 4.59 us -> none  [shards(): updated = pool_local.at[target_pages].set(arrived, mode='drop')]
    dot_general x5 -> x1, matrix products: 8.63 us -> 5.65 us  [shards(): jnp.dot(attended, out_weight[0], preferred_element_type=F32).astype(BF16)]
    all_to_all x1 -> x2, waiting for transfers between devices: 20.4 us -> 23.3 us  [the longest x1 16.8 us: shards(): lax.all_to_all(contribution.reshape(n_tp, own, model), 'tp', split_axis=0...]
  transfers between devices with their start and end apart: 3 -> 3, of which waited for: 3 -> 3; matrix products, arithmetic and copies ran while one was open for 5% -> 3% of each run, Pallas kernels for 0% -> 18%
where the time goes in v1:
time: 87.3 us; the launch traced here: 86.7 us
  waiting for transfers between devices  29.1 us (33%)
  Pallas kernels  21 us (24%)
  starting transfers between devices  15.1 us (17%)
  local copies, waits for them, and re-layouts  14.7 us (17%)
  matrix products  5.65 us (6%)
    all_to_all x1, waiting for transfers between devices, shards(): lax.all_to_all(contribution.reshape(n_tp, own, model), 'tp', split_axis=0...  16.8 us
    pallas_call x1, Pallas kernels, shards(): local(table, lengths, arrivals, query, fresh, arrival_rows[:, None], pool)  13.4 us
    unnamed x37, local copies, waits for them, and re-layouts  12.1 us
    all_to_all x1, starting transfers between devices, shards(): lax.all_to_all(outgoing.reshape(sources, moved // sources, 2, page_len, h...  8.7 us
    all_to_all x1, waiting for transfers between devices, shards(): lax.all_to_all(outgoing.reshape(sources, moved // sources, 2, page_len, h...  6.56 us
    ppermute x1, waiting for transfers between devices, shards(): passed = lax.ppermute(first_out, 'pp', [(0, 1)])  5.75 us
    dot_general x1, matrix products, shards(): jnp.dot(attended, out_weight[0], preferred_element_type=F32).astype(BF16)  5.65 us
    all_to_all x1, starting transfers between devices, shards(): lax.all_to_all(contribution.reshape(n_tp, own, model), 'tp', split_axis=0...  5.15 us
  transfers between devices with their start and end apart: 3, of which 3 were waited for; matrix products, arithmetic and copies ran while one was open for 3% of the time, Pallas kernels for 18%

profile of v1, /device:TPU:16, one launch (start us, length us, event | category | flops | bytes accessed | tf_op | source)
XLA Modules:
  0.0 86.7 jit_solution(11765149862325640766)
XLA Ops:
  0.6 0.0 copy-start
  0.6 0.8 copy.15
  1.4 0.1 reshape.42.pages
  1.5 0.0 copy-start.1
  1.6 1.6 %copy-done.1 = bf16[1,256,2,1,16,128]{5,4,3,2,1,0:T(8,128)(2,1)S(1)} copy-done((bf16[1,256,2,1,16,128]{5,4,3,2,1,0:T(8,128)(2,1)S(1)}, bf16[1,256,2,1,16,128]{5,4,3,2,1,0:T(8,128)(2,1)}, u32[]{:S(2)}) %copy-start.1) | copy-done | bytes 2097176
  3.1 0.0 copy-start.16
  3.1 0.0 copy-start.14
  3.1 2.4 %gather_pages.1 = bf16[128,2,16,128]{3,2,1,0:T(8,128)(2,1)S(1)} custom-call(s32[128]{0:T(128)S(1)} %reshape.42.pages, bf16[256,2,16,128]{3,2,1,0:T(8,128)(2,1)S(1)} %bitcast.21), custom_call_target="tpu_custom_call" | custom-call | bytes 2097152 | tf_op jit(solution)/shard_map/gather_pages/pallas_call | solution.py:193
  5.5 0.0 copy-start.3
  5.5 1.0 %copy-done.3 = bf16[128,2,16,128]{3,2,1,0:T(8,128)(2,1)} copy-done((bf16[128,2,16,128]{3,2,1,0:T(8,128)(2,1)}, bf16[128,2,16,128]{3,2,1,0:T(8,128)(2,1)S(1)}, u32[]{:S(2)}) %copy-start.3) | copy-done | bytes 1048600
  6.5 0.0 copy-start.2
  6.5 0.0 copy-start.13
  6.5 8.7 %all-to-all-start = ((bf16[16,8,2,16,128]{4,3,2,1,0:T(8,128)(2,1)}), bf16[16,8,2,16,128]{4,3,2,1,0:T(8,128)(2,1)S(1)}, u32[]{:S(2)}, u32[]{:S(2)}) async-start(bf16[16,8,2,16,128]{4,3,2,1,0:T(8,128)(2,1)} %bitcast.23), calls=%async_computation | async-start | bytes 2097152 | tf_op jit(solution)/shard_map/all_to_all | solution.py:203
  15.2 0.0 copy-done
  15.2 0.4 dynamic-slice_reduce_fusion
  15.7 0.1 reshape.41.arrivals
  15.7 0.1 broadcast_in_dim.3
  15.8 0.1 broadcast_in_dim_reshape.8.slot_rows
  15.9 0.1 broadcast_in_dim_reshape.7.slot_cols
  16.0 0.0 copy-done.16
  16.0 0.1 copy.16
  16.1 0.1 reshape.46.table
  16.2 0.0 copy-done.14
  16.2 0.9 %reshape.51.query = f32[128,1024]{1,0:T(8,128)} reshape(bf16[1,64,2,1024]{3,2,1,0:T(2,128)(2,1)S(1)} %copy-done.14) | data formatting | bytes 786432 | tf_op jit(solution)/shard_map/convert_element_type | solution.py:212
  17.1 0.8 copy.21
  17.9 0.0 copy-done.2
  18.0 0.0 copy-done.13
  18.0 0.0 copy-start.4
  18.0 1.0 %copy-done.4 = f32[128,1024]{1,0:T(8,128)S(1)} copy-done((f32[128,1024]{1,0:T(8,128)S(1)}, f32[128,1024]{1,0:T(8,128)}, u32[]{:S(2)}) %copy-start.4) | copy-done | bytes 524312
  19.0 13.4 %local_attention.1 = (f32[128,1024]{1,0:T(8,128)S(1)}, bf16[8,64,128]{2,1,0:T(8,128)(2,1)S(1)}, f32[8,64,128]{2,1,0:T(8,128)S(1)}, f32[8,64,128]{2,1,0:T(8,128)S...) custom-call(s32[256]{0:T(256)S(1)} %reshape.46.table, s32[64]{0:T(128)S(1)} %copy-done.13, ...), custom_call_target="tpu_custom_call" | custom-call | flops 268435456 | bytes 16777216 | tf_op jit(solution)/shard_map/local_attention/pallas_call | solution.py:233
  32.4 0.0 copy-start.5
  32.4 0.8 copy-done.5
  33.2 0.0 copy-start.7
  33.2 0.7 copy-done.7
  33.9 0.0 copy-start.9
  33.9 0.7 copy-done.9
  34.7 0.0 copy-start.11
  34.7 0.7 copy-done.11
  35.3 6.6 %all-to-all-done = bf16[16,8,2,16,128]{4,3,2,1,0:T(8,128)(2,1)S(1)} async-done(((bf16[16,8,2,16,128]{4,3,2,1,0:T(8,128)(2,1)}), bf16[16,8,2,16,128]{4,3,2,1,0:T(8,128)(2,1)S(1)}, u32[]{:S(2)}, u32[]{:S(2)}) %all-to-all-start) | async-done | bytes 1048608 | tf_op jit(solution)/shard_map/all_to_all | solution.py:203
  41.9 0.0 copy-start.6
  41.9 1.0 %copy-done.6 = f32[128,1024]{1,0:T(8,128)S(1)} copy-done((f32[128,1024]{1,0:T(8,128)S(1)}, f32[128,1024]{1,0:T(8,128)}, u32[]{:S(2)}) %copy-start.6) | copy-done | bytes 524312
  42.9 0.0 copy-start.8
  42.9 0.9 %copy-done.8 = f32[8,64,128]{2,1,0:T(8,128)S(1)} copy-done((f32[8,64,128]{2,1,0:T(8,128)S(1)}, f32[8,64,128]{2,1,0:T(8,128)}, u32[]{:S(2)}) %copy-start.8) | copy-done | bytes 262168
  43.9 0.0 copy-start.10
  43.9 0.9 %copy-done.10 = f32[8,64,128]{2,1,0:T(8,128)S(1)} copy-done((f32[8,64,128]{2,1,0:T(8,128)S(1)}, f32[8,64,128]{2,1,0:T(8,128)}, u32[]{:S(2)}) %copy-start.10) | copy-done | bytes 262168
  44.8 0.0 copy-start.12
  44.8 0.9 %copy-done.12 = bf16[8,64,128]{2,1,0:T(8,128)(2,1)S(1)} copy-done((bf16[8,64,128]{2,1,0:T(8,128)(2,1)S(1)}, bf16[8,64,128]{2,1,0:T(8,128)(2,1)}, u32[]{:S(2)}) %copy-start.12) | copy-done | bytes 131096
  45.7 3.4 %arrival_attention.1 = bf16[128,1024]{1,0:T(8,128)(2,1)S(1)} custom-call(s32[64]{0:T(128)S(1)} %copy-done.13, s32[32]{0:T(128)S(1)} %reshape.41.arrivals, bf16[128,2,16,128]{3,2,1,0:T(8,128)(2,1)S(1)} %bitcast.19, bf16[8,64,128]{2,1,0:T(8,128)(2,1)S(1)} %copy-done.12, f32[8,64,128]{2,1,0:T(8,128)S(1)} %get-tuple-element.9.arrival_top, ...), custom_call_target="tpu_custom_call" | custom-call | flops 134217728 | bytes 4194304 | tf_op jit(solution)/shard_map/arrival_attention/pallas_call | solution.py:236
  49.1 5.6 %fusion.2 = bf16[128,4096]{1,0:T(8,128)(2,1)} fusion(bf16[128,1024]{1,0:T(8,128)(2,1)S(1)} %arrival_attention.1, bf16[1,1024,4096]{2,1,0:T(8,128)(2,1)} %param.13), kind=kOutput, calls=%fused_computation.2 | convolution fusion | flops 1074266112 | bytes 9699328 | tf_op jit(solution)/shard_map/dot_general | solution.py:247
  54.8 0.0 copy-start.15
  54.8 5.2 %all-to-all-start.1 = ((bf16[8,16,4096]{2,1,0:T(8,128)(2,1)}), bf16[8,16,4096]{2,1,0:T(8,128)(2,1)S(1)}, u32[]{:S(2)}, u32[]{:S(2)}) async-start(bf16[8,16,4096]{2,1,0:T(8,128)(2,1)} %bitcast.4), calls=%async_computation.1 | async-start | bytes 2097152 | tf_op jit(solution)/shard_map/all_to_all | solution.py:250
  60.0 0.0 copy-done.15
  60.0 16.8 %all-to-all-done.1 = bf16[8,16,4096]{2,1,0:T(8,128)(2,1)S(1)} async-done(((bf16[8,16,4096]{2,1,0:T(8,128)(2,1)}), bf16[8,16,4096]{2,1,0:T(8,128)(2,1)S(1)}, u32[]{:S(2)}, u32[]{:S(2)}) %all-to-all-start.1) | async-done | bytes 1048608 | tf_op jit(solution)/shard_map/all_to_all | solution.py:250
  76.8 0.1 convert_reduce_fusion
  76.9 1.3 %collective-permute-start = (bf16[16,4096]{1,0:T(8,128)(2,1)S(1)}, bf16[16,4096]{1,0:T(8,128)(2,1)S(1)}, u32[]{:S(2)}, u32[]{:S(2)}) collective-permute-start(bf16[16,4096]{1,0:T(8,128)(2,1)S(1)} %add_convert_fusion.1), channel_id=1, source_target_pairs={{0,1},{2,3},{4,5},{6,7},{8,9},{10,11},{12,13},{14,15},{16,17},{18,... | collective-permute-start | bytes 393224 | tf_op jit(solution)/shard_map/ppermute | solution.py:266
  78.2 1.9 %place_pages.1 = bf16[256,2,16,128]{3,2,1,0:T(8,128)(2,1)} custom-call(s32[256]{0:T(256)S(1)} %reshape.46.table, s32[32]{0:T(128)S(1)} %reshape.41.arrivals, bf16[128,2,16,128]{3,2,1,0:T(8,128)(2,1)S(1)} %bitcast.20, bf16[256,2,16,128]{3,2,1,0:T(8,128)(2,1)} %get-tuple-element.13.pool_in), custom_call_target="tpu_custom_call", output_to_operand_aliasing={{}: (3, {})} | custom-call | bytes 2097152 | tf_op jit(solution)/shard_map/place_pages/pallas_call | solution.py:253
  80.1 5.7 %collective-permute-done = bf16[16,4096]{1,0:T(8,128)(2,1)S(1)} collective-permute-done((bf16[16,4096]{1,0:T(8,128)(2,1)S(1)}, bf16[16,4096]{1,0:T(8,128)(2,1)S(1)}, u32[]{:S(2)}, u32[]{:S(2)}) %collective-permute-start) | collective-permute-done | bytes 131104 | tf_op jit(solution)/shard_map/ppermute | solution.py:266
  85.9 0.8 reshape.48
  (3 shorter events, 0.1 us)
Async XLA Ops:
  0.6 14.6 %copy-start = (s32[16,16,2]{1,2,0:T(2,128)S(1)}, s32[16,16,2]{1,2,0:T(2,128)}, u32[]{:S(2)}) copy-start(s32[16,16,2]{1,2,0:T(2,128)} %param.16) | copy-start | bytes 6148
  1.5 1.6 %copy-start.1 = (bf16[1,256,2,1,16,128]{5,4,3,2,1,0:T(8,128)(2,1)S(1)}, bf16[1,256,2,1,16,128]{5,4,3,2,1,0:T(8,128)(2,1)}, u32[]{:S(2)}) copy-start(bf16[1,256,2,1,16,128]{5,4,3,2,1,0:T(8,128)(2,1)} %param.12) | copy-start | bytes 6291460
  3.1 12.9 %copy-start.16 = (s32[64,4]{0,1:T(4,128)S(1)}, s32[64,4]{0,1:T(4,128)}, u32[]{:S(2)}) copy-start(s32[64,4]{0,1:T(4,128)} %param.15) | copy-start | bytes 3076
  3.1 13.1 %copy-start.14 = (bf16[1,64,2,1024]{3,2,1,0:T(2,128)(2,1)S(1)}, bf16[1,64,2,1024]{3,2,1,0:T(2,128)(2,1)}, u32[]{:S(2)}) copy-start(bf16[1,64,2,1024]{3,2,1,0:T(2,128)(2,1)} %param.10) | copy-start | bytes 786436
  5.5 1.0 %copy-start.3 = (bf16[128,2,16,128]{3,2,1,0:T(8,128)(2,1)}, bf16[128,2,16,128]{3,2,1,0:T(8,128)(2,1)S(1)}, u32[]{:S(2)}) copy-start(bf16[128,2,16,128]{3,2,1,0:T(8,128)(2,1)S(1)} %gather_pages.1) | copy-start | bytes 3145732
  6.5 11.4 %copy-start.2 = (bf16[1,256,2,1,16,128]{5,4,3,2,1,0:T(8,128)(2,1)S(1)}, bf16[1,256,2,1,16,128]{5,4,3,2,1,0:T(8,128)(2,1)}, u32[]{:S(2)}) copy-start(bf16[1,256,2,1,16,128]{5,4,3,2,1,0:T(8,128)(2,1)} %param.12) | copy-start | bytes 6291460
  6.5 11.5 %copy-start.13 = (s32[64]{0:T(128)S(1)}, s32[64]{0:T(128)}, u32[]{:S(2)}) copy-start(s32[64]{0:T(128)} %lengths.3) | copy-start | bytes 772
  6.5 35.4 %all-to-all-start = ((bf16[16,8,2,16,128]{4,3,2,1,0:T(8,128)(2,1)}), bf16[16,8,2,16,128]{4,3,2,1,0:T(8,128)(2,1)S(1)}, u32[]{:S(2)}, u32[]{:S(2)}) async-start(bf16[16,8,2,16,128]{4,3,2,1,0:T(8,128)(2,1)} %bitcast.23), calls=%async_computation | async-start | bytes 2097152 | tf_op jit(solution)/shard_map/all_to_all | solution.py:203
  18.0 1.0 %copy-start.4 = (f32[128,1024]{1,0:T(8,128)S(1)}, f32[128,1024]{1,0:T(8,128)}, u32[]{:S(2)}) copy-start(f32[128,1024]{1,0:T(8,128)} %reshape.51.query) | copy-start | bytes 1572868
  32.4 0.8 copy-start.5
  33.2 0.7 copy-start.7
  33.9 0.7 copy-start.9
  34.7 0.7 copy-start.11
  41.9 1.0 %copy-start.6 = (f32[128,1024]{1,0:T(8,128)S(1)}, f32[128,1024]{1,0:T(8,128)}, u32[]{:S(2)}) copy-start(f32[128,1024]{1,0:T(8,128)} %copy-done.5) | copy-start | bytes 1572868
  42.9 0.9 %copy-start.8 = (f32[8,64,128]{2,1,0:T(8,128)S(1)}, f32[8,64,128]{2,1,0:T(8,128)}, u32[]{:S(2)}) copy-start(f32[8,64,128]{2,1,0:T(8,128)} %copy-done.7) | copy-start | bytes 786436
  43.9 0.9 %copy-start.10 = (f32[8,64,128]{2,1,0:T(8,128)S(1)}, f32[8,64,128]{2,1,0:T(8,128)}, u32[]{:S(2)}) copy-start(f32[8,64,128]{2,1,0:T(8,128)} %copy-done.9) | copy-start | bytes 786436
  44.8 0.9 %copy-start.12 = (bf16[8,64,128]{2,1,0:T(8,128)(2,1)S(1)}, bf16[8,64,128]{2,1,0:T(8,128)(2,1)}, u32[]{:S(2)}) copy-start(bf16[8,64,128]{2,1,0:T(8,128)(2,1)} %copy-done.11) | copy-start | bytes 393220
  54.8 5.2 %copy-start.15 = (bf16[8,2,4096]{2,1,0:T(2,128)(2,1)S(1)}, bf16[8,2,4096]{2,1,0:T(2,128)(2,1)}, u32[]{:S(2)}) copy-start(bf16[8,2,4096]{2,1,0:T(2,128)(2,1)} %param.9) | copy-start | bytes 393220
  54.8 22.0 %all-to-all-start.1 = ((bf16[8,16,4096]{2,1,0:T(8,128)(2,1)}), bf16[8,16,4096]{2,1,0:T(8,128)(2,1)S(1)}, u32[]{:S(2)}, u32[]{:S(2)}) async-start(bf16[8,16,4096]{2,1,0:T(8,128)(2,1)} %bitcast.4), calls=%async_computation.1 | async-start | bytes 2097152 | tf_op jit(solution)/shard_map/all_to_all | solution.py:250
  76.9 8.9 %collective-permute-start = (bf16[16,4096]{1,0:T(8,128)(2,1)S(1)}, bf16[16,4096]{1,0:T(8,128)(2,1)S(1)}, u32[]{:S(2)}, u32[]{:S(2)}) collective-permute-start(bf16[16,4096]{1,0:T(8,128)(2,1)S(1)} %add_convert_fusion.1), channel_id=1, source_target_pairs={{0,1},{2,3},{4,5},{6,7},{8,9},{10,11},{12,13},{14,15},{16,17},{18,... | collective-permute-start | bytes 393224 | tf_op jit(solution)/shard_map/ppermute | solution.py:266

commit v2 on v1

v2 whole, which is shorter than its diff:
```python
import functools
import math

import jax
import jax.numpy as jnp
from jax import lax
from jax.experimental import pallas as pl
from jax.experimental.pallas import tpu as pltpu
from jax.sharding import PartitionSpec as P

SMEM = pl.BlockSpec(memory_space=pltpu.SMEM)
VMEM = pl.BlockSpec(memory_space=pltpu.VMEM)
ANY = pl.BlockSpec(memory_space=pl.ANY)
MASKED = -1e30
HBM = pl.BlockSpec(memory_space=pltpu.HBM)
MIB = 1024 * 1024
BF16 = jnp.bfloat16
F32 = jnp.float32


def iota(shape, axis):
    return lax.broadcasted_iota(jnp.int32, shape, axis)


def dot_last(a, b):
    return lax.dot_general(a, b, (((1,), (1,)), ((), ())), preferred_element_type=F32)


def fresh_part(query, keys, values, bias, scale):
    score = dot_last(query, keys) * scale + bias
    top = jnp.max(score, axis=1, keepdims=True)
    weight = jnp.exp(score - top)
    total = jnp.sum(weight, axis=1, keepdims=True)
    return top, total, jnp.dot(weight.astype(BF16), values, preferred_element_type=F32)


def group_bias():
    row, col = iota((64, 256), 0), iota((64, 256), 1)
    return jnp.where(row // 2 % 4 == col // 64, 0.0, MASKED)


def limit_bias(limits):
    col = iota((8, 256), 1)
    request, token = col // 64, col % 64
    limit = jnp.where(request == 0, limits[0], limits[1])
    limit = jnp.where(request == 2, limits[2], limit)
    limit = jnp.where(request == 3, limits[3], limit)
    return jnp.where(token < limit, 0.0, MASKED)[:1]


def cached_part(query, keys, values, bias, fresh, scale):
    fresh_top, fresh_total, fresh_sum = fresh
    score = dot_last(query, keys) * scale + bias
    top = jnp.maximum(jnp.max(score, axis=1, keepdims=True), fresh_top)
    weight = jnp.exp(score - top)
    rescale = jnp.exp(fresh_top - top)
    total = jnp.sum(weight, axis=1, keepdims=True) + fresh_total * rescale
    summed = jnp.dot(weight.astype(BF16), values, preferred_element_type=F32)
    return (summed + fresh_sum * rescale) / total


def stacked(ref, start):
    part = ref[:, pl.ds(start, 8), :]
    return part.reshape(part.shape[0] * 8, part.shape[2])


def gather_kernel(pages, pool, same_core, other_core):
    me = lax.axis_index("inst")
    moves, span, targets = pages.shape
    for distance in range(targets // 2):
        position = lax.rem(me // 2 + distance, targets // 2) * 2
        for core, out in ((lax.rem(me, 2), same_core), (1 - lax.rem(me, 2), other_core)):
            for index in range(moves * span):
                page = pages[index // span, index % span, position + core]
                out[distance, index] = pool[page]


GROUPS = (
    ((0, False), None),
    ((2, True), (2, False)),
    ((-2, True), (-2, False)),
    ((1, True), (1, False)),
    ((-1, True), (-1, False)),
    ((3, True), (3, False)),
    ((-3, True), (-3, False)),
    ((4, True), (-4, False)),
)
EARLY = 3


def arrival_slots(moves):
    me = lax.axis_index("inst")
    ring, core = moves.shape[0] // 2, lax.rem(me, 2)
    out = []
    for group in GROUPS:
        for block in group:
            if block is None:
                out += [jnp.int32(-1)] * moves.shape[1]
                continue
            distance, same = block
            source = lax.rem(me // 2 + ring - distance, ring) * 2 + (core if same else 1 - core)
            out += [moves[source, move, me] for move in range(moves.shape[1])]
    return out


def spread(index, values):
    out = jnp.full(index.shape, -1, jnp.int32)
    for position, value in enumerate(values):
        out = jnp.where(index == position, value, out)
    return out


def local_kernel(
    scale, table, lengths, moves, query, fresh, pool,
    attended, early_place, late_place,
    arrival_query, arrival_top, arrival_total, arrival_sum, pool_copy,
    heads_query, heads_top, heads_total, heads_sum, found, sem,
):
    copy = pltpu.make_async_copy(pool, pool_copy, sem)
    copy.start()
    head_dim = pool.shape[-1]
    rows = query.shape[0]
    heads = query.shape[1] // head_dim
    fresh_keys = fresh[:, :head_dim].astype(BF16)
    fresh_values = fresh[:, head_dim:].astype(BF16)
    arrivals = arrival_slots(moves)

    shape = (arrival_query.shape[1], rows)
    row, col = iota(shape, 0), iota(shape, 1)
    wanted = spread(row // 2, arrivals)
    pick = jnp.where(wanted * 2 + row % 2 == col, 1.0, 0.0).astype(BF16)
    seen = (jnp.maximum(wanted, 0) == col // 2) & (col % 2 <= row % 2)
    arrival_bias = jnp.where(seen, 0.0, MASKED)
    row, col = iota((rows, rows), 0), iota((rows, rows), 1)
    local_bias = jnp.where((row // 2 == col // 2) & (col % 2 <= row % 2), 0.0, MASKED)
    for h in range(heads):
        part = query[:, h * head_dim : (h + 1) * head_dim]
        chosen = jnp.dot(pick, part.astype(BF16), preferred_element_type=F32)
        for rows_in, bias, into in (
            (part, local_bias, (heads_query, heads_top, heads_total, heads_sum)),
            (chosen, arrival_bias, (arrival_query, arrival_top, arrival_total, arrival_sum)),
        ):
            top, total, summed = fresh_part(
                rows_in.astype(BF16), fresh_keys, fresh_values, bias, scale
            )
            into[0][h] = rows_in
            into[1][h] = jnp.broadcast_to(top, summed.shape)
            into[2][h] = jnp.broadcast_to(total, summed.shape)
            into[3][h] = summed

    base = group_bias()

    def one_group(group, carry):
        start = pl.multiple_of(group * 8, 8)
        part = (
            stacked(heads_top, start)[:, :1],
            stacked(heads_total, start)[:, :1],
            stacked(heads_sum, start),
        )
        pages = [table[i % 4, group * 4 + i // 4] for i in range(16)]
        keys = jnp.concatenate([pool[page, 0] for page in pages], axis=0)
        values = jnp.concatenate([pool[page, 1] for page in pages], axis=0)
        bias = base + limit_bias([lengths[group * 4 + i] for i in range(4)])
        rows_in = stacked(heads_query, start).astype(BF16)
        out = cached_part(rows_in, keys, values, bias, part, scale)
        for h in range(heads):
            found[pl.ds(start, 8), h * head_dim : (h + 1) * head_dim] = out[h * 8 : h * 8 + 8]
        return carry

    lax.fori_loop(0, rows // 8, one_group, 0, unroll=4)
    shape = (rows, arrival_query.shape[1])
    row, col = iota(shape, 0), iota(shape, 1)
    placed = jnp.where(spread(col // 2, arrivals) * 2 + col % 2 == row, 1.0, 0.0)
    early = early_place.shape[1]
    early_place[...] = placed[:, :early].astype(BF16)
    late_place[...] = placed[:, early:].astype(BF16)
    taken = jnp.sum(placed, axis=1, keepdims=True) > 0
    attended[...] = jnp.where(taken, 0.0, found[...]).astype(BF16)
    copy.wait()


def arrival_kernel(scale, first, places, *refs):
    lengths, moves = refs[:2]
    arrays = refs[2:-8]
    arrival_query, arrival_top, arrival_total, arrival_sum, attended, place, out, found = refs[-8:]
    arrival_rows(scale, first, places, lengths, moves, arrays, refs[-8:-4], found)
    moved = jnp.dot(place[...], found[...].astype(BF16), preferred_element_type=F32)
    out[...] = (attended[...].astype(F32) + moved).astype(BF16)


def arrival_rows(scale, first, places, lengths, moves, arrays, parts, found):
    arrival_query, arrival_top, arrival_total, arrival_sum = parts
    heads, _, head_dim = arrival_query.shape
    arrivals = arrival_slots(moves)[first * 4 :]
    base = group_bias()
    for position, blocks in enumerate(places):
        start = (first + position) * 8
        slots = arrivals[position * 4 : position * 4 + 4]
        limits = [jnp.where(slot < 0, 0, lengths[jnp.maximum(slot, 0)]) for slot in slots]
        held = [arrays[array][index] for array, index in blocks]
        keys = jnp.concatenate([block[:, 0].reshape(128, head_dim) for block in held], axis=0)
        values = jnp.concatenate([block[:, 1].reshape(128, head_dim) for block in held], axis=0)
        part = (
            stacked(arrival_top, start)[:, :1],
            stacked(arrival_total, start)[:, :1],
            stacked(arrival_sum, start),
        )
        bias = base + limit_bias(limits)
        rows_in = stacked(arrival_query, start).astype(BF16)
        result = cached_part(rows_in, keys, values, bias, part, scale)
        for h in range(heads):
            found[position * 8 : position * 8 + 8, h * head_dim : (h + 1) * head_dim] = result[
                h * 8 : h * 8 + 8
            ]


def project_kernel(scale, first, places, *refs):
    lengths, moves = refs[:2]
    arrays = refs[2:-9]
    attended, place, weight, out, found = refs[-5:]
    arrival_rows(scale, first, places, lengths, moves, arrays, refs[-9:-5], found)
    moved = jnp.dot(place[...], found[...].astype(BF16), preferred_element_type=F32)
    rows = (attended[...].astype(F32) + moved).astype(BF16)
    step = 512
    for start in range(0, out.shape[1], step):
        span = slice(start, start + step)
        product = jnp.dot(rows, weight[:, span], preferred_element_type=F32)
        out[:, span] = product.astype(BF16)


def place_kernel(first, places, *refs):
    table, moves = refs[:2]
    arrays = refs[2:-3]
    pool, sems = refs[-2:]
    slots = arrival_slots(moves)[first * 4 :]
    work = []
    for position, blocks in enumerate(places):
        for half, (array, index) in enumerate(blocks):
            if GROUPS[first + position][half] is None:
                continue
            for move in range(2):
                number = position * 4 + half * 2 + move
                work.append((slots[number], arrays[array], index, move * 4, sems.at[number]))

    for slot, array, index, start, sem in work:

        @pl.when(slot >= 0)
        def _(slot=slot, array=array, index=index, start=start, sem=sem):
            for page in range(4):
                target = pool.at[table[page, jnp.maximum(slot, 0)]]
                pltpu.make_async_copy(array.at[index, start + page], target, sem).start()

    for slot, array, index, start, sem in work:

        @pl.when(slot >= 0)
        def _(array=array, index=index, start=start, sem=sem):
            span = array.at[index, pl.ds(start, 4)]
            pltpu.make_async_copy(span, span, sem).wait()


def shards(
    residual, queries, new_kv, kv_pool, out_weight, lengths, page_table, move_slot, move_pages
):
    n_tp = lax.axis_size("tp")
    pages, _, _, page_len, head_dim = kv_pool.shape[1:]
    slots, steps, width = queries.shape[1:]
    rows = slots * steps
    scale = 1.0 / math.sqrt(head_dim)
    pool = kv_pool.reshape(pages, 2, page_len, head_dim)
    table = page_table.T
    moves = move_slot.transpose(0, 2, 1)
    sources, cap, _ = moves.shape
    count = sources * cap
    moved = count * page_table.shape[1]

    ring = sources // 2
    block_shape = (ring, moved // sources, 2, page_len, head_dim)
    query = queries.reshape(rows, width).astype(F32)
    wanted, query = lax.optimization_barrier((move_pages[0].transpose(1, 2, 0), query))
    same_core, other_core = pl.pallas_call(
        gather_kernel,
        out_shape=[jax.ShapeDtypeStruct(block_shape, BF16)] * 2,
        in_specs=[SMEM, VMEM],
        out_specs=[VMEM, VMEM],
        compiler_params=pltpu.CompilerParams(vmem_limit_bytes=MIB),
        cost_estimate=pl.CostEstimate(flops=0, bytes_accessed=2**21, transcendentals=0),
        name="gather_pages",
    )(wanted, pool)
    crossed = lax.ppermute(other_core, "inst", [(index, index ^ 1) for index in range(sources)])

    def pair(distance):
        index = distance % ring
        return [same_core[index : index + 1], crossed[index : index + 1]]

    def along_ring(blocks, distance):
        pairs = [
            (2 * position + core, 2 * ((position + distance) % ring) + core)
            for position in range(ring)
            for core in range(2)
        ]
        return lax.ppermute(jnp.concatenate(blocks, axis=0), "inst", pairs)

    up2 = along_ring(pair(2) + pair(3) + pair(4)[:1], 2)
    down2 = along_ring(pair(-2) + pair(-3) + pair(4)[1:], -2)
    early_arrays = [crossed, up2, down2]
    early_places = [[(0, 0), (0, 0)]] + [[(i, 0), (i, 1)] for i in range(1, EARLY)]
    late_places = [[(i, j), (i, j + 1)] for j in (0, 2) for i in (0, 1)] + [[(2, 0), (3, 0)]]

    groups = len(GROUPS)
    fresh = new_kv.reshape(rows, 2 * head_dim).astype(F32)
    heads = width // head_dim
    part_shape = jax.ShapeDtypeStruct((heads, groups * 8, head_dim), F32)
    heads_scratch = pltpu.VMEM((heads, rows, head_dim), F32)
    attended, early_place, late_place, arrival_query, top, total, summed, pool_copy = pl.pallas_call(
        functools.partial(local_kernel, scale),
        out_shape=[
            jax.ShapeDtypeStruct((rows, width), BF16),
            jax.ShapeDtypeStruct((rows, EARLY * 8), BF16),
            jax.ShapeDtypeStruct((rows, (groups - EARLY) * 8), BF16),
            part_shape,
            part_shape,
            part_shape,
            part_shape,
            jax.ShapeDtypeStruct(pool.shape, BF16),
        ],
        in_specs=[SMEM, SMEM, SMEM, VMEM, VMEM, VMEM],
        out_specs=[VMEM] * 7 + [HBM],
        scratch_shapes=[heads_scratch] * 4
        + [pltpu.VMEM((rows, width), F32), pltpu.SemaphoreType.DMA(())],
        compiler_params=pltpu.CompilerParams(vmem_limit_bytes=8 * MIB),
        cost_estimate=pl.CostEstimate(flops=2**28, bytes_accessed=2**24, transcendentals=2**18),
        name="local_attention",
    )(table, lengths, moves, query, fresh, pool)

    near1, near7, attended = lax.optimization_barrier((pair(1), pair(-1), attended))
    late_arrays = [
        along_ring(near1 + [up2[2:4]], 1),
        along_ring(near7 + [down2[2:4]], -1),
        along_ring([up2[4:]], 2),
        along_ring([down2[4:]], -2),
    ]

    def arrival(kernel, name, first, arrays, places, others, out_shape, limit):
        return pl.pallas_call(
            functools.partial(kernel, scale, first, places),
            out_shape=out_shape,
            in_specs=[SMEM, SMEM] + [VMEM] * (len(arrays) + 4 + len(others)),
            out_specs=VMEM,
            scratch_shapes=[pltpu.VMEM((len(places) * 8, width), F32)],
            compiler_params=pltpu.CompilerParams(vmem_limit_bytes=limit),
            cost_estimate=pl.CostEstimate(
                flops=2**26, bytes_accessed=2**21, transcendentals=2**16
            ),
            name=name,
        )(lengths, moves, *arrays, arrival_query, top, total, summed, *others)

    def place_pages(first, arrays, places, held):
        return pl.pallas_call(
            functools.partial(place_kernel, first, places),
            out_shape=jax.ShapeDtypeStruct(pool.shape, BF16),
            in_specs=[SMEM, SMEM] + [ANY] * len(arrays) + [HBM],
            out_specs=HBM,
            input_output_aliases={2 + len(arrays): 0},
            scratch_shapes=[pltpu.SemaphoreType.DMA((len(places) * 4,))],
            compiler_params=pltpu.CompilerParams(vmem_limit_bytes=MIB),
            cost_estimate=pl.CostEstimate(flops=0, bytes_accessed=2**21, transcendentals=0),
            name="place_pages",
        )(table, moves, *arrays, held)

    attended = arrival(
        arrival_kernel, "arrival_attention", 0, early_arrays, early_places,
        (attended, early_place), jax.ShapeDtypeStruct((rows, width), BF16), 4 * MIB,
    )
    weight = out_weight[0]
    contribution = arrival(
        project_kernel, "project", EARLY, late_arrays, late_places,
        (attended, late_place, weight),
        jax.ShapeDtypeStruct((rows, weight.shape[1]), BF16), 4 * MIB,
    )
    pool_after = place_pages(0, early_arrays, early_places, pool_copy)
    pool_after = place_pages(EARLY, late_arrays, late_places, pool_after)

    model = contribution.shape[1]
    own = rows // n_tp
    received = lax.all_to_all(
        contribution.reshape(n_tp, own, model), "tp", split_axis=0, concat_axis=0, tiled=True
    )
    branch = jnp.sum(received.astype(F32), axis=0)
    first_out = (residual.reshape(own, model).astype(F32) + branch).astype(BF16)
    first_out, pool_after = lax.optimization_barrier((first_out, pool_after))
    passed = lax.ppermute(first_out, "pp", [(0, 1)])
    second_out = (passed.astype(F32) + branch).astype(BF16)
    hidden_out = jnp.where(lax.axis_index("pp") == 0, first_out, second_out)
    return (hidden_out.reshape((1,) + residual.shape), pool_after.reshape(kv_pool.shape))


def solution(mesh):
    return jax.shard_map(
        shards,
        mesh=mesh,
        in_specs=(
            P(("inst", "tp"), None, None),
            P("pp", "inst", None, "tp"),
            P("pp", "inst", None, None, "tp"),
            P("pp", "inst", None, "tp", None, None),
            P("pp", "tp", None),
            P("inst"),
            P("inst", None),
            P(),
            P("inst", None, None, None),
        ),
        out_specs=(P("pp", ("inst", "tp"), None, None), P("pp", "inst", None, "tp", None, None)),
        check_vma=False,
    )
```

time: 87.3 us -> 76 us (0.87)
  local copies, waits for them, and re-layouts: 14.7 us -> 4.33 us
  starting transfers between devices: 15.1 us -> 23.5 us
  matrix products: 5.65 us -> 0 us
  waiting for transfers between devices: 29.1 us -> 25.6 us
    ppermute x0 -> x7, starting transfers between devices: none -> 17 us  [the longest x6 17 us: along_ring(): return lax.ppermute(jnp.concatenate(blocks, axis=0), 'inst', pairs)]
    unnamed x37 -> x24, local copies, waits for them, and re-layouts: 12.1 us -> 2.4 us
    all_to_all x1 -> x0, starting transfers between devices: 8.7 us -> none  [shards(): lax.all_to_all(outgoing.reshape(sources, moved // sources, 2, page_len, h...]
    ppermute x0 -> x7, waiting for transfers between devices: none -> 7.63 us  [the longest x6 5.75 us: along_ring(): return lax.ppermute(jnp.concatenate(blocks, axis=0), 'inst', pairs)]
    all_to_all x1 -> x0, waiting for transfers between devices: 6.56 us -> none  [shards(): lax.all_to_all(outgoing.reshape(sources, moved // sources, 2, page_len, h...]
    all_to_all x1, waiting for transfers between devices: 16.8 us -> 10.8 us  [shards(): lax.all_to_all(contribution.reshape(n_tp, own, model), 'tp', split_axis=0...]
    dot_general x1 -> x0, matrix products: 5.65 us -> none  [shards(): jnp.dot(attended, out_weight[0], preferred_element_type=F32).astype(BF16)]
    ppermute x1, waiting for transfers between devices: 5.75 us -> 7.15 us  [shards(): passed = lax.ppermute(first_out, 'pp', [(0, 1)])]
  transfers between devices with their start and end apart: 3 -> 9, of which waited for: 3 -> 6; matrix products, arithmetic and copies ran while one was open for 3% -> 0% of each run, Pallas kernels for 18% -> 20%
where the time goes in v2:
time: 76 us; the launch traced here: 75.8 us
  waiting for transfers between devices  25.6 us (34%)
  starting transfers between devices  23.5 us (31%)
  Pallas kernels  21.2 us (28%)
  local copies, waits for them, and re-layouts  4.33 us (6%)
  between operations  0.88 us (1%)
    ppermute x6, starting transfers between devices, along_ring(): return lax.ppermute(jnp.concatenate(blocks, axis=0), 'inst', pairs)  17 us
    all_to_all x1, waiting for transfers between devices, shards(): lax.all_to_all(contribution.reshape(n_tp, own, model), 'tp', split_axis=0...  10.8 us
    pallas_call x1, Pallas kernels, shards(): pl.pallas_call(functools.partial(local_kernel, scale), out_shape=[jax.Sha...  9.57 us
    ppermute x1, waiting for transfers between devices, shards(): passed = lax.ppermute(first_out, 'pp', [(0, 1)])  7.15 us
    pallas_call x2, Pallas kernels, arrival(): pl.pallas_call(functools.partial(kernel, scale, first, places), out_shape...  7.13 us
    ppermute x6, waiting for transfers between devices, along_ring(): return lax.ppermute(jnp.concatenate(blocks, axis=0), 'inst', pairs)  5.75 us
    all_to_all x1, starting transfers between devices, shards(): lax.all_to_all(contribution.reshape(n_tp, own, model), 'tp', split_axis=0...  5.15 us
    pallas_call x2, Pallas kernels, place_pages(): pl.pallas_call(functools.partial(place_kernel, first, places), out_shape=...  3.7 us
  transfers between devices with their start and end apart: 9, of which 6 were waited for; matrix products, arithmetic and copies ran while one was open for 0% of the time, Pallas kernels for 20%

profile of v2, /device:TPU:16, one launch (start us, length us, event | category | flops | bytes accessed | tf_op | source)
XLA Modules:
  0.0 75.8 jit_solution(7758173393759490063)
XLA Ops:
  0.6 0.0 copy-start.8
  0.6 0.0 copy-start.3
  0.7 1.1 %reshape.30.query = f32[128,1024]{1,0:T(8,128)S(1)} reshape(bf16[1,64,2,1024]{3,2,1,0:T(2,128)(2,1)} %param.10) | data formatting | bytes 786432 | tf_op jit(solution)/shard_map/convert_element_type | solution.py:278
  1.7 0.0 copy-start.4
  1.7 0.0 copy-start.5
  1.7 0.0 copy-start.1
  1.7 1.6 %copy-done.1 = bf16[1,256,2,1,16,128]{5,4,3,2,1,0:T(8,128)(2,1)S(1)} copy-done((bf16[1,256,2,1,16,128]{5,4,3,2,1,0:T(8,128)(2,1)S(1)}, bf16[1,256,2,1,16,128]{5,4,3,2,1,0:T(8,128)(2,1)}, u32[]{:S(2)}) %copy-start.1) | copy-done | bytes 2097176
  3.3 0.0 copy-start.6
  3.3 0.7 copy-done.6
  4.0 0.0 copy-start.2
  4.0 0.8 %gather_pages.1 = (bf16[8,8,2,16,128]{4,3,2,1,0:T(8,128)(2,1)S(1)}, bf16[8,8,2,16,128]{4,3,2,1,0:T(8,128)(2,1)S(1)}) custom-call(s32[2,4,16]{2,1,0:T(4,128)S(1)} %bitcast.29, bf16[256,2,16,128]{3,2,1,0:T(8,128)(2,1)S(1)} %bitcast.18), custom_call_target="tpu_custom_call" | custom-call | bytes 2097152 | tf_op jit(solution)/shard_map/gather_pages/pallas_call | solution.py:280
  4.8 0.1 collective-permute-start
  5.0 1.9 %collective-permute-done.refs_2_ = bf16[8,8,2,16,128]{4,3,2,1,0:T(8,128)(2,1)S(1)} collective-permute-done((bf16[8,8,2,16,128]{4,3,2,1,0:T(8,128)(2,1)S(1)}, bf16[8,8,2,16,128]{4,3,2,1,0:T(8,128)(2,1)S(1)}, u32[]{:S(2)}, u32[]{:S(2)}) %collective-permute-start) | collective-permute-done | bytes 524320 | tf_op jit(solution)/shard_map/ppermute | solution.py:289
  6.9 0.0 copy-start
  7.0 3.3 %collective-permute-start.1 = (bf16[5,8,2,16,128]{4,3,2,1,0:T(8,128)(2,1)S(1)}, bf16[5,8,2,16,128]{4,3,2,1,0:T(8,128)(2,1)S(1)}, u32[]{:S(2)}, u32[]{:S(2)}) collective-permute-start(bf16[5,8,2,16,128]{4,3,2,1,0:T(8,128)(2,1)S(1)} %slice_dynamic-update-slice_fusion.7), channel_id=1, source_target_pairs={{0,64},{16,80},{32,96},{48,112},{64,128},{80,144},{96,160},{112,17... | collective-permute-start | bytes 983048 | tf_op jit(solution)/shard_map/ppermute | solution.py:301
  10.4 3.1 %collective-permute-start.3 = (bf16[5,8,2,16,128]{4,3,2,1,0:T(8,128)(2,1)S(1)}, bf16[5,8,2,16,128]{4,3,2,1,0:T(8,128)(2,1)S(1)}, u32[]{:S(2)}, u32[]{:S(2)}) collective-permute-start(bf16[5,8,2,16,128]{4,3,2,1,0:T(8,128)(2,1)S(1)} %get-tuple-element.42), channel_id=1, source_target_pairs={{0,192},{16,208},{32,224},{48,240},{64,0},{80,16},{96,32},{112,48}... | collective-permute-start | bytes 983048 | tf_op jit(solution)/shard_map/ppermute | solution.py:301
  13.5 0.0 copy-done.8
  13.5 0.0 copy-done.3
  13.5 0.0 copy-done.4
  13.5 0.0 copy-done.5
  13.5 0.0 copy-done.2
  13.5 9.6 %local_attention.1 = (bf16[128,1024]{1,0:T(8,128)(2,1)S(1)}, bf16[128,24]{1,0:T(8,128)(2,1)S(1)}, bf16[128,40]{1,0:T(8,128)(2,1)S(1)}, f32[8,64,128]{2,1,0:T(8,1...) custom-call(s32[4,64]{1,0:T(4,128)S(1)} %bitcast.26, ...), custom_call_target="tpu_custom_call" | custom-call | flops 268435456 | bytes 16777216 | tf_op jit(solution)/shard_map/local_attention/pallas_call | solution.py:314
  23.1 1.0 %collective-permute-done.1.refs_3_ = bf16[5,8,2,16,128]{4,3,2,1,0:T(8,128)(2,1)S(1)} collective-permute-done((bf16[5,8,2,16,128]{4,3,2,1,0:T(8,128)(2,1)S(1)}, bf16[5,8,2,16,128]{4,3,2,1,0:T(8,128)(2,1)S(1)}, u32[]{:S(2)}, u32[]{:S(2)}) %collective-permute-start.1) | collective-permute-done | bytes 327712 | tf_op jit(solution)/shard_map/ppermute | solution.py:301
  24.2 5.4 %collective-permute-start.2 = (bf16[4,8,2,16,128]{4,3,2,1,0:T(8,128)(2,1)S(1)}, bf16[4,8,2,16,128]{4,3,2,1,0:T(8,128)(2,1)S(1)}, u32[]{:S(2)}, u32[]{:S(2)}) collective-permute-start(bf16[4,8,2,16,128]{4,3,2,1,0:T(8,128)(2,1)S(1)} %pad_maximum_fusion), channel_id=1, source_target_pairs={{0,32},{16,48},{32,64},{48,80},{64,96},{80,112},{96,128},{112,144}... | collective-permute-start | bytes 786440 | tf_op jit(solution)/shard_map/ppermute | solution.py:301
  29.6 0.0 collective-permute-done.3.refs_4_
  29.6 0.9 %collective-permute-start.4 = (bf16[4,8,2,16,128]{4,3,2,1,0:T(8,128)(2,1)S(1)}, bf16[4,8,2,16,128]{4,3,2,1,0:T(8,128)(2,1)S(1)}, u32[]{:S(2)}, u32[]{:S(2)}) collective-permute-start(bf16[4,8,2,16,128]{4,3,2,1,0:T(8,128)(2,1)S(1)} %pad_maximum_fusion.1), channel_id=1, source_target_pairs={{0,224},{16,240},{32,0},{48,16},{64,32},{80,48},{96,64},{112,80},{... | collective-permute-start | bytes 786440 | tf_op jit(solution)/shard_map/ppermute | solution.py:301
  30.6 3.0 %collective-permute-start.5 = (bf16[1,8,2,16,128]{4,3,2,1,0:T(8,128)(2,1)S(1)}, bf16[1,8,2,16,128]{4,3,2,1,0:T(8,128)(2,1)S(1)}, u32[]{:S(2)}, u32[]{:S(2)}) collective-permute-start(bf16[1,8,2,16,128]{4,3,2,1,0:T(8,128)(2,1)S(1)} %slice.81), channel_id=1, source_target_pairs={{0,64},{16,80},{32,96},{48,112},{64,128},{80,144},{96,160},{112,17... | collective-permute-start | bytes 196616 | tf_op jit(solution)/shard_map/ppermute | solution.py:301
  33.6 1.1 %collective-permute-start.6 = (bf16[1,8,2,16,128]{4,3,2,1,0:T(8,128)(2,1)S(1)}, bf16[1,8,2,16,128]{4,3,2,1,0:T(8,128)(2,1)S(1)}, u32[]{:S(2)}, u32[]{:S(2)}) collective-permute-start(bf16[1,8,2,16,128]{4,3,2,1,0:T(8,128)(2,1)S(1)} %slice.82), channel_id=1, source_target_pairs={{0,192},{16,208},{32,224},{48,240},{64,0},{80,16},{96,32},{112,48}... | collective-permute-start | bytes 196616 | tf_op jit(solution)/shard_map/ppermute | solution.py:301
  34.7 2.2 %arrival_attention.1.refs_10_ = bf16[128,1024]{1,0:T(8,128)(2,1)S(1)} custom-call(s32[64]{0:T(128)S(1)} %copy-done.5, s32[16,2,16]{2,1,0:T(2,128)S(1)} %bitcast.22, bf16[8,8,2,16,128]{4,3,2,1,0:T(8,128)(2,1)S(1)} %collective-permute-done.refs_2_, bf16[5,8,2,16,128]{4,3,2,1,0:T(8,128)(2,1)S(1)} %collective-permute-done.1.refs_3_, ...), custom_call_target="tpu_custom_call" | custom-call | flops 67108864 | bytes 2097152 | tf_op jit(solution)/shard_map/arrival_attention/pallas_call | solution.py:344
  37.0 3.5 %collective-permute-done.5.refs_4_ = bf16[1,8,2,16,128]{4,3,2,1,0:T(8,128)(2,1)S(1)} collective-permute-done((bf16[1,8,2,16,128]{4,3,2,1,0:T(8,128)(2,1)S(1)}, bf16[1,8,2,16,128]{4,3,2,1,0:T(8,128)(2,1)S(1)}, u32[]{:S(2)}, u32[]{:S(2)}) %collective-permute-start.5) | collective-permute-done | bytes 65568 | tf_op jit(solution)/shard_map/ppermute | solution.py:301
  40.5 1.2 %collective-permute-done.6.refs_5_ = bf16[1,8,2,16,128]{4,3,2,1,0:T(8,128)(2,1)S(1)} collective-permute-done((bf16[1,8,2,16,128]{4,3,2,1,0:T(8,128)(2,1)S(1)}, bf16[1,8,2,16,128]{4,3,2,1,0:T(8,128)(2,1)S(1)}, u32[]{:S(2)}, u32[]{:S(2)}) %collective-permute-start.6) | collective-permute-done | bytes 65568 | tf_op jit(solution)/shard_map/ppermute | solution.py:301
  41.7 0.0 collective-permute-done.2.refs_2_
  41.7 0.0 collective-permute-done.4.refs_3_
  41.7 0.0 copy-done
  41.7 4.9 %project.1 = bf16[128,4096]{1,0:T(8,128)(2,1)} custom-call(s32[64]{0:T(128)S(1)} %copy-done.5, s32[16,2,16]{2,1,0:T(2,128)S(1)} %bitcast.23, bf16[4,8,2,16,128]{4,3,2,1,0:T(8,128)(2,1)S(1)} %collective-permute-done.2.refs_2_, bf16[4,8,2,16,128]{4,3,2,1,0:T(8,128)(2,1)S(1)} %collective-permute-done.4.refs_3_, ...), custom_call_target="tpu_custom_call" | custom-call | flops 67108864 | bytes 2097152 | tf_op jit(solution)/shard_map/project/pallas_call | solution.py:344
  46.6 0.0 copy-start.7
  46.6 5.1 %all-to-all-start = ((bf16[8,16,4096]{2,1,0:T(8,128)(2,1)}), bf16[8,16,4096]{2,1,0:T(8,128)(2,1)S(1)}, u32[]{:S(2)}, u32[]{:S(2)}) async-start(bf16[8,16,4096]{2,1,0:T(8,128)(2,1)} %bitcast.6), calls=%async_computation | async-start | bytes 2097152 | tf_op jit(solution)/shard_map/all_to_all | solution.py:385
  51.8 0.0 copy-done.7
  51.8 1.7 %place_pages.2.refs_6_ = bf16[256,2,16,128]{3,2,1,0:T(8,128)(2,1)} custom-call(s32[4,64]{1,0:T(4,128)S(1)} %bitcast.27, s32[16,2,16]{2,1,0:T(2,128)S(1)} %bitcast.24, bf16[8,8,2,16,128]{4,3,2,1,0:T(8,128)(2,1)S(1)} %collective-permute-done.refs_2_, bf16[5,8,2,16,128]{4,3,2,1,0:T(8,128)(2,1)S(1)} %collective-permute-done.1.refs_3_, ...), custom_call_target="tpu_custom_call", output_to_operand_aliasing={{}: (5, {})} | custom-call | bytes 2097152 | tf_op jit(solution)/shard_map/place_pages/pallas_call | solution.py:358
  53.5 2.0 %place_pages.3 = bf16[256,2,16,128]{3,2,1,0:T(8,128)(2,1)} custom-call(s32[4,64]{1,0:T(4,128)S(1)} %bitcast.28, s32[16,2,16]{2,1,0:T(2,128)S(1)} %bitcast.25, bf16[4,8,2,16,128]{4,3,2,1,0:T(8,128)(2,1)S(1)} %collective-permute-done.2.refs_2_, bf16[4,8,2,16,128]{4,3,2,1,0:T(8,128)(2,1)S(1)} %collective-permute-done.4.refs_3_, ...), custom_call_target="tpu_custom_call", output_to_operand_aliasing={{}: (6, {})} | custom-call | bytes 2097152 | tf_op jit(solution)/shard_map/place_pages/pallas_call | solution.py:358
  55.5 10.8 %all-to-all-done = bf16[8,16,4096]{2,1,0:T(8,128)(2,1)S(1)} async-done(((bf16[8,16,4096]{2,1,0:T(8,128)(2,1)}), bf16[8,16,4096]{2,1,0:T(8,128)(2,1)S(1)}, u32[]{:S(2)}, u32[]{:S(2)}) %all-to-all-start) | async-done | bytes 1048608 | tf_op jit(solution)/shard_map/all_to_all | solution.py:385
  66.3 0.1 convert_reduce_fusion
  66.5 1.3 %collective-permute-start.7 = (bf16[16,4096]{1,0:T(8,128)(2,1)S(1)}, bf16[16,4096]{1,0:T(8,128)(2,1)S(1)}, u32[]{:S(2)}, u32[]{:S(2)}) collective-permute-start(bf16[16,4096]{1,0:T(8,128)(2,1)S(1)} %add_convert_fusion.1), channel_id=1, source_target_pairs={{0,1},{2,3},{4,5},{6,7},{8,9},{10,11},{12,13},{14,15},{16,17},{18,... | collective-permute-start | bytes 393224 | tf_op jit(solution)/shard_map/ppermute | solution.py:391
  67.8 7.1 %collective-permute-done.7 = bf16[16,4096]{1,0:T(8,128)(2,1)S(1)} collective-permute-done((bf16[16,4096]{1,0:T(8,128)(2,1)S(1)}, bf16[16,4096]{1,0:T(8,128)(2,1)S(1)}, u32[]{:S(2)}, u32[]{:S(2)}) %collective-permute-start.7) | collective-permute-done | bytes 131104 | tf_op jit(solution)/shard_map/ppermute | solution.py:391
  75.0 0.8 %reshape.27 = bf16[1,8,2,4096]{3,2,1,0:T(2,128)(2,1)} reshape(bf16[16,4096]{1,0:T(8,128)(2,1)S(1)} %fusion) | data formatting | bytes 262144 | tf_op jit(solution)/shard_map/reshape | solution.py:394
  (17 shorter events, 0.3 us)
Async XLA Ops:
  0.6 12.8 %copy-start.8 = (bf16[1,64,2,2,128]{4,3,2,1,0:T(2,128)(2,1)S(1)}, bf16[1,64,2,2,128]{4,3,2,1,0:T(2,128)(2,1)}, u32[]{:S(2)}) copy-start(bf16[1,64,2,2,128]{4,3,2,1,0:T(2,128)(2,1)} %param.11) | copy-start | bytes 196612
  0.6 12.9 %copy-start.3 = (s32[16,16,2]{1,2,0:T(2,128)S(1)}, s32[16,16,2]{1,2,0:T(2,128)}, u32[]{:S(2)}) copy-start(s32[16,16,2]{1,2,0:T(2,128)} %param.16) | copy-start | bytes 6148
  1.7 11.8 %copy-start.4 = (s32[64,4]{0,1:T(4,128)S(1)}, s32[64,4]{0,1:T(4,128)}, u32[]{:S(2)}) copy-start(s32[64,4]{0,1:T(4,128)} %param.15) | copy-start | bytes 3076
  1.7 11.8 %copy-start.5 = (s32[64]{0:T(128)S(1)}, s32[64]{0:T(128)}, u32[]{:S(2)}) copy-start(s32[64]{0:T(128)} %refs_0_.3) | copy-start | bytes 772
  1.7 1.6 %copy-start.1 = (bf16[1,256,2,1,16,128]{5,4,3,2,1,0:T(8,128)(2,1)S(1)}, bf16[1,256,2,1,16,128]{5,4,3,2,1,0:T(8,128)(2,1)}, u32[]{:S(2)}) copy-start(bf16[1,256,2,1,16,128]{5,4,3,2,1,0:T(8,128)(2,1)} %param.12) | copy-start | bytes 6291460
  3.3 0.7 copy-start.6
  4.0 9.5 %copy-start.2 = (bf16[1,256,2,1,16,128]{5,4,3,2,1,0:T(8,128)(2,1)S(1)}, bf16[1,256,2,1,16,128]{5,4,3,2,1,0:T(8,128)(2,1)}, u32[]{:S(2)}) copy-start(bf16[1,256,2,1,16,128]{5,4,3,2,1,0:T(8,128)(2,1)} %param.12) | copy-start | bytes 6291460
  4.8 2.0 %collective-permute-start = (bf16[8,8,2,16,128]{4,3,2,1,0:T(8,128)(2,1)S(1)}, bf16[8,8,2,16,128]{4,3,2,1,0:T(8,128)(2,1)S(1)}, u32[]{:S(2)}, u32[]{:S(2)}) collective-permute-start(bf16[8,8,2,16,128]{4,3,2,1,0:T(8,128)(2,1)S(1)} %get-tuple-element.23), channel_id=1, source_target_pairs={{0,16},{16,0},{32,48},{48,32},{64,80},{80,64},{96,112},{112,96},{1... | collective-permute-start | bytes 1572872 | tf_op jit(solution)/shard_map/ppermute | solution.py:289
  6.9 34.8 %copy-start = (bf16[1,1024,4096]{2,1,0:T(8,128)(2,1)S(1)}, bf16[1,1024,4096]{2,1,0:T(8,128)(2,1)}, u32[]{:S(2)}) copy-start(bf16[1,1024,4096]{2,1,0:T(8,128)(2,1)} %param.13) | copy-start | bytes 25165828
  7.0 17.1 %collective-permute-start.1 = (bf16[5,8,2,16,128]{4,3,2,1,0:T(8,128)(2,1)S(1)}, bf16[5,8,2,16,128]{4,3,2,1,0:T(8,128)(2,1)S(1)}, u32[]{:S(2)}, u32[]{:S(2)}) collective-permute-start(bf16[5,8,2,16,128]{4,3,2,1,0:T(8,128)(2,1)S(1)} %slice_dynamic-update-slice_fusion.7), channel_id=1, source_target_pairs={{0,64},{16,80},{32,96},{48,112},{64,128},{80,144},{96,160},{112,17... | collective-permute-start | bytes 983048 | tf_op jit(solution)/shard_map/ppermute | solution.py:301
  10.4 19.2 %collective-permute-start.3 = (bf16[5,8,2,16,128]{4,3,2,1,0:T(8,128)(2,1)S(1)}, bf16[5,8,2,16,128]{4,3,2,1,0:T(8,128)(2,1)S(1)}, u32[]{:S(2)}, u32[]{:S(2)}) collective-permute-start(bf16[5,8,2,16,128]{4,3,2,1,0:T(8,128)(2,1)S(1)} %get-tuple-element.42), channel_id=1, source_target_pairs={{0,192},{16,208},{32,224},{48,240},{64,0},{80,16},{96,32},{112,48}... | collective-permute-start | bytes 983048 | tf_op jit(solution)/shard_map/ppermute | solution.py:301
  24.2 17.5 %collective-permute-start.2 = (bf16[4,8,2,16,128]{4,3,2,1,0:T(8,128)(2,1)S(1)}, bf16[4,8,2,16,128]{4,3,2,1,0:T(8,128)(2,1)S(1)}, u32[]{:S(2)}, u32[]{:S(2)}) collective-permute-start(bf16[4,8,2,16,128]{4,3,2,1,0:T(8,128)(2,1)S(1)} %pad_maximum_fusion), channel_id=1, source_target_pairs={{0,32},{16,48},{32,64},{48,80},{64,96},{80,112},{96,128},{112,144}... | collective-permute-start | bytes 786440 | tf_op jit(solution)/shard_map/ppermute | solution.py:301
  29.6 12.1 %collective-permute-start.4 = (bf16[4,8,2,16,128]{4,3,2,1,0:T(8,128)(2,1)S(1)}, bf16[4,8,2,16,128]{4,3,2,1,0:T(8,128)(2,1)S(1)}, u32[]{:S(2)}, u32[]{:S(2)}) collective-permute-start(bf16[4,8,2,16,128]{4,3,2,1,0:T(8,128)(2,1)S(1)} %pad_maximum_fusion.1), channel_id=1, source_target_pairs={{0,224},{16,240},{32,0},{48,16},{64,32},{80,48},{96,64},{112,80},{... | collective-permute-start | bytes 786440 | tf_op jit(solution)/shard_map/ppermute | solution.py:301
  30.6 9.9 %collective-permute-start.5 = (bf16[1,8,2,16,128]{4,3,2,1,0:T(8,128)(2,1)S(1)}, bf16[1,8,2,16,128]{4,3,2,1,0:T(8,128)(2,1)S(1)}, u32[]{:S(2)}, u32[]{:S(2)}) collective-permute-start(bf16[1,8,2,16,128]{4,3,2,1,0:T(8,128)(2,1)S(1)} %slice.81), channel_id=1, source_target_pairs={{0,64},{16,80},{32,96},{48,112},{64,128},{80,144},{96,160},{112,17... | collective-permute-start | bytes 196616 | tf_op jit(solution)/shard_map/ppermute | solution.py:301
  33.6 8.1 %collective-permute-start.6 = (bf16[1,8,2,16,128]{4,3,2,1,0:T(8,128)(2,1)S(1)}, bf16[1,8,2,16,128]{4,3,2,1,0:T(8,128)(2,1)S(1)}, u32[]{:S(2)}, u32[]{:S(2)}) collective-permute-start(bf16[1,8,2,16,128]{4,3,2,1,0:T(8,128)(2,1)S(1)} %slice.82), channel_id=1, source_target_pairs={{0,192},{16,208},{32,224},{48,240},{64,0},{80,16},{96,32},{112,48}... | collective-permute-start | bytes 196616 | tf_op jit(solution)/shard_map/ppermute | solution.py:301
  46.6 5.2 %copy-start.7 = (bf16[8,2,4096]{2,1,0:T(2,128)(2,1)S(1)}, bf16[8,2,4096]{2,1,0:T(2,128)(2,1)}, u32[]{:S(2)}) copy-start(bf16[8,2,4096]{2,1,0:T(2,128)(2,1)} %param.9) | copy-start | bytes 393220
  46.6 19.7 %all-to-all-start = ((bf16[8,16,4096]{2,1,0:T(8,128)(2,1)}), bf16[8,16,4096]{2,1,0:T(8,128)(2,1)S(1)}, u32[]{:S(2)}, u32[]{:S(2)}) async-start(bf16[8,16,4096]{2,1,0:T(8,128)(2,1)} %bitcast.6), calls=%async_computation | async-start | bytes 2097152 | tf_op jit(solution)/shard_map/all_to_all | solution.py:385
  66.5 8.5 %collective-permute-start.7 = (bf16[16,4096]{1,0:T(8,128)(2,1)S(1)}, bf16[16,4096]{1,0:T(8,128)(2,1)S(1)}, u32[]{:S(2)}, u32[]{:S(2)}) collective-permute-start(bf16[16,4096]{1,0:T(8,128)(2,1)S(1)} %add_convert_fusion.1), channel_id=1, source_target_pairs={{0,1},{2,3},{4,5},{6,7},{8,9},{10,11},{12,13},{14,15},{16,17},{18,... | collective-permute-start | bytes 393224 | tf_op jit(solution)/shard_map/ppermute | solution.py:391

commit v3 on v2

--- a/solution.py
+++ b/solution.py
@@ -26,17 +26,11 @@
     return lax.dot_general(a, b, (((1,), (1,)), ((), ())), preferred_element_type=F32)
 
 
-def fresh_part(query, keys, values, bias, scale):
-    score = dot_last(query, keys) * scale + bias
-    top = jnp.max(score, axis=1, keepdims=True)
-    weight = jnp.exp(score - top)
-    total = jnp.sum(weight, axis=1, keepdims=True)
-    return top, total, jnp.dot(weight.astype(BF16), values, preferred_element_type=F32)
-
-
 def group_bias():
     row, col = iota((64, 256), 0), iota((64, 256), 1)
-    return jnp.where(row // 2 % 4 == col // 64, 0.0, MASKED)
+    cached = jnp.where(row // 2 % 4 == col // 64, 0.0, MASKED)
+    row, col = iota((64, 8), 0), iota((64, 8), 1)
+    return cached, jnp.where((row // 2 % 4 == col // 2) & (col % 2 <= row % 2), 0.0, MASKED)
 
 
 def limit_bias(limits):
@@ -48,20 +42,30 @@
     return jnp.where(token < limit, 0.0, MASKED)[:1]
 
 
-def cached_part(query, keys, values, bias, fresh, scale):
-    fresh_top, fresh_total, fresh_sum = fresh
-    score = dot_last(query, keys) * scale + bias
-    top = jnp.maximum(jnp.max(score, axis=1, keepdims=True), fresh_top)
-    weight = jnp.exp(score - top)
-    rescale = jnp.exp(fresh_top - top)
-    total = jnp.sum(weight, axis=1, keepdims=True) + fresh_total * rescale
-    summed = jnp.dot(weight.astype(BF16), values, preferred_element_type=F32)
-    return (summed + fresh_sum * rescale) / total
-
-
-def stacked(ref, start):
-    part = ref[:, pl.ds(start, 8), :]
-    return part.reshape(part.shape[0] * 8, part.shape[2])
+def with_ones(values):
+    return jnp.concatenate([values, jnp.ones_like(values)], axis=1)
+
+
+def attend(query, fresh, keys, values, biases, limits, scale):
+    head_dim = keys.shape[1]
+    heads = query.shape[1] // head_dim
+    lanes = [slice(h * head_dim, (h + 1) * head_dim) for h in range(heads)]
+    query = jnp.concatenate([query[:, span] for span in lanes], axis=0).astype(BF16)
+    fresh = fresh.astype(BF16)
+    cached_score = dot_last(query, keys) + (biases[0] + limit_bias(limits))
+    fresh_score = dot_last(query, fresh[:, :head_dim]) + biases[1]
+    top = jnp.maximum(
+        jnp.max(cached_score, axis=1, keepdims=True), jnp.max(fresh_score, axis=1, keepdims=True)
+    )
+    factor = scale * math.log2(math.e)
+    cached_weight = jnp.exp2((cached_score - top) * factor).astype(BF16)
+    fresh_weight = jnp.exp2((fresh_score - top) * factor).astype(BF16)
+    summed = jnp.dot(cached_weight, with_ones(values), preferred_element_type=F32)
+    summed += jnp.dot(
+        fresh_weight, with_ones(fresh[:, head_dim:]), preferred_element_type=F32
+    )
+    out = summed[:, :head_dim] / summed[:, head_dim:]
+    return jnp.concatenate([out[h * 8 : h * 8 + 8] for h in range(heads)], axis=1)
 
 
 def gather_kernel(pages, pool, same_core, other_core):
@@ -83,9 +87,9 @@
     ((-1, True), (-1, False)),
     ((3, True), (3, False)),
     ((-3, True), (-3, False)),
-    ((4, True), (-4, False)),
+    ((4, True), (4, False)),
 )
-EARLY = 3
+EARLY = 5
 
 
 def arrival_slots(moves):
@@ -111,64 +115,36 @@
 
 
 def local_kernel(
-    scale, table, lengths, moves, query, fresh, pool,
-    attended, early_place, late_place,
-    arrival_query, arrival_top, arrival_total, arrival_sum, pool_copy,
-    heads_query, heads_top, heads_total, heads_sum, found, sem,
+    scale, table, lengths, moves, query_in, fresh, pool,
+    attended, early_place, late_place, arrival_query, arrival_fresh, pool_copy,
+    query, found, sem,
 ):
     copy = pltpu.make_async_copy(pool, pool_copy, sem)
     copy.start()
-    head_dim = pool.shape[-1]
-    rows = query.shape[0]
-    heads = query.shape[1] // head_dim
-    fresh_keys = fresh[:, :head_dim].astype(BF16)
-    fresh_values = fresh[:, head_dim:].astype(BF16)
+    rows, width = query.shape
+    query[...] = query_in[...].astype(F32).reshape(rows, width)
     arrivals = arrival_slots(moves)
-
-    shape = (arrival_query.shape[1], rows)
+    shape = (arrival_query.shape[0], rows)
     row, col = iota(shape, 0), iota(shape, 1)
-    wanted = spread(row // 2, arrivals)
+    wanted = jnp.maximum(spread(row // 2, arrivals), 0)
     pick = jnp.where(wanted * 2 + row % 2 == col, 1.0, 0.0).astype(BF16)
-    seen = (jnp.maximum(wanted, 0) == col // 2) & (col % 2 <= row % 2)
-    arrival_bias = jnp.where(seen, 0.0, MASKED)
-    row, col = iota((rows, rows), 0), iota((rows, rows), 1)
-    local_bias = jnp.where((row // 2 == col // 2) & (col % 2 <= row % 2), 0.0, MASKED)
-    for h in range(heads):
-        part = query[:, h * head_dim : (h + 1) * head_dim]
-        chosen = jnp.dot(pick, part.astype(BF16), preferred_element_type=F32)
-        for rows_in, bias, into in (
-            (part, local_bias, (heads_query, heads_top, heads_total, heads_sum)),
-            (chosen, arrival_bias, (arrival_query, arrival_top, arrival_total, arrival_sum)),
-        ):
-            top, total, summed = fresh_part(
-                rows_in.astype(BF16), fresh_keys, fresh_values, bias, scale
-            )
-            into[0][h] = rows_in
-            into[1][h] = jnp.broadcast_to(top, summed.shape)
-            into[2][h] = jnp.broadcast_to(total, summed.shape)
-            into[3][h] = summed
-
-    base = group_bias()
+    for source, chosen in ((query, arrival_query), (fresh, arrival_fresh)):
+        chosen[...] = jnp.dot(pick, source[...].astype(BF16), preferred_element_type=F32)
+    biases = group_bias()
 
     def one_group(group, carry):
-        start = pl.multiple_of(group * 8, 8)
-        part = (
-            stacked(heads_top, start)[:, :1],
-            stacked(heads_total, start)[:, :1],
-            stacked(heads_sum, start),
-        )
+        span = pl.ds(pl.multiple_of(group * 8, 8), 8)
         pages = [table[i % 4, group * 4 + i // 4] for i in range(16)]
         keys = jnp.concatenate([pool[page, 0] for page in pages], axis=0)
         values = jnp.concatenate([pool[page, 1] for page in pages], axis=0)
-        bias = base + limit_bias([lengths[group * 4 + i] for i in range(4)])
-        rows_in = stacked(heads_query, start).astype(BF16)
-        out = cached_part(rows_in, keys, values, bias, part, scale)
-        for h in range(heads):
-            found[pl.ds(start, 8), h * head_dim : (h + 1) * head_dim] = out[h * 8 : h * 8 + 8]
+        limits = [lengths[group * 4 + i] for i in range(4)]
+        found[span, :] = attend(
+            query[span, :], fresh[span, :], keys, values, biases, limits, scale
+        )
         return carry
 
     lax.fori_loop(0, rows // 8, one_group, 0, unroll=4)
-    shape = (rows, arrival_query.shape[1])
+    shape = (rows, arrival_query.shape[0])
     row, col = iota(shape, 0), iota(shape, 1)
     placed = jnp.where(spread(col // 2, arrivals) * 2 + col % 2 == row, 1.0, 0.0)
     early = early_place.shape[1]
@@ -179,20 +155,10 @@
     copy.wait()
 
 
-def arrival_kernel(scale, first, places, *refs):
-    lengths, moves = refs[:2]
-    arrays = refs[2:-8]
-    arrival_query, arrival_top, arrival_total, arrival_sum, attended, place, out, found = refs[-8:]
-    arrival_rows(scale, first, places, lengths, moves, arrays, refs[-8:-4], found)
-    moved = jnp.dot(place[...], found[...].astype(BF16), preferred_element_type=F32)
-    out[...] = (attended[...].astype(F32) + moved).astype(BF16)
-
-
-def arrival_rows(scale, first, places, lengths, moves, arrays, parts, found):
-    arrival_query, arrival_top, arrival_total, arrival_sum = parts
-    heads, _, head_dim = arrival_query.shape
+def arrival_rows(scale, first, places, lengths, moves, arrays, query, fresh, found):
+    head_dim = fresh.shape[1] // 2
     arrivals = arrival_slots(moves)[first * 4 :]
-    base = group_bias()
+    biases = group_bias()
     for position, blocks in enumerate(places):
         start = (first + position) * 8
         slots = arrivals[position * 4 : position * 4 + 4]
@@ -200,25 +166,24 @@
         held = [arrays[array][index] for array, index in blocks]
         keys = jnp.concatenate([block[:, 0].reshape(128, head_dim) for block in held], axis=0)
         values = jnp.concatenate([block[:, 1].reshape(128, head_dim) for block in held], axis=0)
-        part = (
-            stacked(arrival_top, start)[:, :1],
-            stacked(arrival_total, start)[:, :1],
-            stacked(arrival_sum, start),
+        span = slice(start, start + 8)
+        found[position * 8 : position * 8 + 8, :] = attend(
+            query[span, :], fresh[span, :], keys, values, biases, limits, scale
         )
-        bias = base + limit_bias(limits)
-        rows_in = stacked(arrival_query, start).astype(BF16)
-        result = cached_part(rows_in, keys, values, bias, part, scale)
-        for h in range(heads):
-            found[position * 8 : position * 8 + 8, h * head_dim : (h + 1) * head_dim] = result[
-                h * 8 : h * 8 + 8
-            ]
+
+
+def arrival_kernel(scale, first, places, *refs):
+    lengths, moves = refs[:2]
+    query, fresh, attended, place, out, found = refs[-6:]
+    arrival_rows(scale, first, places, lengths, moves, refs[2:-6], query, fresh, found)
+    moved = jnp.dot(place[...], found[...].astype(BF16), preferred_element_type=F32)
+    out[...] = (attended[...].astype(F32) + moved).astype(BF16)
 
 
 def project_kernel(scale, first, places, *refs):
     lengths, moves = refs[:2]
-    arrays = refs[2:-9]
-    attended, place, weight, out, found = refs[-5:]
-    arrival_rows(scale, first, places, lengths, moves, arrays, refs[-9:-5], found)
+    query, fresh, attended, place, weight, out, found = refs[-7:]
+    arrival_rows(scale, first, places, lengths, moves, refs[2:-7], query, fresh, found)
     moved = jnp.dot(place[...], found[...].astype(BF16), preferred_element_type=F32)
     rows = (attended[...].astype(F32) + moved).astype(BF16)
     step = 512
@@ -275,8 +240,6 @@
 
     ring = sources // 2
     block_shape = (ring, moved // sources, 2, page_len, head_dim)
-    query = queries.reshape(rows, width).astype(F32)
-    wanted, query = lax.optimization_barrier((move_pages[0].transpose(1, 2, 0), query))
     same_core, other_core = pl.pallas_call(
         gather_kernel,
         out_shape=[jax.ShapeDtypeStruct(block_shape, BF16)] * 2,
@@ -285,7 +248,7 @@
         compiler_params=pltpu.CompilerParams(vmem_limit_bytes=MIB),
         cost_estimate=pl.CostEstimate(flops=0, bytes_accessed=2**21, transcendentals=0),
         name="gather_pages",
-    )(wanted, pool)
+    )(move_pages[0].transpose(1, 2, 0), pool)
     crossed = lax.ppermute(other_core, "inst", [(index, index ^ 1) for index in range(sources)])
 
     def pair(distance):
@@ -300,51 +263,45 @@
         ]
         return lax.ppermute(jnp.concatenate(blocks, axis=0), "inst", pairs)
 
-    up2 = along_ring(pair(2) + pair(3) + pair(4)[:1], 2)
-    down2 = along_ring(pair(-2) + pair(-3) + pair(4)[1:], -2)
-    early_arrays = [crossed, up2, down2]
+    up2 = along_ring(pair(2) + pair(3), 2)
+    down2 = along_ring(pair(-2) + pair(-3), -2)
     early_places = [[(0, 0), (0, 0)]] + [[(i, 0), (i, 1)] for i in range(1, EARLY)]
-    late_places = [[(i, j), (i, j + 1)] for j in (0, 2) for i in (0, 1)] + [[(2, 0), (3, 0)]]
+    late_places = [[(0, 0), (0, 1)], [(1, 0), (1, 1)], [(2, 0), (2, 1)]]
 
     groups = len(GROUPS)
+    queries, crossed = lax.optimization_barrier((queries, crossed))
     fresh = new_kv.reshape(rows, 2 * head_dim).astype(F32)
-    heads = width // head_dim
-    part_shape = jax.ShapeDtypeStruct((heads, groups * 8, head_dim), F32)
-    heads_scratch = pltpu.VMEM((heads, rows, head_dim), F32)
-    attended, early_place, late_place, arrival_query, top, total, summed, pool_copy = pl.pallas_call(
+    attended, early_place, late_place, arrival_query, arrival_fresh, pool_copy = pl.pallas_call(
         functools.partial(local_kernel, scale),
         out_shape=[
             jax.ShapeDtypeStruct((rows, width), BF16),
             jax.ShapeDtypeStruct((rows, EARLY * 8), BF16),
             jax.ShapeDtypeStruct((rows, (groups - EARLY) * 8), BF16),
-            part_shape,
-            part_shape,
-            part_shape,
-            part_shape,
+            jax.ShapeDtypeStruct((groups * 8, width), F32),
+            jax.ShapeDtypeStruct((groups * 8, 2 * head_dim), F32),
             jax.ShapeDtypeStruct(pool.shape, BF16),
         ],
         in_specs=[SMEM, SMEM, SMEM, VMEM, VMEM, VMEM],
-        out_specs=[VMEM] * 7 + [HBM],
-        scratch_shapes=[heads_scratch] * 4
-        + [pltpu.VMEM((rows, width), F32), pltpu.SemaphoreType.DMA(())],
+        out_specs=[VMEM] * 5 + [HBM],
+        scratch_shapes=[pltpu.VMEM((rows, width), F32)] * 2 + [pltpu.SemaphoreType.DMA(())],
         compiler_params=pltpu.CompilerParams(vmem_limit_bytes=8 * MIB),
         cost_estimate=pl.CostEstimate(flops=2**28, bytes_accessed=2**24, transcendentals=2**18),
         name="local_attention",
-    )(table, lengths, moves, query, fresh, pool)
-
-    near1, near7, attended = lax.optimization_barrier((pair(1), pair(-1), attended))
+    )(table, lengths, moves, queries[0], fresh, pool)
+
+    near, attended = lax.optimization_barrier((pair(1) + pair(-1) + pair(4), attended))
+    early_arrays = [crossed, up2, down2, along_ring(near[:2], 1), along_ring(near[2:4], -1)]
     late_arrays = [
-        along_ring(near1 + [up2[2:4]], 1),
-        along_ring(near7 + [down2[2:4]], -1),
-        along_ring([up2[4:]], 2),
-        along_ring([down2[4:]], -2),
+        along_ring([up2[2:]], 1),
+        along_ring([down2[2:]], -1),
+        along_ring(near[4:], 4),
     ]
 
     def arrival(kernel, name, first, arrays, places, others, out_shape, limit):
         return pl.pallas_call(
             functools.partial(kernel, scale, first, places),
             out_shape=out_shape,
-            in_specs=[SMEM, SMEM] + [VMEM] * (len(arrays) + 4 + len(others)),
+            in_specs=[SMEM, SMEM] + [VMEM] * (len(arrays) + 2 + len(others)),
             out_specs=VMEM,
             scratch_shapes=[pltpu.VMEM((len(places) * 8, width), F32)],
             compiler_params=pltpu.CompilerParams(vmem_limit_bytes=limit),
@@ -352,7 +309,7 @@
                 flops=2**26, bytes_accessed=2**21, transcendentals=2**16
             ),
             name=name,
-        )(lengths, moves, *arrays, arrival_query, top, total, summed, *others)
+        )(lengths, moves, *arrays, arrival_query, arrival_fresh, *others)
 
     def place_pages(first, arrays, places, held):
         return pl.pallas_call(

time: 76 us -> 71.4 us (0.939)
  Pallas kernels: 21.2 us -> 15.7 us
  starting transfers between devices: 23.5 us -> 24.7 us
    pallas_call x1, Pallas kernels: 9.57 us -> 5.05 us  [shards(): pl.pallas_call(functools.partial(local_kernel, scale), out_shape=[jax.Sha...]
    all_to_all x1, waiting for transfers between devices: 10.8 us -> 12 us  [shards(): lax.all_to_all(contribution.reshape(n_tp, own, model), 'tp', split_axis=0...]
    ppermute x6 -> x7, starting transfers between devices: 17 us -> 18.2 us  [along_ring(): return lax.ppermute(jnp.concatenate(blocks, axis=0), 'inst', pairs)]
    convert_element_type x1 -> x0, local copies, waits for them, and re-layouts: 1.06 us -> none  [shards(): query = queries.reshape(rows, width).astype(F32)]
    pallas_call x2, Pallas kernels: 7.13 us -> 6.16 us  [arrival(): pl.pallas_call(functools.partial(kernel, scale, first, places), out_shape...]
    ppermute x1, waiting for transfers between devices: 1.88 us -> 0.99 us  [shards(): lax.ppermute(other_core, 'inst', [(index, index ^ 1) for index in range(s...]
    unnamed x24 -> x19, local copies, waits for them, and re-layouts: 2.4 us -> 3.15 us
    ppermute x6 -> x7, waiting for transfers between devices: 5.75 us -> 5.25 us  [along_ring(): return lax.ppermute(jnp.concatenate(blocks, axis=0), 'inst', pairs)]
  transfers between devices with their start and end apart: 9 -> 10, of which waited for: 6 -> 7; matrix products, arithmetic and copies ran while one was open for 0% -> 1% of each run, Pallas kernels for 20% -> 15%
where the time goes in v3:
time: 71.4 us; the launch traced here: 71.1 us
  waiting for transfers between devices  25.5 us (36%)
  starting transfers between devices  24.7 us (35%)
  Pallas kernels  15.7 us (22%)
  local copies, waits for them, and re-layouts  4.03 us (6%)
  between operations  0.85 us (1%)
    ppermute x7, starting transfers between devices, along_ring(): return lax.ppermute(jnp.concatenate(blocks, axis=0), 'inst', pairs)  18.2 us
    all_to_all x1, waiting for transfers between devices, shards(): lax.all_to_all(contribution.reshape(n_tp, own, model), 'tp', split_axis=0...  12 us
    ppermute x1, waiting for transfers between devices, shards(): passed = lax.ppermute(first_out, 'pp', [(0, 1)])  7.18 us
    pallas_call x2, Pallas kernels, arrival(): pl.pallas_call(functools.partial(kernel, scale, first, places), out_shape...  6.16 us
    ppermute x7, waiting for transfers between devices, along_ring(): return lax.ppermute(jnp.concatenate(blocks, axis=0), 'inst', pairs)  5.25 us
    all_to_all x1, starting transfers between devices, shards(): lax.all_to_all(contribution.reshape(n_tp, own, model), 'tp', split_axis=0...  5.15 us
    pallas_call x1, Pallas kernels, shards(): pl.pallas_call(functools.partial(local_kernel, scale), out_shape=[jax.Sha...  5.05 us
    pallas_call x2, Pallas kernels, place_pages(): pl.pallas_call(functools.partial(place_kernel, first, places), out_shape=...  3.71 us
  transfers between devices with their start and end apart: 10, of which 7 were waited for; matrix products, arithmetic and copies ran while one was open for 1% of the time, Pallas kernels for 15%

profile of v3, /device:TPU:16, one launch (start us, length us, event | category | flops | bytes accessed | tf_op | source)
XLA Modules:
  0.0 71.1 jit_solution(16414890144185883658)
XLA Ops:
  0.6 0.0 copy-start.1
  0.6 1.6 %copy-done.1 = bf16[1,256,2,1,16,128]{5,4,3,2,1,0:T(8,128)(2,1)S(1)} copy-done((bf16[1,256,2,1,16,128]{5,4,3,2,1,0:T(8,128)(2,1)S(1)}, bf16[1,256,2,1,16,128]{5,4,3,2,1,0:T(8,128)(2,1)}, u32[]{:S(2)}) %copy-start.1) | copy-done | bytes 2097176
  2.2 0.0 copy-start.7
  2.2 0.7 copy-done.7
  2.9 0.0 copy-start.2
  2.9 0.0 copy-start.3
  2.9 0.0 copy-start.4
  2.9 0.0 copy-start.5
  2.9 0.0 copy-start.6
  2.9 0.8 %gather_pages.1 = (bf16[8,8,2,16,128]{4,3,2,1,0:T(8,128)(2,1)S(1)}, bf16[8,8,2,16,128]{4,3,2,1,0:T(8,128)(2,1)S(1)}) custom-call(s32[2,4,16]{2,1,0:T(4,128)S(1)} %bitcast.31, bf16[256,2,16,128]{3,2,1,0:T(8,128)(2,1)S(1)} %bitcast.19), custom_call_target="tpu_custom_call" | custom-call | bytes 2097152 | tf_op jit(solution)/shard_map/gather_pages/pallas_call | solution.py:243
  3.8 0.1 collective-permute-start
  3.9 0.9 %copy.16 = f32[16,8,2,128]{3,1,2,0:T(8,128)S(1)} copy(bf16[16,8,2,128]{3,2,1,0:T(2,128)(2,1)} %bitcast.33) | data formatting | bytes 196608
  4.7 0.0 copy-start
  4.8 1.0 %collective-permute-done.refs_2_ = bf16[8,8,2,16,128]{4,3,2,1,0:T(8,128)(2,1)S(1)} collective-permute-done((bf16[8,8,2,16,128]{4,3,2,1,0:T(8,128)(2,1)S(1)}, bf16[8,8,2,16,128]{4,3,2,1,0:T(8,128)(2,1)S(1)}, u32[]{:S(2)}, u32[]{:S(2)}) %collective-permute-start) | collective-permute-done | bytes 524320 | tf_op jit(solution)/shard_map/ppermute | solution.py:252
  5.8 3.3 %collective-permute-start.1 = (bf16[4,8,2,16,128]{4,3,2,1,0:T(8,128)(2,1)S(1)}, bf16[4,8,2,16,128]{4,3,2,1,0:T(8,128)(2,1)S(1)}, u32[]{:S(2)}, u32[]{:S(2)}) collective-permute-start(bf16[4,8,2,16,128]{4,3,2,1,0:T(8,128)(2,1)S(1)} %pad_maximum_fusion), channel_id=1, source_target_pairs={{0,64},{16,80},{32,96},{48,112},{64,128},{80,144},{96,160},{112,17... | collective-permute-start | bytes 786440 | tf_op jit(solution)/shard_map/ppermute | solution.py:264
  9.2 3.1 %collective-permute-start.3 = (bf16[4,8,2,16,128]{4,3,2,1,0:T(8,128)(2,1)S(1)}, bf16[4,8,2,16,128]{4,3,2,1,0:T(8,128)(2,1)S(1)}, u32[]{:S(2)}, u32[]{:S(2)}) collective-permute-start(bf16[4,8,2,16,128]{4,3,2,1,0:T(8,128)(2,1)S(1)} %pad_maximum_fusion.1), channel_id=1, source_target_pairs={{0,192},{16,208},{32,224},{48,240},{64,0},{80,16},{96,32},{112,48}... | collective-permute-start | bytes 786440 | tf_op jit(solution)/shard_map/ppermute | solution.py:264
  12.4 0.0 copy-done.2
  12.4 0.0 copy-done.3
  12.4 0.0 copy-done.4
  12.4 0.0 copy-done.5
  12.4 0.0 copy-done.6
  12.4 5.0 %local_attention.1 = (bf16[128,1024]{1,0:T(8,128)(2,1)S(1)}, bf16[128,40]{1,0:T(8,128)(2,1)S(1)}, bf16[128,24]{1,0:T(8,128)(2,1)S(1)}, f32[64,1024]{1,0:T(8,128)...) custom-call(s32[4,64]{1,0:T(4,128)S(1)} %bitcast.28, s32[64]{0:T(128)S(1)} %copy-done.6, ...), custom_call_target="tpu_custom_call" | custom-call | flops 268435456 | bytes 16777216 | tf_op jit(solution)/shard_map/local_attention/pallas_call | solution.py:274
  17.5 1.1 %collective-permute-start.6 = (bf16[2,8,2,16,128]{4,3,2,1,0:T(8,128)(2,1)S(1)}, bf16[2,8,2,16,128]{4,3,2,1,0:T(8,128)(2,1)S(1)}, u32[]{:S(2)}, u32[]{:S(2)}) collective-permute-start(bf16[2,8,2,16,128]{4,3,2,1,0:T(8,128)(2,1)S(1)} %pad_maximum_fusion.3), channel_id=1, source_target_pairs={{0,32},{16,48},{32,64},{48,80},{64,96},{80,112},{96,128},{112,144}... | collective-permute-start | bytes 393224 | tf_op jit(solution)/shard_map/ppermute | solution.py:264
  18.6 2.3 %collective-permute-start.7 = (bf16[2,8,2,16,128]{4,3,2,1,0:T(8,128)(2,1)S(1)}, bf16[2,8,2,16,128]{4,3,2,1,0:T(8,128)(2,1)S(1)}, u32[]{:S(2)}, u32[]{:S(2)}) collective-permute-start(bf16[2,8,2,16,128]{4,3,2,1,0:T(8,128)(2,1)S(1)} %pad_maximum_fusion.4), channel_id=1, source_target_pairs={{0,224},{16,240},{32,0},{48,16},{64,32},{80,48},{96,64},{112,80},{... | collective-permute-start | bytes 393224 | tf_op jit(solution)/shard_map/ppermute | solution.py:264
  20.9 5.1 %collective-permute-start.5 = (bf16[2,8,2,16,128]{4,3,2,1,0:T(8,128)(2,1)S(1)}, bf16[2,8,2,16,128]{4,3,2,1,0:T(8,128)(2,1)S(1)}, u32[]{:S(2)}, u32[]{:S(2)}) collective-permute-start(bf16[2,8,2,16,128]{4,3,2,1,0:T(8,128)(2,1)S(1)} %pad_maximum_fusion.2), channel_id=1, source_target_pairs={{0,128},{16,144},{32,160},{48,176},{64,192},{80,208},{96,224},{112... | collective-permute-start | bytes 393224 | tf_op jit(solution)/shard_map/ppermute | solution.py:264
  26.0 0.0 collective-permute-done.1.refs_3_
  26.0 0.1 collective-permute-start.2
  26.1 0.2 collective-permute-done.3.refs_4_
  26.3 3.1 %collective-permute-start.4 = (bf16[2,8,2,16,128]{4,3,2,1,0:T(8,128)(2,1)S(1)}, bf16[2,8,2,16,128]{4,3,2,1,0:T(8,128)(2,1)S(1)}, u32[]{:S(2)}, u32[]{:S(2)}) collective-permute-start(bf16[2,8,2,16,128]{4,3,2,1,0:T(8,128)(2,1)S(1)} %slice.69), channel_id=1, source_target_pairs={{0,224},{16,240},{32,0},{48,16},{64,32},{80,48},{96,64},{112,80},{... | collective-permute-start | bytes 393224 | tf_op jit(solution)/shard_map/ppermute | solution.py:264
  29.4 0.0 collective-permute-done.6.refs_5_
  29.4 0.0 collective-permute-done.7.refs_6_
  29.4 2.1 %arrival_attention.1.refs_7_ = bf16[128,1024]{1,0:T(8,128)(2,1)S(1)} custom-call(s32[64]{0:T(128)S(1)} %copy-done.6, s32[16,2,16]{2,1,0:T(2,128)S(1)} %bitcast.23, bf16[8,8,2,16,128]{4,3,2,1,0:T(8,128)(2,1)S(1)} %collective-permute-done.refs_2_, bf16[4,8,2,16,128]{4,3,2,1,0:T(8,128)(2,1)S(1)} %collective-permute-done.1.refs_3_, ...), custom_call_target="tpu_custom_call" | custom-call | flops 67108864 | bytes 2097152 | tf_op jit(solution)/shard_map/arrival_attention/pallas_call | solution.py:301
  31.5 1.3 %collective-permute-done.5.refs_4_ = bf16[2,8,2,16,128]{4,3,2,1,0:T(8,128)(2,1)S(1)} collective-permute-done((bf16[2,8,2,16,128]{4,3,2,1,0:T(8,128)(2,1)S(1)}, bf16[2,8,2,16,128]{4,3,2,1,0:T(8,128)(2,1)S(1)}, u32[]{:S(2)}, u32[]{:S(2)}) %collective-permute-start.5) | collective-permute-done | bytes 131104 | tf_op jit(solution)/shard_map/ppermute | solution.py:264
  32.8 3.7 %collective-permute-done.2.refs_2_ = bf16[2,8,2,16,128]{4,3,2,1,0:T(8,128)(2,1)S(1)} collective-permute-done((bf16[2,8,2,16,128]{4,3,2,1,0:T(8,128)(2,1)S(1)}, bf16[2,8,2,16,128]{4,3,2,1,0:T(8,128)(2,1)S(1)}, u32[]{:S(2)}, u32[]{:S(2)}) %collective-permute-start.2) | collective-permute-done | bytes 131104 | tf_op jit(solution)/shard_map/ppermute | solution.py:264
  36.5 0.1 collective-permute-done.4.refs_3_
  36.6 0.0 copy-done
  36.6 4.1 %project.1 = bf16[128,4096]{1,0:T(8,128)(2,1)} custom-call(s32[64]{0:T(128)S(1)} %copy-done.6, s32[16,2,16]{2,1,0:T(2,128)S(1)} %bitcast.24, bf16[2,8,2,16,128]{4,3,2,1,0:T(8,128)(2,1)S(1)} %collective-permute-done.2.refs_2_, bf16[2,8,2,16,128]{4,3,2,1,0:T(8,128)(2,1)S(1)} %collective-permute-done.4.refs_3_, ...), custom_call_target="tpu_custom_call" | custom-call | flops 67108864 | bytes 2097152 | tf_op jit(solution)/shard_map/project/pallas_call | solution.py:301
  40.7 0.0 copy-start.8
  40.7 5.2 %all-to-all-start = ((bf16[8,16,4096]{2,1,0:T(8,128)(2,1)}), bf16[8,16,4096]{2,1,0:T(8,128)(2,1)S(1)}, u32[]{:S(2)}, u32[]{:S(2)}) async-start(bf16[8,16,4096]{2,1,0:T(8,128)(2,1)} %bitcast.7), calls=%async_computation | async-start | bytes 2097152 | tf_op jit(solution)/shard_map/all_to_all | solution.py:342
  45.8 0.0 copy-done.8
  45.9 1.9 %place_pages.2.refs_5_ = bf16[256,2,16,128]{3,2,1,0:T(8,128)(2,1)} custom-call(s32[4,64]{1,0:T(4,128)S(1)} %bitcast.29, s32[16,2,16]{2,1,0:T(2,128)S(1)} %bitcast.25, bf16[8,8,2,16,128]{4,3,2,1,0:T(8,128)(2,1)S(1)} %collective-permute-done.refs_2_, bf16[4,8,2,16,128]{4,3,2,1,0:T(8,128)(2,1)S(1)} %collective-permute-done.1.refs_3_, ...), custom_call_target="tpu_custom_call", output_to_operand_aliasing={{}: (7, {})} | custom-call | bytes 2097152 | tf_op jit(solution)/shard_map/place_pages/pallas_call | solution.py:315
  47.8 1.8 %place_pages.3 = bf16[256,2,16,128]{3,2,1,0:T(8,128)(2,1)} custom-call(s32[4,64]{1,0:T(4,128)S(1)} %bitcast.30, s32[16,2,16]{2,1,0:T(2,128)S(1)} %bitcast.26, bf16[2,8,2,16,128]{4,3,2,1,0:T(8,128)(2,1)S(1)} %collective-permute-done.2.refs_2_, bf16[2,8,2,16,128]{4,3,2,1,0:T(8,128)(2,1)S(1)} %collective-permute-done.4.refs_3_, ...), custom_call_target="tpu_custom_call", output_to_operand_aliasing={{}: (5, {})} | custom-call | bytes 2097152 | tf_op jit(solution)/shard_map/place_pages/pallas_call | solution.py:315
  49.6 12.0 %all-to-all-done = bf16[8,16,4096]{2,1,0:T(8,128)(2,1)S(1)} async-done(((bf16[8,16,4096]{2,1,0:T(8,128)(2,1)}), bf16[8,16,4096]{2,1,0:T(8,128)(2,1)S(1)}, u32[]{:S(2)}, u32[]{:S(2)}) %all-to-all-start) | async-done | bytes 1048608 | tf_op jit(solution)/shard_map/all_to_all | solution.py:342
  61.7 0.1 convert_reduce_fusion
  61.8 1.3 %collective-permute-start.8 = (bf16[16,4096]{1,0:T(8,128)(2,1)S(1)}, bf16[16,4096]{1,0:T(8,128)(2,1)S(1)}, u32[]{:S(2)}, u32[]{:S(2)}) collective-permute-start(bf16[16,4096]{1,0:T(8,128)(2,1)S(1)} %add_convert_fusion.1), channel_id=1, source_target_pairs={{0,1},{2,3},{4,5},{6,7},{8,9},{10,11},{12,13},{14,15},{16,17},{18,... | collective-permute-start | bytes 393224 | tf_op jit(solution)/shard_map/ppermute | solution.py:348
  63.1 7.2 %collective-permute-done.8 = bf16[16,4096]{1,0:T(8,128)(2,1)S(1)} collective-permute-done((bf16[16,4096]{1,0:T(8,128)(2,1)S(1)}, bf16[16,4096]{1,0:T(8,128)(2,1)S(1)}, u32[]{:S(2)}, u32[]{:S(2)}) %collective-permute-start.8) | collective-permute-done | bytes 131104 | tf_op jit(solution)/shard_map/ppermute | solution.py:348
  70.4 0.8 %reshape.24 = bf16[1,8,2,4096]{3,2,1,0:T(2,128)(2,1)} reshape(bf16[16,4096]{1,0:T(8,128)(2,1)S(1)} %fusion) | data formatting | bytes 262144 | tf_op jit(solution)/shard_map/reshape | solution.py:351
  (13 shorter events, 0.3 us)
Async XLA Ops:
  0.6 1.6 %copy-start.1 = (bf16[1,256,2,1,16,128]{5,4,3,2,1,0:T(8,128)(2,1)S(1)}, bf16[1,256,2,1,16,128]{5,4,3,2,1,0:T(8,128)(2,1)}, u32[]{:S(2)}) copy-start(bf16[1,256,2,1,16,128]{5,4,3,2,1,0:T(8,128)(2,1)} %param.12) | copy-start | bytes 6291460
  2.2 0.7 copy-start.7
  2.9 9.4 %copy-start.2 = (bf16[1,256,2,1,16,128]{5,4,3,2,1,0:T(8,128)(2,1)S(1)}, bf16[1,256,2,1,16,128]{5,4,3,2,1,0:T(8,128)(2,1)}, u32[]{:S(2)}) copy-start(bf16[1,256,2,1,16,128]{5,4,3,2,1,0:T(8,128)(2,1)} %param.12) | copy-start | bytes 6291460
  2.9 9.5 %copy-start.3 = (s32[16,16,2]{1,2,0:T(2,128)S(1)}, s32[16,16,2]{1,2,0:T(2,128)}, u32[]{:S(2)}) copy-start(s32[16,16,2]{1,2,0:T(2,128)} %param.16) | copy-start | bytes 6148
  2.9 9.5 %copy-start.4 = (bf16[1,64,2,1024]{3,2,1,0:T(2,128)(2,1)S(1)}, bf16[1,64,2,1024]{3,2,1,0:T(2,128)(2,1)}, u32[]{:S(2)}) copy-start(bf16[1,64,2,1024]{3,2,1,0:T(2,128)(2,1)} %param.10) | copy-start | bytes 786436
  2.9 9.5 %copy-start.5 = (s32[64,4]{0,1:T(4,128)S(1)}, s32[64,4]{0,1:T(4,128)}, u32[]{:S(2)}) copy-start(s32[64,4]{0,1:T(4,128)} %param.15) | copy-start | bytes 3076
  2.9 9.5 %copy-start.6 = (s32[64]{0:T(128)S(1)}, s32[64]{0:T(128)}, u32[]{:S(2)}) copy-start(s32[64]{0:T(128)} %refs_0_.3) | copy-start | bytes 772
  3.8 2.0 %collective-permute-start = (bf16[8,8,2,16,128]{4,3,2,1,0:T(8,128)(2,1)S(1)}, bf16[8,8,2,16,128]{4,3,2,1,0:T(8,128)(2,1)S(1)}, u32[]{:S(2)}, u32[]{:S(2)}) collective-permute-start(bf16[8,8,2,16,128]{4,3,2,1,0:T(8,128)(2,1)S(1)} %get-tuple-element.22), channel_id=1, source_target_pairs={{0,16},{16,0},{32,48},{48,32},{64,80},{80,64},{96,112},{112,96},{1... | collective-permute-start | bytes 1572872 | tf_op jit(solution)/shard_map/ppermute | solution.py:252
  4.7 31.9 %copy-start = (bf16[1,1024,4096]{2,1,0:T(8,128)(2,1)S(1)}, bf16[1,1024,4096]{2,1,0:T(8,128)(2,1)}, u32[]{:S(2)}) copy-start(bf16[1,1024,4096]{2,1,0:T(8,128)(2,1)} %param.13) | copy-start | bytes 25165828
  5.8 20.2 %collective-permute-start.1 = (bf16[4,8,2,16,128]{4,3,2,1,0:T(8,128)(2,1)S(1)}, bf16[4,8,2,16,128]{4,3,2,1,0:T(8,128)(2,1)S(1)}, u32[]{:S(2)}, u32[]{:S(2)}) collective-permute-start(bf16[4,8,2,16,128]{4,3,2,1,0:T(8,128)(2,1)S(1)} %pad_maximum_fusion), channel_id=1, source_target_pairs={{0,64},{16,80},{32,96},{48,112},{64,128},{80,144},{96,160},{112,17... | collective-permute-start | bytes 786440 | tf_op jit(solution)/shard_map/ppermute | solution.py:264
  9.2 17.1 %collective-permute-start.3 = (bf16[4,8,2,16,128]{4,3,2,1,0:T(8,128)(2,1)S(1)}, bf16[4,8,2,16,128]{4,3,2,1,0:T(8,128)(2,1)S(1)}, u32[]{:S(2)}, u32[]{:S(2)}) collective-permute-start(bf16[4,8,2,16,128]{4,3,2,1,0:T(8,128)(2,1)S(1)} %pad_maximum_fusion.1), channel_id=1, source_target_pairs={{0,192},{16,208},{32,224},{48,240},{64,0},{80,16},{96,32},{112,48}... | collective-permute-start | bytes 786440 | tf_op jit(solution)/shard_map/ppermute | solution.py:264
  17.5 11.9 %collective-permute-start.6 = (bf16[2,8,2,16,128]{4,3,2,1,0:T(8,128)(2,1)S(1)}, bf16[2,8,2,16,128]{4,3,2,1,0:T(8,128)(2,1)S(1)}, u32[]{:S(2)}, u32[]{:S(2)}) collective-permute-start(bf16[2,8,2,16,128]{4,3,2,1,0:T(8,128)(2,1)S(1)} %pad_maximum_fusion.3), channel_id=1, source_target_pairs={{0,32},{16,48},{32,64},{48,80},{64,96},{80,112},{96,128},{112,144}... | collective-permute-start | bytes 393224 | tf_op jit(solution)/shard_map/ppermute | solution.py:264
  18.6 10.8 %collective-permute-start.7 = (bf16[2,8,2,16,128]{4,3,2,1,0:T(8,128)(2,1)S(1)}, bf16[2,8,2,16,128]{4,3,2,1,0:T(8,128)(2,1)S(1)}, u32[]{:S(2)}, u32[]{:S(2)}) collective-permute-start(bf16[2,8,2,16,128]{4,3,2,1,0:T(8,128)(2,1)S(1)} %pad_maximum_fusion.4), channel_id=1, source_target_pairs={{0,224},{16,240},{32,0},{48,16},{64,32},{80,48},{96,64},{112,80},{... | collective-permute-start | bytes 393224 | tf_op jit(solution)/shard_map/ppermute | solution.py:264
  20.9 11.9 %collective-permute-start.5 = (bf16[2,8,2,16,128]{4,3,2,1,0:T(8,128)(2,1)S(1)}, bf16[2,8,2,16,128]{4,3,2,1,0:T(8,128)(2,1)S(1)}, u32[]{:S(2)}, u32[]{:S(2)}) collective-permute-start(bf16[2,8,2,16,128]{4,3,2,1,0:T(8,128)(2,1)S(1)} %pad_maximum_fusion.2), channel_id=1, source_target_pairs={{0,128},{16,144},{32,160},{48,176},{64,192},{80,208},{96,224},{112... | collective-permute-start | bytes 393224 | tf_op jit(solution)/shard_map/ppermute | solution.py:264
  26.0 10.5 %collective-permute-start.2 = (bf16[2,8,2,16,128]{4,3,2,1,0:T(8,128)(2,1)S(1)}, bf16[2,8,2,16,128]{4,3,2,1,0:T(8,128)(2,1)S(1)}, u32[]{:S(2)}, u32[]{:S(2)}) collective-permute-start(bf16[2,8,2,16,128]{4,3,2,1,0:T(8,128)(2,1)S(1)} %slice.66), channel_id=1, source_target_pairs={{0,32},{16,48},{32,64},{48,80},{64,96},{80,112},{96,128},{112,144}... | collective-permute-start | bytes 393224 | tf_op jit(solution)/shard_map/ppermute | solution.py:264
  26.3 10.3 %collective-permute-start.4 = (bf16[2,8,2,16,128]{4,3,2,1,0:T(8,128)(2,1)S(1)}, bf16[2,8,2,16,128]{4,3,2,1,0:T(8,128)(2,1)S(1)}, u32[]{:S(2)}, u32[]{:S(2)}) collective-permute-start(bf16[2,8,2,16,128]{4,3,2,1,0:T(8,128)(2,1)S(1)} %slice.69), channel_id=1, source_target_pairs={{0,224},{16,240},{32,0},{48,16},{64,32},{80,48},{96,64},{112,80},{... | collective-permute-start | bytes 393224 | tf_op jit(solution)/shard_map/ppermute | solution.py:264
  40.7 5.2 %copy-start.8 = (bf16[8,2,4096]{2,1,0:T(2,128)(2,1)S(1)}, bf16[8,2,4096]{2,1,0:T(2,128)(2,1)}, u32[]{:S(2)}) copy-start(bf16[8,2,4096]{2,1,0:T(2,128)(2,1)} %param.9) | copy-start | bytes 393220
  40.7 21.0 %all-to-all-start = ((bf16[8,16,4096]{2,1,0:T(8,128)(2,1)}), bf16[8,16,4096]{2,1,0:T(8,128)(2,1)S(1)}, u32[]{:S(2)}, u32[]{:S(2)}) async-start(bf16[8,16,4096]{2,1,0:T(8,128)(2,1)} %bitcast.7), calls=%async_computation | async-start | bytes 2097152 | tf_op jit(solution)/shard_map/all_to_all | solution.py:342
  61.8 8.5 %collective-permute-start.8 = (bf16[16,4096]{1,0:T(8,128)(2,1)S(1)}, bf16[16,4096]{1,0:T(8,128)(2,1)S(1)}, u32[]{:S(2)}, u32[]{:S(2)}) collective-permute-start(bf16[16,4096]{1,0:T(8,128)(2,1)S(1)} %add_convert_fusion.1), channel_id=1, source_target_pairs={{0,1},{2,3},{4,5},{6,7},{8,9},{10,11},{12,13},{14,15},{16,17},{18,... | collective-permute-start | bytes 393224 | tf_op jit(solution)/shard_map/ppermute | solution.py:348

commit v4 on v3

--- a/solution.py
+++ b/solution.py
@@ -182,15 +182,30 @@
 
 def project_kernel(scale, first, places, *refs):
     lengths, moves = refs[:2]
-    query, fresh, attended, place, weight, out, found = refs[-7:]
-    arrival_rows(scale, first, places, lengths, moves, refs[2:-7], query, fresh, found)
+    found, blocks = refs[-2:]
+    peers, own, _ = blocks.shape
+    outs = refs[-2 - peers : -2]
+    query, fresh, attended, place, weight = refs[-7 - peers : -2 - peers]
+    arrays = refs[2 : -7 - peers]
+    arrival_rows(scale, first, places, lengths, moves, arrays, query, fresh, found)
     moved = jnp.dot(place[...], found[...].astype(BF16), preferred_element_type=F32)
     rows = (attended[...].astype(F32) + moved).astype(BF16)
+    for peer in range(peers):
+        blocks[peer] = rows[peer * own : (peer + 1) * own]
+    me = lax.axis_index("tp")
+    rows = jnp.concatenate([blocks[me ^ peer] for peer in range(peers)], axis=0)
     step = 512
-    for start in range(0, out.shape[1], step):
+    for start in range(0, weight.shape[1], step):
         span = slice(start, start + step)
-        product = jnp.dot(rows, weight[:, span], preferred_element_type=F32)
-        out[:, span] = product.astype(BF16)
+        product = jnp.dot(rows, weight[:, span], preferred_element_type=F32).astype(BF16)
+        for peer, out in enumerate(outs):
+            out[:, span] = product[peer * own : (peer + 1) * own]
+
+
+def final_kernel(first, passed, branch, out):
+    late = (passed[...].astype(F32) + branch[...]).astype(BF16).astype(F32)
+    value = jnp.where(lax.axis_index("pp") == 0, first[...].astype(F32), late)
+    out[...] = value.reshape(out.shape).astype(BF16)
 
 
 def place_kernel(first, places, *refs):
@@ -297,14 +312,14 @@
         along_ring(near[4:], 4),
     ]
 
-    def arrival(kernel, name, first, arrays, places, others, out_shape, limit):
+    def arrival(kernel, name, first, arrays, places, others, out_shape, extra=()):
         return pl.pallas_call(
             functools.partial(kernel, scale, first, places),
             out_shape=out_shape,
             in_specs=[SMEM, SMEM] + [VMEM] * (len(arrays) + 2 + len(others)),
-            out_specs=VMEM,
-            scratch_shapes=[pltpu.VMEM((len(places) * 8, width), F32)],
-            compiler_params=pltpu.CompilerParams(vmem_limit_bytes=limit),
+            out_specs=jax.tree.map(lambda _: VMEM, out_shape),
+            scratch_shapes=[pltpu.VMEM((len(places) * 8, width), F32), *extra],
+            compiler_params=pltpu.CompilerParams(vmem_limit_bytes=4 * MIB),
             cost_estimate=pl.CostEstimate(
                 flops=2**26, bytes_accessed=2**21, transcendentals=2**16
             ),
@@ -326,28 +341,35 @@
 
     attended = arrival(
         arrival_kernel, "arrival_attention", 0, early_arrays, early_places,
-        (attended, early_place), jax.ShapeDtypeStruct((rows, width), BF16), 4 * MIB,
+        (attended, early_place), jax.ShapeDtypeStruct((rows, width), BF16),
     )
     weight = out_weight[0]
-    contribution = arrival(
+    model, own = weight.shape[1], rows // n_tp
+    parts = arrival(
         project_kernel, "project", EARLY, late_arrays, late_places,
         (attended, late_place, weight),
-        jax.ShapeDtypeStruct((rows, weight.shape[1]), BF16), 4 * MIB,
+        [jax.ShapeDtypeStruct((own, model), BF16)] * n_tp,
+        (pltpu.VMEM((n_tp, own, width), BF16),),
     )
     pool_after = place_pages(0, early_arrays, early_places, pool_copy)
     pool_after = place_pages(EARLY, late_arrays, late_places, pool_after)
 
-    model = contribution.shape[1]
-    own = rows // n_tp
-    received = lax.all_to_all(
-        contribution.reshape(n_tp, own, model), "tp", split_axis=0, concat_axis=0, tiled=True
-    )
-    branch = jnp.sum(received.astype(F32), axis=0)
+    kept, residual = lax.optimization_barrier((parts[0], residual))
+    branch = kept.astype(F32)
+    for peer in (6, 2, 7, 5, 3, 1, 4):
+        pairs = [(index, index ^ peer) for index in range(n_tp)]
+        branch = branch + lax.ppermute(parts[peer], "tp", pairs).astype(F32)
     first_out = (residual.reshape(own, model).astype(F32) + branch).astype(BF16)
     first_out, pool_after = lax.optimization_barrier((first_out, pool_after))
     passed = lax.ppermute(first_out, "pp", [(0, 1)])
-    second_out = (passed.astype(F32) + branch).astype(BF16)
-    hidden_out = jnp.where(lax.axis_index("pp") == 0, first_out, second_out)
+    hidden_out = pl.pallas_call(
+        final_kernel,
+        out_shape=jax.ShapeDtypeStruct(residual.shape, BF16),
+        in_specs=[VMEM] * 3,
+        out_specs=VMEM,
+        compiler_params=pltpu.CompilerParams(vmem_limit_bytes=4 * MIB),
+        name="second_layer",
+    )(first_out, passed, branch)
     return (hidden_out.reshape((1,) + residual.shape), pool_after.reshape(kv_pool.shape))
 
 

time: 71.4 us -> 69.1 us (0.968)
  the two profiles are of different devices: /device:TPU:16 before, /device:TPU:56 now
where the time goes in v4:
time: 69.1 us; the launch traced here: 68.9 us
  starting transfers between devices  29.1 us (42%)
  waiting for transfers between devices  19.7 us (29%)
  Pallas kernels  15.7 us (23%)
  local copies, waits for them, and re-layouts  3.27 us (5%)
  between operations  0.87 us (1%)
    ppermute x7, starting transfers between devices, along_ring(): return lax.ppermute(jnp.concatenate(blocks, axis=0), 'inst', pairs)  15.3 us
    ppermute x7, starting transfers between devices, shards(): branch = branch + lax.ppermute(parts[peer], 'tp', pairs).astype(F32)  12.4 us
    ppermute x7, waiting for transfers between devices, along_ring(): return lax.ppermute(jnp.concatenate(blocks, axis=0), 'inst', pairs)  8.12 us
    ppermute x1, waiting for transfers between devices, shards(): passed = lax.ppermute(first_out, 'pp', [(0, 1)])  7.07 us
    pallas_call x2, Pallas kernels, arrival(): pl.pallas_call(functools.partial(kernel, scale, first, places), out_shape...  5.28 us
    pallas_call x1, Pallas kernels, shards(): pl.pallas_call(functools.partial(local_kernel, scale), out_shape=[jax.Sha...  5.05 us
    pallas_call x2, Pallas kernels, place_pages(): pl.pallas_call(functools.partial(place_kernel, first, places), out_shape=...  3.71 us
    ppermute x7, waiting for transfers between devices, shards(): branch = branch + lax.ppermute(parts[peer], 'tp', pairs).astype(F32)  3.57 us
  transfers between devices with their start and end apart: 16, of which 7 were waited for; matrix products, arithmetic and copies ran while one was open for 2% of the time, Pallas kernels for 16%

profile of v4, /device:TPU:56, one launch (start us, length us, event | category | flops | bytes accessed | tf_op | source)
XLA Modules:
  0.0 68.9 jit_solution(5960774663536418296)
XLA Ops:
  0.6 0.0 copy-start.1
  0.6 1.6 %copy-done.1 = bf16[1,256,2,1,16,128]{5,4,3,2,1,0:T(8,128)(2,1)S(1)} copy-done((bf16[1,256,2,1,16,128]{5,4,3,2,1,0:T(8,128)(2,1)S(1)}, bf16[1,256,2,1,16,128]{5,4,3,2,1,0:T(8,128)(2,1)}, u32[]{:S(2)}) %copy-start.1) | copy-done | bytes 2097176
  2.2 0.0 copy-start.7
  2.2 0.7 copy-done.7
  2.9 0.0 copy-start.2
  2.9 0.0 copy-start.3
  2.9 0.0 copy-start.4
  2.9 0.0 copy-start.5
  2.9 0.0 copy-start.6
  2.9 0.8 %gather_pages.1 = (bf16[8,8,2,16,128]{4,3,2,1,0:T(8,128)(2,1)S(1)}, bf16[8,8,2,16,128]{4,3,2,1,0:T(8,128)(2,1)S(1)}) custom-call(s32[2,4,16]{2,1,0:T(4,128)S(1)} %bitcast.31, bf16[256,2,16,128]{3,2,1,0:T(8,128)(2,1)S(1)} %bitcast.19), custom_call_target="tpu_custom_call" | custom-call | bytes 2097152 | tf_op jit(solution)/shard_map/gather_pages/pallas_call | solution.py:258
  3.8 0.1 collective-permute-start
  3.9 0.9 %copy.16 = f32[16,8,2,128]{3,1,2,0:T(8,128)S(1)} copy(bf16[16,8,2,128]{3,2,1,0:T(2,128)(2,1)} %bitcast.34) | data formatting | bytes 196608
  4.7 0.0 copy-start
  4.8 1.0 %collective-permute-done.refs_2_ = bf16[8,8,2,16,128]{4,3,2,1,0:T(8,128)(2,1)S(1)} collective-permute-done((bf16[8,8,2,16,128]{4,3,2,1,0:T(8,128)(2,1)S(1)}, bf16[8,8,2,16,128]{4,3,2,1,0:T(8,128)(2,1)S(1)}, u32[]{:S(2)}, u32[]{:S(2)}) %collective-permute-start) | collective-permute-done | bytes 524320 | tf_op jit(solution)/shard_map/ppermute | solution.py:267
  5.8 3.3 %collective-permute-start.1 = (bf16[4,8,2,16,128]{4,3,2,1,0:T(8,128)(2,1)S(1)}, bf16[4,8,2,16,128]{4,3,2,1,0:T(8,128)(2,1)S(1)}, u32[]{:S(2)}, u32[]{:S(2)}) collective-permute-start(bf16[4,8,2,16,128]{4,3,2,1,0:T(8,128)(2,1)S(1)} %pad_maximum_fusion), channel_id=1, source_target_pairs={{0,64},{16,80},{32,96},{48,112},{64,128},{80,144},{96,160},{112,17... | collective-permute-start | bytes 786440 | tf_op jit(solution)/shard_map/ppermute | solution.py:279
  9.2 2.2 %collective-permute-start.3 = (bf16[4,8,2,16,128]{4,3,2,1,0:T(8,128)(2,1)S(1)}, bf16[4,8,2,16,128]{4,3,2,1,0:T(8,128)(2,1)S(1)}, u32[]{:S(2)}, u32[]{:S(2)}) collective-permute-start(bf16[4,8,2,16,128]{4,3,2,1,0:T(8,128)(2,1)S(1)} %pad_maximum_fusion.1), channel_id=1, source_target_pairs={{0,192},{16,208},{32,224},{48,240},{64,0},{80,16},{96,32},{112,48}... | collective-permute-start | bytes 786440 | tf_op jit(solution)/shard_map/ppermute | solution.py:279
  11.5 0.0 copy-done.2
  11.5 0.0 copy-done.3
  11.5 0.0 copy-done.4
  11.5 0.0 copy-done.5
  11.5 0.0 copy-done.6
  11.5 5.1 %local_attention.1 = (bf16[128,1024]{1,0:T(8,128)(2,1)S(1)}, bf16[128,40]{1,0:T(8,128)(2,1)S(1)}, bf16[128,24]{1,0:T(8,128)(2,1)S(1)}, f32[64,1024]{1,0:T(8,128)...) custom-call(s32[4,64]{1,0:T(4,128)S(1)} %bitcast.28, s32[64]{0:T(128)S(1)} %copy-done.6, ...), custom_call_target="tpu_custom_call" | custom-call | flops 268435456 | bytes 16777216 | tf_op jit(solution)/shard_map/local_attention/pallas_call | solution.py:289
  16.6 1.1 %collective-permute-start.6 = (bf16[2,8,2,16,128]{4,3,2,1,0:T(8,128)(2,1)S(1)}, bf16[2,8,2,16,128]{4,3,2,1,0:T(8,128)(2,1)S(1)}, u32[]{:S(2)}, u32[]{:S(2)}) collective-permute-start(bf16[2,8,2,16,128]{4,3,2,1,0:T(8,128)(2,1)S(1)} %pad_maximum_fusion.3), channel_id=1, source_target_pairs={{0,32},{16,48},{32,64},{48,80},{64,96},{80,112},{96,128},{112,144}... | collective-permute-start | bytes 393224 | tf_op jit(solution)/shard_map/ppermute | solution.py:279
  17.7 1.1 %collective-permute-start.7 = (bf16[2,8,2,16,128]{4,3,2,1,0:T(8,128)(2,1)S(1)}, bf16[2,8,2,16,128]{4,3,2,1,0:T(8,128)(2,1)S(1)}, u32[]{:S(2)}, u32[]{:S(2)}) collective-permute-start(bf16[2,8,2,16,128]{4,3,2,1,0:T(8,128)(2,1)S(1)} %pad_maximum_fusion.4), channel_id=1, source_target_pairs={{0,224},{16,240},{32,0},{48,16},{64,32},{80,48},{96,64},{112,80},{... | collective-permute-start | bytes 393224 | tf_op jit(solution)/shard_map/ppermute | solution.py:279
  18.8 5.1 %collective-permute-start.5 = (bf16[2,8,2,16,128]{4,3,2,1,0:T(8,128)(2,1)S(1)}, bf16[2,8,2,16,128]{4,3,2,1,0:T(8,128)(2,1)S(1)}, u32[]{:S(2)}, u32[]{:S(2)}) collective-permute-start(bf16[2,8,2,16,128]{4,3,2,1,0:T(8,128)(2,1)S(1)} %pad_maximum_fusion.2), channel_id=1, source_target_pairs={{0,128},{16,144},{32,160},{48,176},{64,192},{80,208},{96,224},{112... | collective-permute-start | bytes 393224 | tf_op jit(solution)/shard_map/ppermute | solution.py:279
  23.9 0.1 collective-permute-done.1.refs_3_
  24.0 0.2 collective-permute-start.2
  24.2 0.0 collective-permute-done.3.refs_4_
  24.3 2.2 %collective-permute-start.4 = (bf16[2,8,2,16,128]{4,3,2,1,0:T(8,128)(2,1)S(1)}, bf16[2,8,2,16,128]{4,3,2,1,0:T(8,128)(2,1)S(1)}, u32[]{:S(2)}, u32[]{:S(2)}) collective-permute-start(bf16[2,8,2,16,128]{4,3,2,1,0:T(8,128)(2,1)S(1)} %slice.69), channel_id=1, source_target_pairs={{0,224},{16,240},{32,0},{48,16},{64,32},{80,48},{96,64},{112,80},{... | collective-permute-start | bytes 393224 | tf_op jit(solution)/shard_map/ppermute | solution.py:279
  26.5 0.0 collective-permute-done.6.refs_5_
  26.5 0.7 %collective-permute-done.7.refs_6_ = bf16[2,8,2,16,128]{4,3,2,1,0:T(8,128)(2,1)S(1)} collective-permute-done((bf16[2,8,2,16,128]{4,3,2,1,0:T(8,128)(2,1)S(1)}, bf16[2,8,2,16,128]{4,3,2,1,0:T(8,128)(2,1)S(1)}, u32[]{:S(2)}, u32[]{:S(2)}) %collective-permute-start.7) | collective-permute-done | bytes 131104 | tf_op jit(solution)/shard_map/ppermute | solution.py:279
  27.2 2.1 %arrival_attention.1.refs_7_ = bf16[128,1024]{1,0:T(8,128)(2,1)S(1)} custom-call(s32[64]{0:T(128)S(1)} %copy-done.6, s32[16,2,16]{2,1,0:T(2,128)S(1)} %bitcast.23, bf16[8,8,2,16,128]{4,3,2,1,0:T(8,128)(2,1)S(1)} %collective-permute-done.refs_2_, bf16[4,8,2,16,128]{4,3,2,1,0:T(8,128)(2,1)S(1)} %collective-permute-done.1.refs_3_, ...), custom_call_target="tpu_custom_call" | custom-call | flops 67108864 | bytes 2097152 | tf_op jit(solution)/shard_map/arrival_attention/pallas_call | solution.py:316
  29.3 7.3 %collective-permute-done.5.refs_4_ = bf16[2,8,2,16,128]{4,3,2,1,0:T(8,128)(2,1)S(1)} collective-permute-done((bf16[2,8,2,16,128]{4,3,2,1,0:T(8,128)(2,1)S(1)}, bf16[2,8,2,16,128]{4,3,2,1,0:T(8,128)(2,1)S(1)}, u32[]{:S(2)}, u32[]{:S(2)}) %collective-permute-start.5) | collective-permute-done | bytes 131104 | tf_op jit(solution)/shard_map/ppermute | solution.py:279
  36.5 0.0 collective-permute-done.2.refs_2_
  36.5 0.0 collective-permute-done.4.refs_3_
  36.6 0.0 copy-done
  36.6 3.2 %project.1 = (bf16[16,4096]{1,0:T(8,128)(2,1)S(1)}, bf16[16,4096]{1,0:T(8,128)(2,1)S(1)}, bf16[16,4096]{1,0:T(8,128)(2,1)S(1)}, bf16[16,4096]{1,0:T(8,128)(2,1)S...) custom-call(s32[64]{0:T(128)S(1)} %copy-done.6, ...), custom_call_target="tpu_custom_call" | custom-call | flops 67108864 | bytes 2097152 | tf_op jit(solution)/shard_map/project/pallas_call | solution.py:316
  39.8 0.8 %collective-permute-start.14 = (bf16[16,4096]{1,0:T(8,128)(2,1)S(1)}, bf16[16,4096]{1,0:T(8,128)(2,1)S(1)}, u32[]{:S(2)}, u32[]{:S(2)}) collective-permute-start(bf16[16,4096]{1,0:T(8,128)(2,1)S(1)} %get-tuple-element.56), channel_id=1, source_target_pairs={{0,8},{2,10},{4,12},{6,14},{8,0},{10,2},{12,4},{14,6},{1,9},{3,11}... | collective-permute-start | bytes 393224 | tf_op jit(solution)/shard_map/ppermute | solution.py:361
  40.6 1.5 %collective-permute-start.13 = (bf16[16,4096]{1,0:T(8,128)(2,1)S(1)}, bf16[16,4096]{1,0:T(8,128)(2,1)S(1)}, u32[]{:S(2)}, u32[]{:S(2)}) collective-permute-start(bf16[16,4096]{1,0:T(8,128)(2,1)S(1)} %get-tuple-element.55), channel_id=1, source_target_pairs={{0,2},{2,0},{4,6},{6,4},{8,10},{10,8},{12,14},{14,12},{1,3},{3,1},... | collective-permute-start | bytes 393224 | tf_op jit(solution)/shard_map/ppermute | solution.py:361
  42.1 2.1 %collective-permute-start.12 = (bf16[16,4096]{1,0:T(8,128)(2,1)S(1)}, bf16[16,4096]{1,0:T(8,128)(2,1)S(1)}, u32[]{:S(2)}, u32[]{:S(2)}) collective-permute-start(bf16[16,4096]{1,0:T(8,128)(2,1)S(1)} %get-tuple-element.54), channel_id=1, source_target_pairs={{0,6},{2,4},{4,2},{6,0},{8,14},{10,12},{12,10},{14,8},{1,7},{3,5},... | collective-permute-start | bytes 393224 | tf_op jit(solution)/shard_map/ppermute | solution.py:361
  44.2 1.3 %collective-permute-start.11 = (bf16[16,4096]{1,0:T(8,128)(2,1)S(1)}, bf16[16,4096]{1,0:T(8,128)(2,1)S(1)}, u32[]{:S(2)}, u32[]{:S(2)}) collective-permute-start(bf16[16,4096]{1,0:T(8,128)(2,1)S(1)} %get-tuple-element.53), channel_id=1, source_target_pairs={{0,10},{2,8},{4,14},{6,12},{8,2},{10,0},{12,6},{14,4},{1,11},{3,9}... | collective-permute-start | bytes 393224 | tf_op jit(solution)/shard_map/ppermute | solution.py:361
  45.5 0.8 %collective-permute-start.10 = (bf16[16,4096]{1,0:T(8,128)(2,1)S(1)}, bf16[16,4096]{1,0:T(8,128)(2,1)S(1)}, u32[]{:S(2)}, u32[]{:S(2)}) collective-permute-start(bf16[16,4096]{1,0:T(8,128)(2,1)S(1)} %get-tuple-element.52), channel_id=1, source_target_pairs={{0,14},{2,12},{4,10},{6,8},{8,6},{10,4},{12,2},{14,0},{1,15},{3,13... | collective-permute-start | bytes 393224 | tf_op jit(solution)/shard_map/ppermute | solution.py:361
  46.3 0.0 collective-permute-done.14
  46.3 5.9 %collective-permute-start.9 = (bf16[16,4096]{1,0:T(8,128)(2,1)S(1)}, bf16[16,4096]{1,0:T(8,128)(2,1)S(1)}, u32[]{:S(2)}, u32[]{:S(2)}) collective-permute-start(bf16[16,4096]{1,0:T(8,128)(2,1)S(1)} %get-tuple-element.51), channel_id=1, source_target_pairs={{0,4},{2,6},{4,0},{6,2},{8,12},{10,14},{12,8},{14,10},{1,5},{3,7},... | collective-permute-start | bytes 393224 | tf_op jit(solution)/shard_map/ppermute | solution.py:361
  52.2 0.0 collective-permute-done.13
  52.2 0.0 collective-permute-start.8
  52.2 0.0 copy-start.8
  52.2 1.9 %place_pages.2.refs_5_ = bf16[256,2,16,128]{3,2,1,0:T(8,128)(2,1)} custom-call(s32[4,64]{1,0:T(4,128)S(1)} %bitcast.29, s32[16,2,16]{2,1,0:T(2,128)S(1)} %bitcast.25, bf16[8,8,2,16,128]{4,3,2,1,0:T(8,128)(2,1)S(1)} %collective-permute-done.refs_2_, bf16[4,8,2,16,128]{4,3,2,1,0:T(8,128)(2,1)S(1)} %collective-permute-done.1.refs_3_, ...), custom_call_target="tpu_custom_call", output_to_operand_aliasing={{}: (7, {})} | custom-call | bytes 2097152 | tf_op jit(solution)/shard_map/place_pages/pallas_call | solution.py:330
  54.1 0.0 copy-done.8
  54.2 1.8 %place_pages.3 = bf16[256,2,16,128]{3,2,1,0:T(8,128)(2,1)} custom-call(s32[4,64]{1,0:T(4,128)S(1)} %bitcast.30, s32[16,2,16]{2,1,0:T(2,128)S(1)} %bitcast.26, bf16[2,8,2,16,128]{4,3,2,1,0:T(8,128)(2,1)S(1)} %collective-permute-done.2.refs_2_, bf16[2,8,2,16,128]{4,3,2,1,0:T(8,128)(2,1)S(1)} %collective-permute-done.4.refs_3_, ...), custom_call_target="tpu_custom_call", output_to_operand_aliasing={{}: (5, {})} | custom-call | bytes 2097152 | tf_op jit(solution)/shard_map/place_pages/pallas_call | solution.py:330
  56.0 0.0 collective-permute-done.12
  56.0 0.0 collective-permute-done.11
  56.0 0.1 collective-permute-done.10
  56.0 0.0 collective-permute-done.9
  56.0 3.5 %collective-permute-done.8 = bf16[16,4096]{1,0:T(8,128)(2,1)S(1)} collective-permute-done((bf16[16,4096]{1,0:T(8,128)(2,1)S(1)}, bf16[16,4096]{1,0:T(8,128)(2,1)S(1)}, u32[]{:S(2)}, u32[]{:S(2)}) %collective-permute-start.8) | collective-permute-done | bytes 131104 | tf_op jit(solution)/shard_map/ppermute | solution.py:361
  59.5 0.2 add_convert_fusion
  59.7 1.3 %collective-permute-start.15 = (bf16[16,4096]{1,0:T(8,128)(2,1)S(1)}, bf16[16,4096]{1,0:T(8,128)(2,1)S(1)}, u32[]{:S(2)}, u32[]{:S(2)}) collective-permute-start(bf16[16,4096]{1,0:T(8,128)(2,1)S(1)} %get-tuple-element.58.first), channel_id=1, source_target_pairs={{0,1},{2,3},{4,5},{6,7},{8,9},{10,11},{12,13},{14,15},{16,17},{18,... | collective-permute-start | bytes 393224 | tf_op jit(solution)/shard_map/ppermute | solution.py:364
  61.0 7.1 %collective-permute-done.15.passed = bf16[16,4096]{1,0:T(8,128)(2,1)S(1)} collective-permute-done((bf16[16,4096]{1,0:T(8,128)(2,1)S(1)}, bf16[16,4096]{1,0:T(8,128)(2,1)S(1)}, u32[]{:S(2)}, u32[]{:S(2)}) %collective-permute-start.15) | collective-permute-done | bytes 131104 | tf_op jit(solution)/shard_map/ppermute | solution.py:364
  68.1 0.8 %second_layer.1 = bf16[8,2,4096]{2,1,0:T(2,128)(2,1)} custom-call(bf16[16,4096]{1,0:T(8,128)(2,1)S(1)} %get-tuple-element.58.first, bf16[16,4096]{1,0:T(8,128)(2,1)S(1)} %collective-permute-done.15.passed, f32[16,4096]{1,0:T(8,128)S(1)} %get-tuple-element.63.branch), custom_call_target="tpu_custom_call" | custom-call | tf_op jit(solution)/shard_map/second_layer/pallas_call | solution.py:365
  (11 shorter events, 0.2 us)
Async XLA Ops:
  0.6 1.6 %copy-start.1 = (bf16[1,256,2,1,16,128]{5,4,3,2,1,0:T(8,128)(2,1)S(1)}, bf16[1,256,2,1,16,128]{5,4,3,2,1,0:T(8,128)(2,1)}, u32[]{:S(2)}) copy-start(bf16[1,256,2,1,16,128]{5,4,3,2,1,0:T(8,128)(2,1)} %param.12) | copy-start | bytes 6291460
  2.2 0.7 copy-start.7
  2.9 8.5 %copy-start.2 = (bf16[1,256,2,1,16,128]{5,4,3,2,1,0:T(8,128)(2,1)S(1)}, bf16[1,256,2,1,16,128]{5,4,3,2,1,0:T(8,128)(2,1)}, u32[]{:S(2)}) copy-start(bf16[1,256,2,1,16,128]{5,4,3,2,1,0:T(8,128)(2,1)} %param.12) | copy-start | bytes 6291460
  2.9 8.6 %copy-start.3 = (s32[16,16,2]{1,2,0:T(2,128)S(1)}, s32[16,16,2]{1,2,0:T(2,128)}, u32[]{:S(2)}) copy-start(s32[16,16,2]{1,2,0:T(2,128)} %param.16) | copy-start | bytes 6148
  2.9 8.6 %copy-start.4 = (bf16[1,64,2,1024]{3,2,1,0:T(2,128)(2,1)S(1)}, bf16[1,64,2,1024]{3,2,1,0:T(2,128)(2,1)}, u32[]{:S(2)}) copy-start(bf16[1,64,2,1024]{3,2,1,0:T(2,128)(2,1)} %param.10) | copy-start | bytes 786436
  2.9 8.6 %copy-start.5 = (s32[64,4]{0,1:T(4,128)S(1)}, s32[64,4]{0,1:T(4,128)}, u32[]{:S(2)}) copy-start(s32[64,4]{0,1:T(4,128)} %param.15) | copy-start | bytes 3076
  2.9 8.6 %copy-start.6 = (s32[64]{0:T(128)S(1)}, s32[64]{0:T(128)}, u32[]{:S(2)}) copy-start(s32[64]{0:T(128)} %refs_0_.3) | copy-start | bytes 772
  3.8 2.0 %collective-permute-start = (bf16[8,8,2,16,128]{4,3,2,1,0:T(8,128)(2,1)S(1)}, bf16[8,8,2,16,128]{4,3,2,1,0:T(8,128)(2,1)S(1)}, u32[]{:S(2)}, u32[]{:S(2)}) collective-permute-start(bf16[8,8,2,16,128]{4,3,2,1,0:T(8,128)(2,1)S(1)} %get-tuple-element.32), channel_id=1, source_target_pairs={{0,16},{16,0},{32,48},{48,32},{64,80},{80,64},{96,112},{112,96},{1... | collective-permute-start | bytes 1572872 | tf_op jit(solution)/shard_map/ppermute | solution.py:267
  4.7 31.8 %copy-start = (bf16[1,1024,4096]{2,1,0:T(8,128)(2,1)S(1)}, bf16[1,1024,4096]{2,1,0:T(8,128)(2,1)}, u32[]{:S(2)}) copy-start(bf16[1,1024,4096]{2,1,0:T(8,128)(2,1)} %param.13) | copy-start | bytes 25165828
  5.8 18.2 %collective-permute-start.1 = (bf16[4,8,2,16,128]{4,3,2,1,0:T(8,128)(2,1)S(1)}, bf16[4,8,2,16,128]{4,3,2,1,0:T(8,128)(2,1)S(1)}, u32[]{:S(2)}, u32[]{:S(2)}) collective-permute-start(bf16[4,8,2,16,128]{4,3,2,1,0:T(8,128)(2,1)S(1)} %pad_maximum_fusion), channel_id=1, source_target_pairs={{0,64},{16,80},{32,96},{48,112},{64,128},{80,144},{96,160},{112,17... | collective-permute-start | bytes 786440 | tf_op jit(solution)/shard_map/ppermute | solution.py:279
  9.2 15.0 %collective-permute-start.3 = (bf16[4,8,2,16,128]{4,3,2,1,0:T(8,128)(2,1)S(1)}, bf16[4,8,2,16,128]{4,3,2,1,0:T(8,128)(2,1)S(1)}, u32[]{:S(2)}, u32[]{:S(2)}) collective-permute-start(bf16[4,8,2,16,128]{4,3,2,1,0:T(8,128)(2,1)S(1)} %pad_maximum_fusion.1), channel_id=1, source_target_pairs={{0,192},{16,208},{32,224},{48,240},{64,0},{80,16},{96,32},{112,48}... | collective-permute-start | bytes 786440 | tf_op jit(solution)/shard_map/ppermute | solution.py:279
  16.6 9.9 %collective-permute-start.6 = (bf16[2,8,2,16,128]{4,3,2,1,0:T(8,128)(2,1)S(1)}, bf16[2,8,2,16,128]{4,3,2,1,0:T(8,128)(2,1)S(1)}, u32[]{:S(2)}, u32[]{:S(2)}) collective-permute-start(bf16[2,8,2,16,128]{4,3,2,1,0:T(8,128)(2,1)S(1)} %pad_maximum_fusion.3), channel_id=1, source_target_pairs={{0,32},{16,48},{32,64},{48,80},{64,96},{80,112},{96,128},{112,144}... | collective-permute-start | bytes 393224 | tf_op jit(solution)/shard_map/ppermute | solution.py:279
  17.7 9.5 %collective-permute-start.7 = (bf16[2,8,2,16,128]{4,3,2,1,0:T(8,128)(2,1)S(1)}, bf16[2,8,2,16,128]{4,3,2,1,0:T(8,128)(2,1)S(1)}, u32[]{:S(2)}, u32[]{:S(2)}) collective-permute-start(bf16[2,8,2,16,128]{4,3,2,1,0:T(8,128)(2,1)S(1)} %pad_maximum_fusion.4), channel_id=1, source_target_pairs={{0,224},{16,240},{32,0},{48,16},{64,32},{80,48},{96,64},{112,80},{... | collective-permute-start | bytes 393224 | tf_op jit(solution)/shard_map/ppermute | solution.py:279
  18.8 17.7 %collective-permute-start.5 = (bf16[2,8,2,16,128]{4,3,2,1,0:T(8,128)(2,1)S(1)}, bf16[2,8,2,16,128]{4,3,2,1,0:T(8,128)(2,1)S(1)}, u32[]{:S(2)}, u32[]{:S(2)}) collective-permute-start(bf16[2,8,2,16,128]{4,3,2,1,0:T(8,128)(2,1)S(1)} %pad_maximum_fusion.2), channel_id=1, source_target_pairs={{0,128},{16,144},{32,160},{48,176},{64,192},{80,208},{96,224},{112... | collective-permute-start | bytes 393224 | tf_op jit(solution)/shard_map/ppermute | solution.py:279
  24.0 12.5 %collective-permute-start.2 = (bf16[2,8,2,16,128]{4,3,2,1,0:T(8,128)(2,1)S(1)}, bf16[2,8,2,16,128]{4,3,2,1,0:T(8,128)(2,1)S(1)}, u32[]{:S(2)}, u32[]{:S(2)}) collective-permute-start(bf16[2,8,2,16,128]{4,3,2,1,0:T(8,128)(2,1)S(1)} %slice.66), channel_id=1, source_target_pairs={{0,32},{16,48},{32,64},{48,80},{64,96},{80,112},{96,128},{112,144}... | collective-permute-start | bytes 393224 | tf_op jit(solution)/shard_map/ppermute | solution.py:279
  24.3 12.3 %collective-permute-start.4 = (bf16[2,8,2,16,128]{4,3,2,1,0:T(8,128)(2,1)S(1)}, bf16[2,8,2,16,128]{4,3,2,1,0:T(8,128)(2,1)S(1)}, u32[]{:S(2)}, u32[]{:S(2)}) collective-permute-start(bf16[2,8,2,16,128]{4,3,2,1,0:T(8,128)(2,1)S(1)} %slice.69), channel_id=1, source_target_pairs={{0,224},{16,240},{32,0},{48,16},{64,32},{80,48},{96,64},{112,80},{... | collective-permute-start | bytes 393224 | tf_op jit(solution)/shard_map/ppermute | solution.py:279
  39.8 6.5 %collective-permute-start.14 = (bf16[16,4096]{1,0:T(8,128)(2,1)S(1)}, bf16[16,4096]{1,0:T(8,128)(2,1)S(1)}, u32[]{:S(2)}, u32[]{:S(2)}) collective-permute-start(bf16[16,4096]{1,0:T(8,128)(2,1)S(1)} %get-tuple-element.56), channel_id=1, source_target_pairs={{0,8},{2,10},{4,12},{6,14},{8,0},{10,2},{12,4},{14,6},{1,9},{3,11}... | collective-permute-start | bytes 393224 | tf_op jit(solution)/shard_map/ppermute | solution.py:361
  40.6 11.6 %collective-permute-start.13 = (bf16[16,4096]{1,0:T(8,128)(2,1)S(1)}, bf16[16,4096]{1,0:T(8,128)(2,1)S(1)}, u32[]{:S(2)}, u32[]{:S(2)}) collective-permute-start(bf16[16,4096]{1,0:T(8,128)(2,1)S(1)} %get-tuple-element.55), channel_id=1, source_target_pairs={{0,2},{2,0},{4,6},{6,4},{8,10},{10,8},{12,14},{14,12},{1,3},{3,1},... | collective-permute-start | bytes 393224 | tf_op jit(solution)/shard_map/ppermute | solution.py:361
  42.1 13.8 %collective-permute-start.12 = (bf16[16,4096]{1,0:T(8,128)(2,1)S(1)}, bf16[16,4096]{1,0:T(8,128)(2,1)S(1)}, u32[]{:S(2)}, u32[]{:S(2)}) collective-permute-start(bf16[16,4096]{1,0:T(8,128)(2,1)S(1)} %get-tuple-element.54), channel_id=1, source_target_pairs={{0,6},{2,4},{4,2},{6,0},{8,14},{10,12},{12,10},{14,8},{1,7},{3,5},... | collective-permute-start | bytes 393224 | tf_op jit(solution)/shard_map/ppermute | solution.py:361
  44.2 11.8 %collective-permute-start.11 = (bf16[16,4096]{1,0:T(8,128)(2,1)S(1)}, bf16[16,4096]{1,0:T(8,128)(2,1)S(1)}, u32[]{:S(2)}, u32[]{:S(2)}) collective-permute-start(bf16[16,4096]{1,0:T(8,128)(2,1)S(1)} %get-tuple-element.53), channel_id=1, source_target_pairs={{0,10},{2,8},{4,14},{6,12},{8,2},{10,0},{12,6},{14,4},{1,11},{3,9}... | collective-permute-start | bytes 393224 | tf_op jit(solution)/shard_map/ppermute | solution.py:361
  45.5 10.5 %collective-permute-start.10 = (bf16[16,4096]{1,0:T(8,128)(2,1)S(1)}, bf16[16,4096]{1,0:T(8,128)(2,1)S(1)}, u32[]{:S(2)}, u32[]{:S(2)}) collective-permute-start(bf16[16,4096]{1,0:T(8,128)(2,1)S(1)} %get-tuple-element.52), channel_id=1, source_target_pairs={{0,14},{2,12},{4,10},{6,8},{8,6},{10,4},{12,2},{14,0},{1,15},{3,13... | collective-permute-start | bytes 393224 | tf_op jit(solution)/shard_map/ppermute | solution.py:361
  46.3 9.7 %collective-permute-start.9 = (bf16[16,4096]{1,0:T(8,128)(2,1)S(1)}, bf16[16,4096]{1,0:T(8,128)(2,1)S(1)}, u32[]{:S(2)}, u32[]{:S(2)}) collective-permute-start(bf16[16,4096]{1,0:T(8,128)(2,1)S(1)} %get-tuple-element.51), channel_id=1, source_target_pairs={{0,4},{2,6},{4,0},{6,2},{8,12},{10,14},{12,8},{14,10},{1,5},{3,7},... | collective-permute-start | bytes 393224 | tf_op jit(solution)/shard_map/ppermute | solution.py:361
  52.2 7.4 %collective-permute-start.8 = (bf16[16,4096]{1,0:T(8,128)(2,1)S(1)}, bf16[16,4096]{1,0:T(8,128)(2,1)S(1)}, u32[]{:S(2)}, u32[]{:S(2)}) collective-permute-start(bf16[16,4096]{1,0:T(8,128)(2,1)S(1)} %get-tuple-element.50), channel_id=1, source_target_pairs={{0,12},{2,14},{4,8},{6,10},{8,4},{10,6},{12,0},{14,2},{1,13},{3,15... | collective-permute-start | bytes 393224 | tf_op jit(solution)/shard_map/ppermute | solution.py:361
  52.2 2.0 %copy-start.8 = (bf16[8,2,4096]{2,1,0:T(2,128)(2,1)S(1)}, bf16[8,2,4096]{2,1,0:T(2,128)(2,1)}, u32[]{:S(2)}) copy-start(bf16[8,2,4096]{2,1,0:T(2,128)(2,1)} %param.9) | copy-start | bytes 393220
  59.7 8.4 %collective-permute-start.15 = (bf16[16,4096]{1,0:T(8,128)(2,1)S(1)}, bf16[16,4096]{1,0:T(8,128)(2,1)S(1)}, u32[]{:S(2)}, u32[]{:S(2)}) collective-permute-start(bf16[16,4096]{1,0:T(8,128)(2,1)S(1)} %get-tuple-element.58.first), channel_id=1, source_target_pairs={{0,1},{2,3},{4,5},{6,7},{8,9},{10,11},{12,13},{14,15},{16,17},{18,... | collective-permute-start | bytes 393224 | tf_op jit(solution)/shard_map/ppermute | solution.py:364

commit v5 on v4

--- a/solution.py
+++ b/solution.py
@@ -356,7 +356,7 @@
 
     kept, residual = lax.optimization_barrier((parts[0], residual))
     branch = kept.astype(F32)
-    for peer in (6, 2, 7, 5, 3, 1, 4):
+    for peer in (4, 1, 3, 5, 7, 2, 6):
         pairs = [(index, index ^ peer) for index in range(n_tp)]
         branch = branch + lax.ppermute(parts[peer], "tp", pairs).astype(F32)
     first_out = (residual.reshape(own, model).astype(F32) + branch).astype(BF16)

time: 69.1 us -> 68.1 us (0.986)
  the two profiles are of different devices: /device:TPU:56 before, /device:TPU:16 now
where the time goes in v5:
time: 68.1 us; the launch traced here: 67.9 us
  starting transfers between devices  30.6 us (45%)
  waiting for transfers between devices  17.2 us (25%)
  Pallas kernels  15.7 us (23%)
  local copies, waits for them, and re-layouts  3.27 us (5%)
  between operations  0.87 us (1%)
    ppermute x7, starting transfers between devices, along_ring(): return lax.ppermute(jnp.concatenate(blocks, axis=0), 'inst', pairs)  18.2 us
    ppermute x7, starting transfers between devices, shards(): branch = branch + lax.ppermute(parts[peer], 'tp', pairs).astype(F32)  11.1 us
    ppermute x1, waiting for transfers between devices, shards(): passed = lax.ppermute(first_out, 'pp', [(0, 1)])  7.52 us
    pallas_call x2, Pallas kernels, arrival(): pl.pallas_call(functools.partial(kernel, scale, first, places), out_shape...  5.28 us
    ppermute x7, waiting for transfers between devices, along_ring(): return lax.ppermute(jnp.concatenate(blocks, axis=0), 'inst', pairs)  5.25 us
    pallas_call x1, Pallas kernels, shards(): pl.pallas_call(functools.partial(local_kernel, scale), out_shape=[jax.Sha...  5.05 us
    pallas_call x2, Pallas kernels, place_pages(): pl.pallas_call(functools.partial(place_kernel, first, places), out_shape=...  3.7 us
    ppermute x7, waiting for transfers between devices, shards(): branch = branch + lax.ppermute(parts[peer], 'tp', pairs).astype(F32)  3.4 us
  transfers between devices with their start and end apart: 16, of which 10 were waited for; matrix products, arithmetic and copies ran while one was open for 2% of the time, Pallas kernels for 16%

profile of v5, /device:TPU:16, one launch (start us, length us, event | category | flops | bytes accessed | tf_op | source)
XLA Modules:
  0.0 67.9 jit_solution(16752476731765879457)
XLA Ops:
  0.6 0.0 copy-start.1
  0.6 1.6 %copy-done.1 = bf16[1,256,2,1,16,128]{5,4,3,2,1,0:T(8,128)(2,1)S(1)} copy-done((bf16[1,256,2,1,16,128]{5,4,3,2,1,0:T(8,128)(2,1)S(1)}, bf16[1,256,2,1,16,128]{5,4,3,2,1,0:T(8,128)(2,1)}, u32[]{:S(2)}) %copy-start.1) | copy-done | bytes 2097176
  2.2 0.0 copy-start.7
  2.2 0.7 %copy-done.7 = s32[1,16,2,4]{1,3,2,0:T(4,128)S(1)} copy-done((s32[1,16,2,4]{1,3,2,0:T(4,128)S(1)}, s32[1,16,2,4]{1,3,2,0:T(4,128)}, u32[]{:S(2)}) %copy-start.7) | copy-done | bytes 536
  2.9 0.0 copy-start.2
  2.9 0.0 copy-start.3
  2.9 0.0 copy-start.4
  2.9 0.0 copy-start.5
  2.9 0.0 copy-start.6
  2.9 0.8 %gather_pages.1 = (bf16[8,8,2,16,128]{4,3,2,1,0:T(8,128)(2,1)S(1)}, bf16[8,8,2,16,128]{4,3,2,1,0:T(8,128)(2,1)S(1)}) custom-call(s32[2,4,16]{2,1,0:T(4,128)S(1)} %bitcast.31, bf16[256,2,16,128]{3,2,1,0:T(8,128)(2,1)S(1)} %bitcast.19), custom_call_target="tpu_custom_call" | custom-call | bytes 2097152 | tf_op jit(solution)/shard_map/gather_pages/pallas_call | solution.py:258
  3.8 0.1 collective-permute-start
  3.9 0.9 %copy.16 = f32[16,8,2,128]{3,1,2,0:T(8,128)S(1)} copy(bf16[16,8,2,128]{3,2,1,0:T(2,128)(2,1)} %bitcast.34) | data formatting | bytes 196608
  4.7 0.0 copy-start
  4.8 1.0 %collective-permute-done.refs_2_ = bf16[8,8,2,16,128]{4,3,2,1,0:T(8,128)(2,1)S(1)} collective-permute-done((bf16[8,8,2,16,128]{4,3,2,1,0:T(8,128)(2,1)S(1)}, bf16[8,8,2,16,128]{4,3,2,1,0:T(8,128)(2,1)S(1)}, u32[]{:S(2)}, u32[]{:S(2)}) %collective-permute-start) | collective-permute-done | bytes 524320 | tf_op jit(solution)/shard_map/ppermute | solution.py:267
  5.8 3.3 %collective-permute-start.1 = (bf16[4,8,2,16,128]{4,3,2,1,0:T(8,128)(2,1)S(1)}, bf16[4,8,2,16,128]{4,3,2,1,0:T(8,128)(2,1)S(1)}, u32[]{:S(2)}, u32[]{:S(2)}) collective-permute-start(bf16[4,8,2,16,128]{4,3,2,1,0:T(8,128)(2,1)S(1)} %pad_maximum_fusion), channel_id=1, source_target_pairs={{0,64},{16,80},{32,96},{48,112},{64,128},{80,144},{96,160},{112,17... | collective-permute-start | bytes 786440 | tf_op jit(solution)/shard_map/ppermute | solution.py:279
  9.2 3.1 %collective-permute-start.3 = (bf16[4,8,2,16,128]{4,3,2,1,0:T(8,128)(2,1)S(1)}, bf16[4,8,2,16,128]{4,3,2,1,0:T(8,128)(2,1)S(1)}, u32[]{:S(2)}, u32[]{:S(2)}) collective-permute-start(bf16[4,8,2,16,128]{4,3,2,1,0:T(8,128)(2,1)S(1)} %pad_maximum_fusion.1), channel_id=1, source_target_pairs={{0,192},{16,208},{32,224},{48,240},{64,0},{80,16},{96,32},{112,48}... | collective-permute-start | bytes 786440 | tf_op jit(solution)/shard_map/ppermute | solution.py:279
  12.4 0.0 copy-done.2
  12.4 0.0 copy-done.3
  12.4 0.0 copy-done.4
  12.4 0.0 copy-done.5
  12.4 0.0 copy-done.6
  12.4 5.0 %local_attention.1 = (bf16[128,1024]{1,0:T(8,128)(2,1)S(1)}, bf16[128,40]{1,0:T(8,128)(2,1)S(1)}, bf16[128,24]{1,0:T(8,128)(2,1)S(1)}, f32[64,1024]{1,0:T(8,128)...) custom-call(s32[4,64]{1,0:T(4,128)S(1)} %bitcast.28, s32[64]{0:T(128)S(1)} %copy-done.6, ...), custom_call_target="tpu_custom_call" | custom-call | flops 268435456 | bytes 16777216 | tf_op jit(solution)/shard_map/local_attention/pallas_call | solution.py:289
  17.5 1.1 %collective-permute-start.6 = (bf16[2,8,2,16,128]{4,3,2,1,0:T(8,128)(2,1)S(1)}, bf16[2,8,2,16,128]{4,3,2,1,0:T(8,128)(2,1)S(1)}, u32[]{:S(2)}, u32[]{:S(2)}) collective-permute-start(bf16[2,8,2,16,128]{4,3,2,1,0:T(8,128)(2,1)S(1)} %pad_maximum_fusion.3), channel_id=1, source_target_pairs={{0,32},{16,48},{32,64},{48,80},{64,96},{80,112},{96,128},{112,144}... | collective-permute-start | bytes 393224 | tf_op jit(solution)/shard_map/ppermute | solution.py:279
  18.6 2.3 %collective-permute-start.7 = (bf16[2,8,2,16,128]{4,3,2,1,0:T(8,128)(2,1)S(1)}, bf16[2,8,2,16,128]{4,3,2,1,0:T(8,128)(2,1)S(1)}, u32[]{:S(2)}, u32[]{:S(2)}) collective-permute-start(bf16[2,8,2,16,128]{4,3,2,1,0:T(8,128)(2,1)S(1)} %pad_maximum_fusion.4), channel_id=1, source_target_pairs={{0,224},{16,240},{32,0},{48,16},{64,32},{80,48},{96,64},{112,80},{... | collective-permute-start | bytes 393224 | tf_op jit(solution)/shard_map/ppermute | solution.py:279
  20.9 5.1 %collective-permute-start.5 = (bf16[2,8,2,16,128]{4,3,2,1,0:T(8,128)(2,1)S(1)}, bf16[2,8,2,16,128]{4,3,2,1,0:T(8,128)(2,1)S(1)}, u32[]{:S(2)}, u32[]{:S(2)}) collective-permute-start(bf16[2,8,2,16,128]{4,3,2,1,0:T(8,128)(2,1)S(1)} %pad_maximum_fusion.2), channel_id=1, source_target_pairs={{0,128},{16,144},{32,160},{48,176},{64,192},{80,208},{96,224},{112... | collective-permute-start | bytes 393224 | tf_op jit(solution)/shard_map/ppermute | solution.py:279
  26.0 0.0 collective-permute-done.1.refs_3_
  26.0 0.1 collective-permute-start.2
  26.1 0.2 collective-permute-done.3.refs_4_
  26.3 3.1 %collective-permute-start.4 = (bf16[2,8,2,16,128]{4,3,2,1,0:T(8,128)(2,1)S(1)}, bf16[2,8,2,16,128]{4,3,2,1,0:T(8,128)(2,1)S(1)}, u32[]{:S(2)}, u32[]{:S(2)}) collective-permute-start(bf16[2,8,2,16,128]{4,3,2,1,0:T(8,128)(2,1)S(1)} %slice.69), channel_id=1, source_target_pairs={{0,224},{16,240},{32,0},{48,16},{64,32},{80,48},{96,64},{112,80},{... | collective-permute-start | bytes 393224 | tf_op jit(solution)/shard_map/ppermute | solution.py:279
  29.4 0.0 collective-permute-done.6.refs_5_
  29.4 0.0 collective-permute-done.7.refs_6_
  29.4 2.1 %arrival_attention.1.refs_7_ = bf16[128,1024]{1,0:T(8,128)(2,1)S(1)} custom-call(s32[64]{0:T(128)S(1)} %copy-done.6, s32[16,2,16]{2,1,0:T(2,128)S(1)} %bitcast.23, bf16[8,8,2,16,128]{4,3,2,1,0:T(8,128)(2,1)S(1)} %collective-permute-done.refs_2_, bf16[4,8,2,16,128]{4,3,2,1,0:T(8,128)(2,1)S(1)} %collective-permute-done.1.refs_3_, ...), custom_call_target="tpu_custom_call" | custom-call | flops 67108864 | bytes 2097152 | tf_op jit(solution)/shard_map/arrival_attention/pallas_call | solution.py:316
  31.5 1.3 %collective-permute-done.5.refs_4_ = bf16[2,8,2,16,128]{4,3,2,1,0:T(8,128)(2,1)S(1)} collective-permute-done((bf16[2,8,2,16,128]{4,3,2,1,0:T(8,128)(2,1)S(1)}, bf16[2,8,2,16,128]{4,3,2,1,0:T(8,128)(2,1)S(1)}, u32[]{:S(2)}, u32[]{:S(2)}) %collective-permute-start.5) | collective-permute-done | bytes 131104 | tf_op jit(solution)/shard_map/ppermute | solution.py:279
  32.8 3.7 %collective-permute-done.2.refs_2_ = bf16[2,8,2,16,128]{4,3,2,1,0:T(8,128)(2,1)S(1)} collective-permute-done((bf16[2,8,2,16,128]{4,3,2,1,0:T(8,128)(2,1)S(1)}, bf16[2,8,2,16,128]{4,3,2,1,0:T(8,128)(2,1)S(1)}, u32[]{:S(2)}, u32[]{:S(2)}) %collective-permute-start.2) | collective-permute-done | bytes 131104 | tf_op jit(solution)/shard_map/ppermute | solution.py:279
  36.5 0.1 collective-permute-done.4.refs_3_
  36.6 0.0 copy-done
  36.6 3.2 %project.1 = (bf16[16,4096]{1,0:T(8,128)(2,1)S(1)}, bf16[16,4096]{1,0:T(8,128)(2,1)S(1)}, bf16[16,4096]{1,0:T(8,128)(2,1)S(1)}, bf16[16,4096]{1,0:T(8,128)(2,1)S...) custom-call(s32[64]{0:T(128)S(1)} %copy-done.6, ...), custom_call_target="tpu_custom_call" | custom-call | flops 67108864 | bytes 2097152 | tf_op jit(solution)/shard_map/project/pallas_call | solution.py:316
  39.8 3.8 %collective-permute-start.14 = (bf16[16,4096]{1,0:T(8,128)(2,1)S(1)}, bf16[16,4096]{1,0:T(8,128)(2,1)S(1)}, u32[]{:S(2)}, u32[]{:S(2)}) collective-permute-start(bf16[16,4096]{1,0:T(8,128)(2,1)S(1)} %get-tuple-element.56), channel_id=1, source_target_pairs={{0,12},{2,14},{4,8},{6,10},{8,4},{10,6},{12,0},{14,2},{1,13},{3,15... | collective-permute-start | bytes 393224 | tf_op jit(solution)/shard_map/ppermute | solution.py:361
  43.6 0.5 collective-permute-start.13
  44.1 2.9 %collective-permute-start.12 = (bf16[16,4096]{1,0:T(8,128)(2,1)S(1)}, bf16[16,4096]{1,0:T(8,128)(2,1)S(1)}, u32[]{:S(2)}, u32[]{:S(2)}) collective-permute-start(bf16[16,4096]{1,0:T(8,128)(2,1)S(1)} %get-tuple-element.54), channel_id=1, source_target_pairs={{0,14},{2,12},{4,10},{6,8},{8,6},{10,4},{12,2},{14,0},{1,15},{3,13... | collective-permute-start | bytes 393224 | tf_op jit(solution)/shard_map/ppermute | solution.py:361
  47.1 0.9 %collective-permute-start.11 = (bf16[16,4096]{1,0:T(8,128)(2,1)S(1)}, bf16[16,4096]{1,0:T(8,128)(2,1)S(1)}, u32[]{:S(2)}, u32[]{:S(2)}) collective-permute-start(bf16[16,4096]{1,0:T(8,128)(2,1)S(1)} %get-tuple-element.53), channel_id=1, source_target_pairs={{0,10},{2,8},{4,14},{6,12},{8,2},{10,0},{12,6},{14,4},{1,11},{3,9}... | collective-permute-start | bytes 393224 | tf_op jit(solution)/shard_map/ppermute | solution.py:361
  48.0 1.1 %collective-permute-start.10 = (bf16[16,4096]{1,0:T(8,128)(2,1)S(1)}, bf16[16,4096]{1,0:T(8,128)(2,1)S(1)}, u32[]{:S(2)}, u32[]{:S(2)}) collective-permute-start(bf16[16,4096]{1,0:T(8,128)(2,1)S(1)} %get-tuple-element.52), channel_id=1, source_target_pairs={{0,6},{2,4},{4,2},{6,0},{8,14},{10,12},{12,10},{14,8},{1,7},{3,5},... | collective-permute-start | bytes 393224 | tf_op jit(solution)/shard_map/ppermute | solution.py:361
  49.2 0.0 collective-permute-done.14
  49.2 1.1 %collective-permute-start.9 = (bf16[16,4096]{1,0:T(8,128)(2,1)S(1)}, bf16[16,4096]{1,0:T(8,128)(2,1)S(1)}, u32[]{:S(2)}, u32[]{:S(2)}) collective-permute-start(bf16[16,4096]{1,0:T(8,128)(2,1)S(1)} %get-tuple-element.51), channel_id=1, source_target_pairs={{0,2},{2,0},{4,6},{6,4},{8,10},{10,8},{12,14},{14,12},{1,3},{3,1},... | collective-permute-start | bytes 393224 | tf_op jit(solution)/shard_map/ppermute | solution.py:361
  50.2 1.0 %collective-permute-done.13 = bf16[16,4096]{1,0:T(8,128)(2,1)S(1)} collective-permute-done((bf16[16,4096]{1,0:T(8,128)(2,1)S(1)}, bf16[16,4096]{1,0:T(8,128)(2,1)S(1)}, u32[]{:S(2)}, u32[]{:S(2)}) %collective-permute-start.13) | collective-permute-done | bytes 131104 | tf_op jit(solution)/shard_map/ppermute | solution.py:361
  51.3 0.7 collective-permute-start.8
  51.9 0.0 copy-start.8
  51.9 1.9 %place_pages.2.refs_5_ = bf16[256,2,16,128]{3,2,1,0:T(8,128)(2,1)} custom-call(s32[4,64]{1,0:T(4,128)S(1)} %bitcast.29, s32[16,2,16]{2,1,0:T(2,128)S(1)} %bitcast.25, bf16[8,8,2,16,128]{4,3,2,1,0:T(8,128)(2,1)S(1)} %collective-permute-done.refs_2_, bf16[4,8,2,16,128]{4,3,2,1,0:T(8,128)(2,1)S(1)} %collective-permute-done.1.refs_3_, ...), custom_call_target="tpu_custom_call", output_to_operand_aliasing={{}: (7, {})} | custom-call | bytes 2097152 | tf_op jit(solution)/shard_map/place_pages/pallas_call | solution.py:330
  53.9 0.0 copy-done.8
  53.9 1.8 %place_pages.3 = bf16[256,2,16,128]{3,2,1,0:T(8,128)(2,1)} custom-call(s32[4,64]{1,0:T(4,128)S(1)} %bitcast.30, s32[16,2,16]{2,1,0:T(2,128)S(1)} %bitcast.26, bf16[2,8,2,16,128]{4,3,2,1,0:T(8,128)(2,1)S(1)} %collective-permute-done.2.refs_2_, bf16[2,8,2,16,128]{4,3,2,1,0:T(8,128)(2,1)S(1)} %collective-permute-done.4.refs_3_, ...), custom_call_target="tpu_custom_call", output_to_operand_aliasing={{}: (5, {})} | custom-call | bytes 2097152 | tf_op jit(solution)/shard_map/place_pages/pallas_call | solution.py:330
  55.7 0.0 collective-permute-done.12
  55.7 0.0 collective-permute-done.11
  55.7 0.2 collective-permute-done.10
  55.9 0.2 collective-permute-done.9
  56.1 2.0 %collective-permute-done.8 = bf16[16,4096]{1,0:T(8,128)(2,1)S(1)} collective-permute-done((bf16[16,4096]{1,0:T(8,128)(2,1)S(1)}, bf16[16,4096]{1,0:T(8,128)(2,1)S(1)}, u32[]{:S(2)}, u32[]{:S(2)}) %collective-permute-start.8) | collective-permute-done | bytes 131104 | tf_op jit(solution)/shard_map/ppermute | solution.py:361
  58.1 0.2 add_convert_fusion
  58.2 1.3 %collective-permute-start.15 = (bf16[16,4096]{1,0:T(8,128)(2,1)S(1)}, bf16[16,4096]{1,0:T(8,128)(2,1)S(1)}, u32[]{:S(2)}, u32[]{:S(2)}) collective-permute-start(bf16[16,4096]{1,0:T(8,128)(2,1)S(1)} %get-tuple-element.58.first), channel_id=1, source_target_pairs={{0,1},{2,3},{4,5},{6,7},{8,9},{10,11},{12,13},{14,15},{16,17},{18,... | collective-permute-start | bytes 393224 | tf_op jit(solution)/shard_map/ppermute | solution.py:364
  59.5 7.5 %collective-permute-done.15.passed = bf16[16,4096]{1,0:T(8,128)(2,1)S(1)} collective-permute-done((bf16[16,4096]{1,0:T(8,128)(2,1)S(1)}, bf16[16,4096]{1,0:T(8,128)(2,1)S(1)}, u32[]{:S(2)}, u32[]{:S(2)}) %collective-permute-start.15) | collective-permute-done | bytes 131104 | tf_op jit(solution)/shard_map/ppermute | solution.py:364
  67.1 0.8 %second_layer.1 = bf16[8,2,4096]{2,1,0:T(2,128)(2,1)} custom-call(bf16[16,4096]{1,0:T(8,128)(2,1)S(1)} %get-tuple-element.58.first, bf16[16,4096]{1,0:T(8,128)(2,1)S(1)} %collective-permute-done.15.passed, f32[16,4096]{1,0:T(8,128)S(1)} %get-tuple-element.63.branch), custom_call_target="tpu_custom_call" | custom-call | tf_op jit(solution)/shard_map/second_layer/pallas_call | solution.py:365
  (11 shorter events, 0.2 us)
Async XLA Ops:
  0.6 1.6 %copy-start.1 = (bf16[1,256,2,1,16,128]{5,4,3,2,1,0:T(8,128)(2,1)S(1)}, bf16[1,256,2,1,16,128]{5,4,3,2,1,0:T(8,128)(2,1)}, u32[]{:S(2)}) copy-start(bf16[1,256,2,1,16,128]{5,4,3,2,1,0:T(8,128)(2,1)} %param.12) | copy-start | bytes 6291460
  2.2 0.7 %copy-start.7 = (s32[1,16,2,4]{1,3,2,0:T(4,128)S(1)}, s32[1,16,2,4]{1,3,2,0:T(4,128)}, u32[]{:S(2)}) copy-start(s32[1,16,2,4]{1,3,2,0:T(4,128)} %param.17) | copy-start | bytes 1540
  2.9 9.4 %copy-start.2 = (bf16[1,256,2,1,16,128]{5,4,3,2,1,0:T(8,128)(2,1)S(1)}, bf16[1,256,2,1,16,128]{5,4,3,2,1,0:T(8,128)(2,1)}, u32[]{:S(2)}) copy-start(bf16[1,256,2,1,16,128]{5,4,3,2,1,0:T(8,128)(2,1)} %param.12) | copy-start | bytes 6291460
  2.9 9.5 %copy-start.3 = (s32[16,16,2]{1,2,0:T(2,128)S(1)}, s32[16,16,2]{1,2,0:T(2,128)}, u32[]{:S(2)}) copy-start(s32[16,16,2]{1,2,0:T(2,128)} %param.16) | copy-start | bytes 6148
  2.9 9.5 %copy-start.4 = (bf16[1,64,2,1024]{3,2,1,0:T(2,128)(2,1)S(1)}, bf16[1,64,2,1024]{3,2,1,0:T(2,128)(2,1)}, u32[]{:S(2)}) copy-start(bf16[1,64,2,1024]{3,2,1,0:T(2,128)(2,1)} %param.10) | copy-start | bytes 786436
  2.9 9.5 %copy-start.5 = (s32[64,4]{0,1:T(4,128)S(1)}, s32[64,4]{0,1:T(4,128)}, u32[]{:S(2)}) copy-start(s32[64,4]{0,1:T(4,128)} %param.15) | copy-start | bytes 3076
  2.9 9.5 %copy-start.6 = (s32[64]{0:T(128)S(1)}, s32[64]{0:T(128)}, u32[]{:S(2)}) copy-start(s32[64]{0:T(128)} %refs_0_.3) | copy-start | bytes 772
  3.8 2.0 %collective-permute-start = (bf16[8,8,2,16,128]{4,3,2,1,0:T(8,128)(2,1)S(1)}, bf16[8,8,2,16,128]{4,3,2,1,0:T(8,128)(2,1)S(1)}, u32[]{:S(2)}, u32[]{:S(2)}) collective-permute-start(bf16[8,8,2,16,128]{4,3,2,1,0:T(8,128)(2,1)S(1)} %get-tuple-element.32), channel_id=1, source_target_pairs={{0,16},{16,0},{32,48},{48,32},{64,80},{80,64},{96,112},{112,96},{1... | collective-permute-start | bytes 1572872 | tf_op jit(solution)/shard_map/ppermute | solution.py:267
  4.7 31.9 %copy-start = (bf16[1,1024,4096]{2,1,0:T(8,128)(2,1)S(1)}, bf16[1,1024,4096]{2,1,0:T(8,128)(2,1)}, u32[]{:S(2)}) copy-start(bf16[1,1024,4096]{2,1,0:T(8,128)(2,1)} %param.13) | copy-start | bytes 25165828
  5.8 20.2 %collective-permute-start.1 = (bf16[4,8,2,16,128]{4,3,2,1,0:T(8,128)(2,1)S(1)}, bf16[4,8,2,16,128]{4,3,2,1,0:T(8,128)(2,1)S(1)}, u32[]{:S(2)}, u32[]{:S(2)}) collective-permute-start(bf16[4,8,2,16,128]{4,3,2,1,0:T(8,128)(2,1)S(1)} %pad_maximum_fusion), channel_id=1, source_target_pairs={{0,64},{16,80},{32,96},{48,112},{64,128},{80,144},{96,160},{112,17... | collective-permute-start | bytes 786440 | tf_op jit(solution)/shard_map/ppermute | solution.py:279
  9.2 17.1 %collective-permute-start.3 = (bf16[4,8,2,16,128]{4,3,2,1,0:T(8,128)(2,1)S(1)}, bf16[4,8,2,16,128]{4,3,2,1,0:T(8,128)(2,1)S(1)}, u32[]{:S(2)}, u32[]{:S(2)}) collective-permute-start(bf16[4,8,2,16,128]{4,3,2,1,0:T(8,128)(2,1)S(1)} %pad_maximum_fusion.1), channel_id=1, source_target_pairs={{0,192},{16,208},{32,224},{48,240},{64,0},{80,16},{96,32},{112,48}... | collective-permute-start | bytes 786440 | tf_op jit(solution)/shard_map/ppermute | solution.py:279
  17.5 11.9 %collective-permute-start.6 = (bf16[2,8,2,16,128]{4,3,2,1,0:T(8,128)(2,1)S(1)}, bf16[2,8,2,16,128]{4,3,2,1,0:T(8,128)(2,1)S(1)}, u32[]{:S(2)}, u32[]{:S(2)}) collective-permute-start(bf16[2,8,2,16,128]{4,3,2,1,0:T(8,128)(2,1)S(1)} %pad_maximum_fusion.3), channel_id=1, source_target_pairs={{0,32},{16,48},{32,64},{48,80},{64,96},{80,112},{96,128},{112,144}... | collective-permute-start | bytes 393224 | tf_op jit(solution)/shard_map/ppermute | solution.py:279
  18.6 10.8 %collective-permute-start.7 = (bf16[2,8,2,16,128]{4,3,2,1,0:T(8,128)(2,1)S(1)}, bf16[2,8,2,16,128]{4,3,2,1,0:T(8,128)(2,1)S(1)}, u32[]{:S(2)}, u32[]{:S(2)}) collective-permute-start(bf16[2,8,2,16,128]{4,3,2,1,0:T(8,128)(2,1)S(1)} %pad_maximum_fusion.4), channel_id=1, source_target_pairs={{0,224},{16,240},{32,0},{48,16},{64,32},{80,48},{96,64},{112,80},{... | collective-permute-start | bytes 393224 | tf_op jit(solution)/shard_map/ppermute | solution.py:279
  20.9 11.9 %collective-permute-start.5 = (bf16[2,8,2,16,128]{4,3,2,1,0:T(8,128)(2,1)S(1)}, bf16[2,8,2,16,128]{4,3,2,1,0:T(8,128)(2,1)S(1)}, u32[]{:S(2)}, u32[]{:S(2)}) collective-permute-start(bf16[2,8,2,16,128]{4,3,2,1,0:T(8,128)(2,1)S(1)} %pad_maximum_fusion.2), channel_id=1, source_target_pairs={{0,128},{16,144},{32,160},{48,176},{64,192},{80,208},{96,224},{112... | collective-permute-start | bytes 393224 | tf_op jit(solution)/shard_map/ppermute | solution.py:279
  26.0 10.5 %collective-permute-start.2 = (bf16[2,8,2,16,128]{4,3,2,1,0:T(8,128)(2,1)S(1)}, bf16[2,8,2,16,128]{4,3,2,1,0:T(8,128)(2,1)S(1)}, u32[]{:S(2)}, u32[]{:S(2)}) collective-permute-start(bf16[2,8,2,16,128]{4,3,2,1,0:T(8,128)(2,1)S(1)} %slice.66), channel_id=1, source_target_pairs={{0,32},{16,48},{32,64},{48,80},{64,96},{80,112},{96,128},{112,144}... | collective-permute-start | bytes 393224 | tf_op jit(solution)/shard_map/ppermute | solution.py:279
  26.3 10.3 %collective-permute-start.4 = (bf16[2,8,2,16,128]{4,3,2,1,0:T(8,128)(2,1)S(1)}, bf16[2,8,2,16,128]{4,3,2,1,0:T(8,128)(2,1)S(1)}, u32[]{:S(2)}, u32[]{:S(2)}) collective-permute-start(bf16[2,8,2,16,128]{4,3,2,1,0:T(8,128)(2,1)S(1)} %slice.69), channel_id=1, source_target_pairs={{0,224},{16,240},{32,0},{48,16},{64,32},{80,48},{96,64},{112,80},{... | collective-permute-start | bytes 393224 | tf_op jit(solution)/shard_map/ppermute | solution.py:279
  39.8 9.4 %collective-permute-start.14 = (bf16[16,4096]{1,0:T(8,128)(2,1)S(1)}, bf16[16,4096]{1,0:T(8,128)(2,1)S(1)}, u32[]{:S(2)}, u32[]{:S(2)}) collective-permute-start(bf16[16,4096]{1,0:T(8,128)(2,1)S(1)} %get-tuple-element.56), channel_id=1, source_target_pairs={{0,12},{2,14},{4,8},{6,10},{8,4},{10,6},{12,0},{14,2},{1,13},{3,15... | collective-permute-start | bytes 393224 | tf_op jit(solution)/shard_map/ppermute | solution.py:361
  43.6 7.6 %collective-permute-start.13 = (bf16[16,4096]{1,0:T(8,128)(2,1)S(1)}, bf16[16,4096]{1,0:T(8,128)(2,1)S(1)}, u32[]{:S(2)}, u32[]{:S(2)}) collective-permute-start(bf16[16,4096]{1,0:T(8,128)(2,1)S(1)} %get-tuple-element.55), channel_id=1, source_target_pairs={{0,4},{2,6},{4,0},{6,2},{8,12},{10,14},{12,8},{14,10},{1,5},{3,7},... | collective-permute-start | bytes 393224 | tf_op jit(solution)/shard_map/ppermute | solution.py:361
  44.1 11.6 %collective-permute-start.12 = (bf16[16,4096]{1,0:T(8,128)(2,1)S(1)}, bf16[16,4096]{1,0:T(8,128)(2,1)S(1)}, u32[]{:S(2)}, u32[]{:S(2)}) collective-permute-start(bf16[16,4096]{1,0:T(8,128)(2,1)S(1)} %get-tuple-element.54), channel_id=1, source_target_pairs={{0,14},{2,12},{4,10},{6,8},{8,6},{10,4},{12,2},{14,0},{1,15},{3,13... | collective-permute-start | bytes 393224 | tf_op jit(solution)/shard_map/ppermute | solution.py:361
  47.1 8.6 %collective-permute-start.11 = (bf16[16,4096]{1,0:T(8,128)(2,1)S(1)}, bf16[16,4096]{1,0:T(8,128)(2,1)S(1)}, u32[]{:S(2)}, u32[]{:S(2)}) collective-permute-start(bf16[16,4096]{1,0:T(8,128)(2,1)S(1)} %get-tuple-element.53), channel_id=1, source_target_pairs={{0,10},{2,8},{4,14},{6,12},{8,2},{10,0},{12,6},{14,4},{1,11},{3,9}... | collective-permute-start | bytes 393224 | tf_op jit(solution)/shard_map/ppermute | solution.py:361
  48.0 7.9 %collective-permute-start.10 = (bf16[16,4096]{1,0:T(8,128)(2,1)S(1)}, bf16[16,4096]{1,0:T(8,128)(2,1)S(1)}, u32[]{:S(2)}, u32[]{:S(2)}) collective-permute-start(bf16[16,4096]{1,0:T(8,128)(2,1)S(1)} %get-tuple-element.52), channel_id=1, source_target_pairs={{0,6},{2,4},{4,2},{6,0},{8,14},{10,12},{12,10},{14,8},{1,7},{3,5},... | collective-permute-start | bytes 393224 | tf_op jit(solution)/shard_map/ppermute | solution.py:361
  49.2 7.0 %collective-permute-start.9 = (bf16[16,4096]{1,0:T(8,128)(2,1)S(1)}, bf16[16,4096]{1,0:T(8,128)(2,1)S(1)}, u32[]{:S(2)}, u32[]{:S(2)}) collective-permute-start(bf16[16,4096]{1,0:T(8,128)(2,1)S(1)} %get-tuple-element.51), channel_id=1, source_target_pairs={{0,2},{2,0},{4,6},{6,4},{8,10},{10,8},{12,14},{14,12},{1,3},{3,1},... | collective-permute-start | bytes 393224 | tf_op jit(solution)/shard_map/ppermute | solution.py:361
  51.3 6.8 %collective-permute-start.8 = (bf16[16,4096]{1,0:T(8,128)(2,1)S(1)}, bf16[16,4096]{1,0:T(8,128)(2,1)S(1)}, u32[]{:S(2)}, u32[]{:S(2)}) collective-permute-start(bf16[16,4096]{1,0:T(8,128)(2,1)S(1)} %get-tuple-element.50), channel_id=1, source_target_pairs={{0,8},{2,10},{4,12},{6,14},{8,0},{10,2},{12,4},{14,6},{1,9},{3,11}... | collective-permute-start | bytes 393224 | tf_op jit(solution)/shard_map/ppermute | solution.py:361
  51.9 1.9 %copy-start.8 = (bf16[8,2,4096]{2,1,0:T(2,128)(2,1)S(1)}, bf16[8,2,4096]{2,1,0:T(2,128)(2,1)}, u32[]{:S(2)}) copy-start(bf16[8,2,4096]{2,1,0:T(2,128)(2,1)} %param.9) | copy-start | bytes 393220
  58.2 8.8 %collective-permute-start.15 = (bf16[16,4096]{1,0:T(8,128)(2,1)S(1)}, bf16[16,4096]{1,0:T(8,128)(2,1)S(1)}, u32[]{:S(2)}, u32[]{:S(2)}) collective-permute-start(bf16[16,4096]{1,0:T(8,128)(2,1)S(1)} %get-tuple-element.58.first), channel_id=1, source_target_pairs={{0,1},{2,3},{4,5},{6,7},{8,9},{10,11},{12,13},{14,15},{16,17},{18,... | collective-permute-start | bytes 393224 | tf_op jit(solution)/shard_map/ppermute | solution.py:364
